TPU v7x, 128 devices: a whole 4x4x4 slice. The times are simulated.
128 devices in a mesh: span: 16 (over z, y), chord: 8 (over x, core).
Axes of the slice: x: 4, y: 4, z: 4, core: 2. Of those that a mesh axis runs over, the one named last changes fastest.
Arguments:
- query_tiles: bfloat16 [32, 16, 128, 512], P('span', 'chord'), may hold values from -67 to 67
- key_tiles: bfloat16 [32, 16, 128, 512], P('span', 'chord'), may hold values from -6 to 6
- value_tiles: bfloat16 [32, 16, 128, 512], P('span', 'chord'), may hold values from -6 to 6
- out_grad: bfloat16 [32, 16, 128, 512], P('span', 'chord'), may hold values from -6 to 6
- mix_gain: float32 [4, 512], replicated, may hold values from 0.1 to 0.8
- partners: int32 [32, 16, 8], P('span', 'chord'), may hold values from 0 to 511, as said below
- counts: int32 [32, 16], P('span', 'chord'), may hold values from 1 to 8
Outputs:
- query_grad: bfloat16 [32, 16, 128, 512], P('span', 'chord')
- key_grad: bfloat16 [32, 16, 128, 512], P('span', 'chord')
- value_grad: bfloat16 [32, 16, 128, 512], P('span', 'chord')
Inputs may be any that keep to these rules, and one draw needn't show every extreme that they name: `partners`: slot j of a patch's list, for j below its count, is the flattened index (span position times 16 plus chord position) of a distinct patch at most one step away along each grid dimension; slot 0 is the patch itself; slots at or past the count hold the patch's own index.
All inputs are finite; a program needn't handle non-finite values.
Results may differ from a plain program's by a relative error of at most 0.012.
The roundings to bfloat16 on the way count: a program that leaves them out, or rounds other values in their place, can miss the bound.
Values may be sent and summed in bfloat16 or wider, within the bound.
No kernel may reach another device: no remote copies, remote signals or barrier semaphores. Data moves between devices by JAX's collectives and lax.ppermute only.
A program may use at most 128 MiB of HBM per device.

v0:
```python
import functools

import jax
import jax.numpy as jnp
from jax import lax
from jax.experimental import pallas as pl
from jax.experimental.pallas import tpu as pltpu
from jax.sharding import PartitionSpec as P

PATCH = 128
D = 512
PAIRS = 4
SCALING = 0.125
LOW_FILL = -1e30
NT = (((1,), (1,)), ((), ()))

OWN = (5, 6, 9, 10)
UP, DOWN, LEFT, RIGHT = (1, 2), (13, 14), (4, 8), (7, 11)
CORNERS = (0, 3, 12, 15)


def shifted(x, span_step, chord_step):
    span, chord = lax.axis_size("span"), lax.axis_size("chord")
    pairs = [
        (s * chord + c, ((s + span_step) % span) * chord + (c + chord_step) % chord)
        for s in range(span)
        for c in range(chord)
    ]
    return lax.ppermute(x, ("span", "chord"), pairs)


def stacked_pair(rows):
    lane = lax.broadcasted_iota(jnp.int32, rows.shape, 1)
    zero = jnp.zeros_like(rows)
    return jnp.concatenate(
        [jnp.where(lane < 64, rows, zero), jnp.where(lane >= 64, rows, zero)], axis=0
    )


def cols(h):
    return pl.ds(pl.multiple_of(h * 128, 128), 128)


def product(rows, pair):
    return lax.dot_general(rows, pair, NT, preferred_element_type=jnp.float32)


def matmul(a, b):
    return jnp.dot(a, b, preferred_element_type=jnp.float32)


def diagonal(x):
    return jnp.concatenate([x[:64, :128], x[64:, 128:]], axis=0)


def per_head(row):
    return jnp.concatenate(
        [jnp.broadcast_to(row[:, :128], (64, 128)), jnp.broadcast_to(row[:, 128:], (64, 128))], axis=0
    )


def penalty(listed, p, w):
    return jnp.where(listed[p * 16 + w] > 0, 0.0, -LOW_FILL)


def exponents(s, row, penalties):
    return jnp.concatenate(
        [jnp.exp(s[128 * i : 128 * (i + 1)] - (row + x)) for i, x in enumerate(penalties)], axis=0
    )


def highest(s, penalties):
    tops = [
        jnp.max(s[128 * i : 128 * (i + 1)], axis=0, keepdims=True) - x for i, x in enumerate(penalties)
    ]
    return functools.reduce(jnp.maximum, tops)


def merged(groups, stats, attended):
    tops = [highest(s, penalties) for s, penalties, _ in groups]
    if stats is not None:
        tops.append(stats[0])
    top = functools.reduce(jnp.maximum, tops)
    total, turned = 0.0, 0.0
    for s, penalties, value_turned in groups:
        e = exponents(s, top, penalties)
        total = total + jnp.sum(e, axis=0, keepdims=True)
        turned = turned + matmul(value_turned, e.astype(jnp.bfloat16))
    turned = diagonal(turned)
    if stats is not None:
        fade = jnp.exp(stats[0] - top)
        total = total + stats[1] * fade
        turned = turned + attended * per_head(fade)
    return top, total, turned


def own_totals_kernel(listed, query, key, value, query_pairs, stats_out, attended_out):
    def step(h, carry):
        value_turned = value[:, cols(h)].T
        for p in range(4):
            pair = stacked_pair(query[p, :, cols(h)] * jnp.bfloat16(SCALING))
            query_pairs[h, p] = pair
            groups = []
            for n in range(2):
                rows = slice(256 * n, 256 * (n + 1))
                groups.append(
                    (
                        product(key[rows, cols(h)], pair),
                        [penalty(listed, p, w) for w in OWN[2 * n : 2 * n + 2]],
                        value_turned[:, rows],
                    )
                )
            top, total, turned = merged(groups, None, None)
            stats_out[h, p : p + 1, :] = top
            stats_out[h, 4 + p : 5 + p, :] = total
            attended_out[h, p] = turned
        return carry

    lax.fori_loop(0, PAIRS, step, 0)


def edge_totals_kernel(
    listed, gain, grad, query_pairs, stats_in, attended_in, from_up, from_down, from_left, from_right,
    grad_pairs, grad_turned, stats_out, attended_out,
):
    ends = ((from_up, UP), (from_down, DOWN))
    sides = ((from_left, LEFT), (from_right, RIGHT))

    def step(h, carry):
        def turned(source):
            return source[1, :, :, cols(h)].reshape(256, 128).T

        values = {id(source): turned(source) for source, _ in ends + sides}
        for p in range(4):
            s, c = p // 2, p % 2
            near = (
                grad[0, c, :, cols(h)] if s == 1 else from_up[2, c, :, cols(h)],
                grad[1, c, :, cols(h)] if s == 0 else from_down[2, c, :, cols(h)],
                grad[s, 0, :, cols(h)] if c == 1 else from_left[2, s, :, cols(h)],
                grad[s, 1, :, cols(h)] if c == 0 else from_right[2, s, :, cols(h)],
            )
            own = (s == 1, s == 0, c == 1, c == 0)
            mixed = grad[s, c, :, cols(h)].astype(jnp.float32)
            for n in range(4):
                row = n if own[n] else n + 4
                mixed = mixed + gain[row : row + 1, cols(h)] * near[n].astype(jnp.float32)
            mixed = mixed.astype(jnp.bfloat16)
            grad_pairs[h, p] = stacked_pair(mixed)
            grad_turned[h, p] = mixed.T
            groups = []
            for source, places in (ends[s], sides[c]):
                groups.append(
                    (
                        product(source[0, :, :, cols(h)].reshape(256, 128), query_pairs[h, p]),
                        [penalty(listed, p, w) for w in places],
                        values[id(source)],
                    )
                )
            stats = stats_in[h, p : p + 1, :], stats_in[h, 4 + p : 5 + p, :]
            top, total, attended = merged(groups, stats, attended_in[h, p])
            stats_out[h, p : p + 1, :] = top
            stats_out[h, 4 + p : 5 + p, :] = total
            attended_out[h, p] = attended
        return carry

    lax.fori_loop(0, PAIRS, step, 0)


def gradients(s, g, penalties, log_total, delta):
    prob = exponents(s, log_total, penalties)
    return prob.astype(jnp.bfloat16), (prob * (g - delta)).astype(jnp.bfloat16)


def corner_kernel(
    listed, stats_in, attended_in, query_pairs, grad_pairs, grad_turned, corner_left, corner_right,
    finals, left_back, right_back, dq_out,
):
    patches = range(4)

    def source(p):
        return (corner_left, corner_right)[p % 2]

    def step(h, carry):
        key_rows = [source(p)[0, p // 2, :, cols(h)] for p in patches]
        value_rows = [source(p)[1, p // 2, :, cols(h)] for p in patches]
        scores = [product(key_rows[p], query_pairs[h, p]) for p in patches]
        g = [product(value_rows[p], grad_pairs[h, p]) for p in patches]
        value_turned = [x.T for x in value_rows]
        key_turned = [x.T for x in key_rows]
        half, score_grad = [], []
        for p in patches:
            missing = penalty(listed, p, CORNERS[p])
            old_top, old_total = stats_in[h, p : p + 1, :], stats_in[h, 4 + p : 5 + p, :]
            top = jnp.maximum(old_top, jnp.max(scores[p], axis=0, keepdims=True) - missing)
            fade = jnp.exp(old_top - top)
            e = jnp.exp(scores[p] - (top + missing))
            total = old_total * fade + jnp.sum(e, axis=0, keepdims=True)
            attended = diagonal(matmul(value_turned[p], e.astype(jnp.bfloat16)))
            attended = attended + attended_in[h, p] * per_head(fade)
            dots = grad_turned[h, p].astype(jnp.float32) * attended
            dot = jnp.concatenate(
                [jnp.sum(dots[:64], axis=0, keepdims=True), jnp.sum(dots[64:], axis=0, keepdims=True)], axis=1
            )
            scale = 1.0 / total
            delta = dot * scale
            finals[h, p : p + 1, :] = top + jnp.log(total)
            finals[h, 4 + p : 5 + p, :] = delta
            prob = e * scale
            half.append(prob.astype(jnp.bfloat16))
            score_grad.append((prob * (g[p] - delta)).astype(jnp.bfloat16))
        for p in patches:
            back = (left_back, right_back)[p % 2]
            back[0, p // 2, :, cols(h)] = matmul(score_grad[p], query_pairs[h, p]).astype(jnp.bfloat16)
            back[1, p // 2, :, cols(h)] = matmul(half[p], grad_pairs[h, p]).astype(jnp.bfloat16)
            dq_out[h, p] = diagonal(matmul(key_turned[p], score_grad[p]))
        return carry

    lax.fori_loop(0, PAIRS, step, 0)


def patch_gradients(h, p, key_rows, value_rows, key_turned, listed, places, finals, query_pairs, grad_pairs):
    half, score_grad = gradients(
        product(key_rows, query_pairs[h, p]),
        product(value_rows, grad_pairs[h, p]),
        [penalty(listed, p, w) for w in places],
        finals[h, p : p + 1, :],
        finals[h, 4 + p : 5 + p, :],
    )
    dk = matmul(score_grad, query_pairs[h, p])
    dv = matmul(half, grad_pairs[h, p])
    return dk, dv, diagonal(matmul(key_turned, score_grad))


def edge_kernel(
    listed, finals, query_pairs, grad_pairs, dq_in, from_up, from_down, from_left, from_right,
    up_sum, down_sum, left_back, right_back, dq_out,
):
    ends = ((from_up, UP), (from_down, DOWN))
    sides = ((from_left, LEFT), (from_right, RIGHT))

    def step(h, carry):
        def rows(source, n):
            return source[n, :, :, cols(h)].reshape(256, 128)

        end_sums, side_sums = [0.0, 0.0], [0.0, 0.0]
        for p in range(4):
            s, c = p // 2, p % 2
            pair = ends[s], sides[c]
            key_rows = jnp.concatenate([rows(source, 0) for source, _ in pair], axis=0)
            value_rows = jnp.concatenate([rows(source, 1) for source, _ in pair], axis=0)
            dk, dv, dq = patch_gradients(
                h, p, key_rows, value_rows, key_rows.T, listed, pair[0][1] + pair[1][1],
                finals, query_pairs, grad_pairs,
            )
            dq_out[h, p] = dq_in[h, p] + dq
            both = jnp.concatenate([dk, dv], axis=1)
            end_sums[s] = end_sums[s] + both[:256]
            side_sums[c] = side_sums[c] + both[256:]
        for s, back in enumerate((up_sum, down_sum)):
            for at in range(2):
                for n in range(2):
                    back[n, at, :, cols(h)] = end_sums[s][128 * at : 128 * (at + 1), 128 * n : 128 * (n + 1)]
        for c, back in enumerate((left_back, right_back)):
            for at in range(2):
                for n in range(2):
                    part = side_sums[c][128 * at : 128 * (at + 1), 128 * n : 128 * (n + 1)]
                    back[n, at, :, cols(h)] = part.astype(jnp.bfloat16)
        return carry

    lax.fori_loop(0, PAIRS, step, 0)


def add_kernel(listed, up_sum, down_sum, add_left, add_right, up_back, down_back):
    for n in range(2):
        for s, (total, back) in enumerate(((up_sum, up_back), (down_sum, down_back))):
            for at, added in enumerate((add_left, add_right)):
                back[n, at] = (total[n, at] + added[n, s].astype(jnp.float32)).astype(jnp.bfloat16)


def last_kernel(listed, own_key, own_value, left, right, up, down, key_grad, value_grad):
    for n, (own, out) in enumerate(((own_key, key_grad), (own_value, value_grad))):
        for p in range(4):
            s, c = p // 2, p % 2
            beside = (left, right)[c][n, s].astype(jnp.float32)
            end = (up, down)[s][n, c].astype(jnp.float32)
            total = own[128 * p : 128 * (p + 1), :] + beside + end
            out[s, c] = total.astype(jnp.bfloat16)


def own_kernel(
    listed, finals, query_pairs, grad_pairs, key, value, dq_in, own_key, own_value, query_grad
):
    def step(h, carry):
        key_rows, value_rows = key[:, cols(h)], value[:, cols(h)]
        key_turned = key_rows.T
        dk, dv = 0.0, 0.0
        for p in range(4):
            more_dk, more_dv, dq = patch_gradients(
                h, p, key_rows, value_rows, key_turned, listed, OWN, finals, query_pairs, grad_pairs
            )
            dk, dv = dk + more_dk, dv + more_dv
            query_grad[p, :, cols(h)] = (SCALING * (dq_in[h, p] + dq).T).astype(jnp.bfloat16)
        own_key[:, cols(h)] = dk
        own_value[:, cols(h)] = dv
        return carry

    lax.fori_loop(0, PAIRS, step, 0)


BF16, F32 = jnp.bfloat16, jnp.float32
TILE = (PATCH, D)
IN_VMEM = pl.BlockSpec(memory_space=pltpu.VMEM)
IN_SMEM = pl.BlockSpec(memory_space=pltpu.SMEM)


def call(kernel, outs, flops, listed, *args):
    return pl.pallas_call(
        kernel,
        out_shape=[jax.ShapeDtypeStruct(shape, kind) for shape, kind in outs],
        in_specs=[IN_SMEM] + [IN_VMEM] * len(args),
        out_specs=[IN_VMEM] * len(outs),
        compiler_params=pltpu.CompilerParams(vmem_limit_bytes=40 * 1024 * 1024),
        cost_estimate=pl.CostEstimate(flops=flops, bytes_accessed=10**6, transcendentals=0),
    )(listed, *args)


PAIR_SHAPE = ((PAIRS, 4, 256, 128), BF16)
TURNED = ((PAIRS, 4, 128, PATCH), F32)
STATS = ((PAIRS, 8, 256), F32)
TWO = ((2, 2) + TILE, BF16)


def local(query_tiles, key_tiles, value_tiles, out_grad, mix_gain, partners, counts):
    span_at, chord_at = lax.axis_index("span"), lax.axis_index("chord")
    span_end, chord_end = lax.axis_size("span") - 1, lax.axis_size("chord") - 1
    chord_total = 2 * lax.axis_size("chord")
    span_pos = partners // chord_total - 2 * span_at + 1
    chord_pos = partners % chord_total - 2 * chord_at + 1
    slots = (span_pos * 4 + chord_pos).reshape(4, 8, 1)
    live = lax.broadcasted_iota(jnp.int32, (4, 8, 16), 1) < counts.reshape(4, 1, 1)
    matches = slots == lax.broadcasted_iota(jnp.int32, (4, 8, 16), 2)
    listed = jnp.any(live & matches, axis=1).astype(jnp.int32).reshape(64)
    inside = jnp.stack([span_at > 0, span_at < span_end, chord_at > 0, chord_at < chord_end])
    gain = jnp.concatenate([mix_gain, jnp.where(inside[:, None], mix_gain, 0.0)], axis=0)

    def packed(*index):
        return jnp.stack([x[index] for x in (key_tiles, value_tiles, out_grad)])

    every = slice(None)
    from_up = shifted(packed(1), 1, 0)
    from_down = shifted(packed(0), -1, 0)
    from_left = shifted(packed(every, 1), 0, 1)
    from_right = shifted(packed(every, 0), 0, -1)

    def corners(c):
        return jnp.stack([from_up[:2, c], from_down[:2, c]], axis=1)

    corner_left = shifted(corners(1), 0, 1)
    corner_right = shifted(corners(0), 0, -1)

    key_rows, value_rows = key_tiles.reshape(4 * PATCH, D), value_tiles.reshape(4 * PATCH, D)
    query_pairs, stats, attended = call(
        own_totals_kernel, [PAIR_SHAPE, STATS, TURNED], 6 * 10**9,
        listed, query_tiles.reshape((4,) + TILE), key_rows, value_rows,
    )
    grad_pairs, grad_turned, stats, attended = call(
        edge_totals_kernel, [PAIR_SHAPE, ((PAIRS, 4, 128, PATCH), BF16), STATS, TURNED], 6 * 10**9,
        listed, gain, out_grad, query_pairs, stats, attended, from_up, from_down, from_left, from_right,
    )
    pairs = query_pairs, grad_pairs
    finals, left_back, right_back, dq = call(
        corner_kernel, [STATS, TWO, TWO, TURNED], 2 * 10**9,
        listed, stats, attended, *pairs, grad_turned, corner_left, corner_right,
    )
    add_right = shifted(left_back, 0, -1)
    add_left = shifted(right_back, 0, 1)
    wide = ((2, 2) + TILE, F32)
    up_sum, down_sum, left_back, right_back, dq = call(
        edge_kernel, [wide, wide, TWO, TWO, TURNED], 8 * 10**9,
        listed, finals, *pairs, dq, from_up, from_down, from_left, from_right,
    )
    up_back, down_back = call(
        add_kernel, [TWO, TWO], 10**7, listed, up_sum, down_sum, add_left, add_right
    )
    end_down = shifted(up_back, -1, 0)
    end_up = shifted(down_back, 1, 0)
    side_right = shifted(left_back, 0, -1)
    side_left = shifted(right_back, 0, 1)
    own_key, own_value, query_grad = call(
        own_kernel, [((4 * PATCH, D), F32), ((4 * PATCH, D), F32), ((4,) + TILE, BF16)], 10**10,
        listed, finals, *pairs, key_rows, value_rows, dq,
    )

    key_grad, value_grad = call(
        last_kernel, [TWO, TWO], 10**7,
        listed, own_key, own_value, side_left, side_right, end_up, end_down,
    )
    return (query_grad.reshape((2, 2) + TILE), key_grad, value_grad)


def solution(mesh):
    tiles = P("span", "chord", None, None)
    in_specs = (tiles, tiles, tiles, tiles, P(), P("span", "chord", None), P("span", "chord"))
    return jax.shard_map(
        local, mesh=mesh, in_specs=in_specs, out_specs=(tiles, tiles, tiles), check_vma=False
    )
```

profile of v0, /device:TPU:0, one launch (start us, length us, event | category | flops | bytes accessed | tf_op | source)
XLA Modules:
  0.0 73.3 jit_solution(9072346754228987604)
XLA Ops:
  0.7 1.2 %fusion.7 = (bf16[1,2,128,512]{3,2,1,0:T(8,128)(2,1)S(1)}, bf16[1,2,128,512]{3,2,1,0:T(8,128)(2,1)S(1)}) fusion(bf16[2,2,128,512]{3,2,1,0:T(8,128)(2,1)} %grad.1), kind=kLoop, calls=%fused_computation.30 | loop fusion | bytes 1048576 | tf_op jit(solution)/shard_map/slice | solution.py:347
  1.8 0.2 copy-done.1
  2.0 0.1 fusion.5
  2.1 1.0 %pad_maximum_fusion = bf16[3,2,128,512]{3,2,1,0:T(8,128)(2,1)} fusion(bf16[1,2,128,512]{3,2,1,0:T(8,128)(2,1)S(1)} %get-tuple-element.64, bf16[1,2,128,512]{3,2,1,0:T(8,128)(2,1)S(1)} %get-tuple-element.65, bf16[1,2,128,512]{3,2,1,0:T(8,128)(2,1)S(1)} %get-tuple-element.60), kind=kLoop, calls=%fused_computation | loop fusion | flops 786432 | bytes 1572864 | tf_op jit(solution)/shard_map/stack | solution.py:347
  3.1 1.7 %collective-permute-start = (bf16[3,2,128,512]{3,2,1,0:T(8,128)(2,1)}, bf16[3,2,128,512]{3,2,1,0:T(8,128)(2,1)S(1)}, u32[]{:S(2)}, u32[]{:S(2)}) collective-permute-start(bf16[3,2,128,512]{3,2,1,0:T(8,128)(2,1)} %pad_maximum_fusion), channel_id=1, source_target_pairs={{0,8},{1,9},{2,10},{3,11},{4,12},{5,13},{6,14},{7,15},{8,16},{9,17... | collective-permute-start | bytes 2359304 | tf_op jit(solution)/shard_map/ppermute | solution.py:29
  4.8 1.0 %pad_maximum_fusion.1 = bf16[3,2,128,512]{3,2,1,0:T(8,128)(2,1)} fusion(bf16[1,2,128,512]{3,2,1,0:T(8,128)(2,1)S(1)} %get-tuple-element.63, bf16[1,2,128,512]{3,2,1,0:T(8,128)(2,1)S(1)} %get-tuple-element.66, bf16[1,2,128,512]{3,2,1,0:T(8,128)(2,1)S(1)} %get-tuple-element.59), kind=kLoop, calls=%fused_computation.1 | loop fusion | flops 786432 | bytes 1572864 | tf_op jit(solution)/shard_map/stack | solution.py:347
  5.8 4.9 %collective-permute-start.1 = (bf16[3,2,128,512]{3,2,1,0:T(8,128)(2,1)}, bf16[3,2,128,512]{3,2,1,0:T(8,128)(2,1)S(1)}, u32[]{:S(2)}, u32[]{:S(2)}) collective-permute-start(bf16[3,2,128,512]{3,2,1,0:T(8,128)(2,1)} %pad_maximum_fusion.1), channel_id=1, source_target_pairs={{0,120},{1,121},{2,122},{3,123},{4,124},{5,125},{6,126},{7,127},{8... | collective-permute-start | bytes 2359304 | tf_op jit(solution)/shard_map/ppermute | solution.py:29
  10.7 0.1 slice_bitcast_fusion
  10.9 1.0 %pad_maximum_fusion.2 = bf16[3,2,128,512]{3,2,1,0:T(8,128)(2,1)} fusion(bf16[1,2,128,512]{3,2,1,0:T(8,128)(2,1)S(1)} %get-tuple-element.58, bf16[1,2,128,512]{3,2,1,0:T(8,128)(2,1)S(1)} %get-tuple-element.67, bf16[1,2,128,512]{3,2,1,0:T(8,128)(2,1)S(1)} %get-tuple-element.54), kind=kLoop, calls=%fused_computation.2 | loop fusion | flops 786432 | bytes 1572864 | tf_op jit(solution)/shard_map/stack | solution.py:347
  11.8 1.0 %pad_maximum_fusion.3 = bf16[3,2,128,512]{3,2,1,0:T(8,128)(2,1)} fusion(bf16[1,2,128,512]{3,2,1,0:T(8,128)(2,1)S(1)} %get-tuple-element.57, bf16[1,2,128,512]{3,2,1,0:T(8,128)(2,1)S(1)} %get-tuple-element.68, bf16[1,2,128,512]{3,2,1,0:T(8,128)(2,1)S(1)} %get-tuple-element.53), kind=kLoop, calls=%fused_computation.3 | loop fusion | flops 786432 | bytes 1572864 | tf_op jit(solution)/shard_map/stack | solution.py:347
  12.8 3.0 %collective-permute-start.3 = (bf16[3,2,128,512]{3,2,1,0:T(8,128)(2,1)}, bf16[3,2,128,512]{3,2,1,0:T(8,128)(2,1)}, u32[]{:S(2)}, u32[]{:S(2)}) collective-permute-start(bf16[3,2,128,512]{3,2,1,0:T(8,128)(2,1)} %pad_maximum_fusion.3), channel_id=1, source_target_pairs={{0,7},{1,0},{2,1},{3,2},{4,3},{5,4},{6,5},{7,6},{8,15},{9,8},{10,9... | collective-permute-start | bytes 2359304 | tf_op jit(solution)/shard_map/ppermute | solution.py:29
  15.8 0.1 lt.22
  15.8 0.1 pad_add_fusion
  15.9 0.5 copy-done.4
  16.5 0.6 copy-done.5
  17.2 0.1 fusion.1
  17.3 0.1 reshape.31.listed
  17.3 1.0 %copy-done.3 = bf16[2,2,128,512]{3,2,1,0:T(8,128)(2,1)S(1)} copy-done((bf16[2,2,128,512]{3,2,1,0:T(8,128)(2,1)S(1)}, bf16[2,2,128,512]{3,2,1,0:T(8,128)(2,1)}, u32[]{:S(2)}) %copy-start.3) | copy-done | bytes 524312
  18.4 6.4 %shard_map.94 = (bf16[4,4,256,128]{3,2,1,0:T(8,128)(2,1)S(1)}, f32[4,8,256]{2,1,0:T(8,128)S(1)}, f32[4,4,128,128]{3,2,1,0:T(8,128)S(1)}) custom-call(s32[64]{0:T(128)S(1)} %reshape.31.listed, bf16[4,128,512]{2,1,0:T(8,128)(2,1)S(1)} %bitcast.37, bf16[512,512]{1,0:T(8,128)(2,1)S(1)} %bitcast.33, bf16[512,512]{1,0:T(8,128)(2,1)S(1)} %bitcast.35), custom_call_target="tpu_custom_call" | custom-call | flops 6000000000 | bytes 1000000 | tf_op jit(solution)/shard_map/pallas_call | solution.py:317
  24.8 2.6 %collective-permute-done.from_up = bf16[3,2,128,512]{3,2,1,0:T(8,128)(2,1)S(1)} collective-permute-done((bf16[3,2,128,512]{3,2,1,0:T(8,128)(2,1)}, bf16[3,2,128,512]{3,2,1,0:T(8,128)(2,1)S(1)}, u32[]{:S(2)}, u32[]{:S(2)}) %collective-permute-start) | collective-permute-done | bytes 786464 | tf_op jit(solution)/shard_map/ppermute | solution.py:29
  27.5 0.3 collective-permute-done.1.from_down
  28.0 2.9 %collective-permute-start.5 = (bf16[2,2,128,512]{3,2,1,0:T(8,128)(2,1)S(1)}, bf16[2,2,128,512]{3,2,1,0:T(8,128)(2,1)S(1)}, u32[]{:S(2)}, u32[]{:S(2)}) collective-permute-start(bf16[2,2,128,512]{3,2,1,0:T(8,128)(2,1)S(1)} %pad_maximum_fusion.5), channel_id=1, source_target_pairs={{0,7},{1,0},{2,1},{3,2},{4,3},{5,4},{6,5},{7,6},{8,15},{9,8},{10,9... | collective-permute-start | bytes 1572872 | tf_op jit(solution)/shard_map/ppermute | solution.py:29
  30.9 7.6 %shard_map.95 = (bf16[4,4,256,128]{3,2,1,0:T(8,128)(2,1)S(1)}, bf16[4,4,128,128]{3,2,1,0:T(8,128)(2,1)S(1)}, f32[4,8,256]{2,1,0:T(8,128)S(1)}, f32[4,4,128,128]{3,2,1,0:T(8,128)S(1)}) custom-call(s32[64]{0:T(128)S(1)} %reshape.31.listed, f32[8,512]{1,0:T(8,128)S(1)} %pad_maximum_fusion.6.gain, bf16[2,2,128,512]{3,2,1,0:T(8,128)(2,1)S(1)} %copy-done, ...), custom_call_target="tpu_custom_call" | custom-call | flops 6000000000 | bytes 1000000 | tf_op jit(solution)/shard_map/pallas_call | solution.py:317
  38.5 3.9 %shard_map.96 = (f32[4,8,256]{2,1,0:T(8,128)S(1)}, bf16[2,2,128,512]{3,2,1,0:T(8,128)(2,1)S(1)}, bf16[2,2,128,512]{3,2,1,0:T(8,128)(2,1)S(1)}, f32[4,4,128,128]{3,2,1,0:T(8,128)S(1)}) custom-call(s32[64]{0:T(128)S(1)} %reshape.31.listed, f32[4,8,256]{2,1,0:T(8,128)S(1)} %get-tuple-element.29.stats_in, f32[4,4,128,128]{3,2,1,0:T(8,128)S(1)} %get-tuple-element.30.attended_in, ...), custom_call_target="tpu_custom_call" | custom-call | flops 2000000000 | bytes 1000000 | tf_op jit(solution)/shard_map/pallas_call | solution.py:317
  42.5 2.9 %collective-permute-start.9 = (bf16[2,2,128,512]{3,2,1,0:T(8,128)(2,1)S(1)}, bf16[2,2,128,512]{3,2,1,0:T(8,128)(2,1)S(1)}, u32[]{:S(2)}, u32[]{:S(2)}) collective-permute-start(bf16[2,2,128,512]{3,2,1,0:T(8,128)(2,1)S(1)} %get-tuple-element.44), channel_id=1, source_target_pairs={{0,7},{1,0},{2,1},{3,2},{4,3},{5,4},{6,5},{7,6},{8,15},{9,8},{10,9... | collective-permute-start | bytes 1572872 | tf_op jit(solution)/shard_map/ppermute | solution.py:29
  45.4 7.0 %shard_map.97 = (f32[2,2,128,512]{3,2,1,0:T(8,128)S(1)}, f32[2,2,128,512]{3,2,1,0:T(8,128)S(1)}, bf16[2,2,128,512]{3,2,1,0:T(8,128)(2,1)S(1)}, bf16[2,2,128,512]...) custom-call(s32[64]{0:T(128)S(1)} %reshape.31.listed, f32[4,8,256]{2,1,0:T(8,128)S(1)} %get-tuple-element.33.finals, ...), custom_call_target="tpu_custom_call" | custom-call | flops 8000000000 | bytes 1000000 | tf_op jit(solution)/shard_map/pallas_call | solution.py:317
  52.4 2.9 %collective-permute-start.7 = (bf16[2,2,128,512]{3,2,1,0:T(8,128)(2,1)S(1)}, bf16[2,2,128,512]{3,2,1,0:T(8,128)(2,1)S(1)}, u32[]{:S(2)}, u32[]{:S(2)}) collective-permute-start(bf16[2,2,128,512]{3,2,1,0:T(8,128)(2,1)S(1)} %get-tuple-element.40), channel_id=1, source_target_pairs={{0,7},{1,0},{2,1},{3,2},{4,3},{5,4},{6,5},{7,6},{8,15},{9,8},{10,9... | collective-permute-start | bytes 1572872 | tf_op jit(solution)/shard_map/ppermute | solution.py:29
  55.4 0.7 shard_map.99
  56.2 5.8 %collective-permute-start.11 = (bf16[2,2,128,512]{3,2,1,0:T(8,128)(2,1)S(1)}, bf16[2,2,128,512]{3,2,1,0:T(8,128)(2,1)S(1)}, u32[]{:S(2)}, u32[]{:S(2)}) collective-permute-start(bf16[2,2,128,512]{3,2,1,0:T(8,128)(2,1)S(1)} %get-tuple-element.46), channel_id=1, source_target_pairs={{0,120},{1,121},{2,122},{3,123},{4,124},{5,125},{6,126},{7,127},{8... | collective-permute-start | bytes 1572872 | tf_op jit(solution)/shard_map/ppermute | solution.py:29
  62.0 7.8 %shard_map.98 = (f32[512,512]{1,0:T(8,128)S(1)}, f32[512,512]{1,0:T(8,128)S(1)}, bf16[4,128,512]{2,1,0:T(8,128)(2,1)}) custom-call(s32[64]{0:T(128)S(1)} %reshape.31.listed, f32[4,8,256]{2,1,0:T(8,128)S(1)} %get-tuple-element.33.finals, bf16[4,4,256,128]{3,2,1,0:T(8,128)(2,1)S(1)} %get-tuple-element.26.query_pairs, ...), custom_call_target="tpu_custom_call" | custom-call | flops 10000000000 | bytes 1000000 | tf_op jit(solution)/shard_map/pallas_call | solution.py:317
  69.7 1.8 %collective-permute-done.10.up = bf16[2,2,128,512]{3,2,1,0:T(8,128)(2,1)S(1)} collective-permute-done((bf16[2,2,128,512]{3,2,1,0:T(8,128)(2,1)S(1)}, bf16[2,2,128,512]{3,2,1,0:T(8,128)(2,1)S(1)}, u32[]{:S(2)}, u32[]{:S(2)}) %collective-permute-start.10) | collective-permute-done | bytes 524320 | tf_op jit(solution)/shard_map/ppermute | solution.py:29
  71.5 1.7 %shard_map.100 = (bf16[2,2,128,512]{3,2,1,0:T(8,128)(2,1)}, bf16[2,2,128,512]{3,2,1,0:T(8,128)(2,1)}) custom-call(s32[64]{0:T(128)S(1)} %reshape.31.listed, f32[512,512]{1,0:T(8,128)S(1)} %get-tuple-element.37.own_key, f32[512,512]{1,0:T(8,128)S(1)} %get-tuple-element.38.own_value, bf16[2,2,128,512]{3,2,1,0:T(8,128)(2,1)S(1)} %collective-permute-done.6.left, ...), custom_call_target="tpu_custom_call" | custom-call | flops 10000000 | bytes 1000000 | tf_op jit(solution)/shard_map/pallas_call | solution.py:317
  (33 shorter events, 0.5 us)
Async XLA Ops:
  0.6 1.2 %copy-start.2 = (bf16[2,2,128,512]{3,2,1,0:T(8,128)(2,1)S(1)}, bf16[2,2,128,512]{3,2,1,0:T(8,128)(2,1)}, u32[]{:S(2)}) copy-start(bf16[2,2,128,512]{3,2,1,0:T(8,128)(2,1)} %param.9) | copy-start | bytes 1572868
  0.6 1.3 %copy-start.1 = (bf16[2,2,128,512]{3,2,1,0:T(8,128)(2,1)S(1)}, bf16[2,2,128,512]{3,2,1,0:T(8,128)(2,1)}, u32[]{:S(2)}) copy-start(bf16[2,2,128,512]{3,2,1,0:T(8,128)(2,1)} %param.8) | copy-start | bytes 1572868
  3.1 24.3 %collective-permute-start = (bf16[3,2,128,512]{3,2,1,0:T(8,128)(2,1)}, bf16[3,2,128,512]{3,2,1,0:T(8,128)(2,1)S(1)}, u32[]{:S(2)}, u32[]{:S(2)}) collective-permute-start(bf16[3,2,128,512]{3,2,1,0:T(8,128)(2,1)} %pad_maximum_fusion), channel_id=1, source_target_pairs={{0,8},{1,9},{2,10},{3,11},{4,12},{5,13},{6,14},{7,15},{8,16},{9,17... | collective-permute-start | bytes 2359304 | tf_op jit(solution)/shard_map/ppermute | solution.py:29
  5.8 5.0 %copy-start = (bf16[2,2,128,512]{3,2,1,0:T(8,128)(2,1)S(1)}, bf16[2,2,128,512]{3,2,1,0:T(8,128)(2,1)}, u32[]{:S(2)}) copy-start(bf16[2,2,128,512]{3,2,1,0:T(8,128)(2,1)} %grad.1) | copy-start | bytes 1572868
  5.8 22.0 %collective-permute-start.1 = (bf16[3,2,128,512]{3,2,1,0:T(8,128)(2,1)}, bf16[3,2,128,512]{3,2,1,0:T(8,128)(2,1)S(1)}, u32[]{:S(2)}, u32[]{:S(2)}) collective-permute-start(bf16[3,2,128,512]{3,2,1,0:T(8,128)(2,1)} %pad_maximum_fusion.1), channel_id=1, source_target_pairs={{0,120},{1,121},{2,122},{3,123},{4,124},{5,125},{6,126},{7,127},{8... | collective-permute-start | bytes 2359304 | tf_op jit(solution)/shard_map/ppermute | solution.py:29
  11.8 19.1 %collective-permute-start.2 = (bf16[3,2,128,512]{3,2,1,0:T(8,128)(2,1)}, bf16[3,2,128,512]{3,2,1,0:T(8,128)(2,1)}, u32[]{:S(2)}, u32[]{:S(2)}) collective-permute-start(bf16[3,2,128,512]{3,2,1,0:T(8,128)(2,1)} %pad_maximum_fusion.2), channel_id=1, source_target_pairs={{0,1},{1,2},{2,3},{3,4},{4,5},{5,6},{6,7},{7,0},{8,9},{9,10},{10,1... | collective-permute-start | bytes 2359304 | tf_op jit(solution)/shard_map/ppermute | solution.py:29
  11.8 3.9 %copy-start.6 = (s32[2,2]{1,0:T(2,128)S(1)}, s32[2,2]{1,0:T(2,128)}, u32[]{:S(2)}) copy-start(s32[2,2]{1,0:T(2,128)} %param.13) | copy-start | bytes 52
  12.8 18.1 %collective-permute-start.3 = (bf16[3,2,128,512]{3,2,1,0:T(8,128)(2,1)}, bf16[3,2,128,512]{3,2,1,0:T(8,128)(2,1)}, u32[]{:S(2)}, u32[]{:S(2)}) collective-permute-start(bf16[3,2,128,512]{3,2,1,0:T(8,128)(2,1)} %pad_maximum_fusion.3), channel_id=1, source_target_pairs={{0,7},{1,0},{2,1},{3,2},{4,3},{5,4},{6,5},{7,6},{8,15},{9,8},{10,9... | collective-permute-start | bytes 2359304 | tf_op jit(solution)/shard_map/ppermute | solution.py:29
  15.8 0.7 copy-start.4
  16.5 0.7 copy-start.5
  17.3 1.0 %copy-start.3 = (bf16[2,2,128,512]{3,2,1,0:T(8,128)(2,1)S(1)}, bf16[2,2,128,512]{3,2,1,0:T(8,128)(2,1)}, u32[]{:S(2)}) copy-start(bf16[2,2,128,512]{3,2,1,0:T(8,128)(2,1)} %param.7) | copy-start | bytes 1572868
  27.9 10.6 %collective-permute-start.4 = (bf16[2,2,128,512]{3,2,1,0:T(8,128)(2,1)S(1)}, bf16[2,2,128,512]{3,2,1,0:T(8,128)(2,1)S(1)}, u32[]{:S(2)}, u32[]{:S(2)}) collective-permute-start(bf16[2,2,128,512]{3,2,1,0:T(8,128)(2,1)S(1)} %pad_maximum_fusion.4), channel_id=1, source_target_pairs={{0,1},{1,2},{2,3},{3,4},{4,5},{5,6},{6,7},{7,0},{8,9},{9,10},{10,1... | collective-permute-start | bytes 1572872 | tf_op jit(solution)/shard_map/ppermute | solution.py:29
  28.0 10.5 %collective-permute-start.5 = (bf16[2,2,128,512]{3,2,1,0:T(8,128)(2,1)S(1)}, bf16[2,2,128,512]{3,2,1,0:T(8,128)(2,1)S(1)}, u32[]{:S(2)}, u32[]{:S(2)}) collective-permute-start(bf16[2,2,128,512]{3,2,1,0:T(8,128)(2,1)S(1)} %pad_maximum_fusion.5), channel_id=1, source_target_pairs={{0,7},{1,0},{2,1},{3,2},{4,3},{5,4},{6,5},{7,6},{8,15},{9,8},{10,9... | collective-permute-start | bytes 1572872 | tf_op jit(solution)/shard_map/ppermute | solution.py:29
  42.5 12.9 %collective-permute-start.8 = (bf16[2,2,128,512]{3,2,1,0:T(8,128)(2,1)S(1)}, bf16[2,2,128,512]{3,2,1,0:T(8,128)(2,1)S(1)}, u32[]{:S(2)}, u32[]{:S(2)}) collective-permute-start(bf16[2,2,128,512]{3,2,1,0:T(8,128)(2,1)S(1)} %get-tuple-element.43), channel_id=1, source_target_pairs={{0,1},{1,2},{2,3},{3,4},{4,5},{5,6},{6,7},{7,0},{8,9},{9,10},{10,1... | collective-permute-start | bytes 1572872 | tf_op jit(solution)/shard_map/ppermute | solution.py:29
  42.5 12.9 %collective-permute-start.9 = (bf16[2,2,128,512]{3,2,1,0:T(8,128)(2,1)S(1)}, bf16[2,2,128,512]{3,2,1,0:T(8,128)(2,1)S(1)}, u32[]{:S(2)}, u32[]{:S(2)}) collective-permute-start(bf16[2,2,128,512]{3,2,1,0:T(8,128)(2,1)S(1)} %get-tuple-element.44), channel_id=1, source_target_pairs={{0,7},{1,0},{2,1},{3,2},{4,3},{5,4},{6,5},{7,6},{8,15},{9,8},{10,9... | collective-permute-start | bytes 1572872 | tf_op jit(solution)/shard_map/ppermute | solution.py:29
  52.4 17.3 %collective-permute-start.6 = (bf16[2,2,128,512]{3,2,1,0:T(8,128)(2,1)S(1)}, bf16[2,2,128,512]{3,2,1,0:T(8,128)(2,1)S(1)}, u32[]{:S(2)}, u32[]{:S(2)}) collective-permute-start(bf16[2,2,128,512]{3,2,1,0:T(8,128)(2,1)S(1)} %get-tuple-element.39), channel_id=1, source_target_pairs={{0,1},{1,2},{2,3},{3,4},{4,5},{5,6},{6,7},{7,0},{8,9},{9,10},{10,1... | collective-permute-start | bytes 1572872 | tf_op jit(solution)/shard_map/ppermute | solution.py:29
  52.4 17.3 %collective-permute-start.7 = (bf16[2,2,128,512]{3,2,1,0:T(8,128)(2,1)S(1)}, bf16[2,2,128,512]{3,2,1,0:T(8,128)(2,1)S(1)}, u32[]{:S(2)}, u32[]{:S(2)}) collective-permute-start(bf16[2,2,128,512]{3,2,1,0:T(8,128)(2,1)S(1)} %get-tuple-element.40), channel_id=1, source_target_pairs={{0,7},{1,0},{2,1},{3,2},{4,3},{5,4},{6,5},{7,6},{8,15},{9,8},{10,9... | collective-permute-start | bytes 1572872 | tf_op jit(solution)/shard_map/ppermute | solution.py:29
  56.1 15.4 %collective-permute-start.10 = (bf16[2,2,128,512]{3,2,1,0:T(8,128)(2,1)S(1)}, bf16[2,2,128,512]{3,2,1,0:T(8,128)(2,1)S(1)}, u32[]{:S(2)}, u32[]{:S(2)}) collective-permute-start(bf16[2,2,128,512]{3,2,1,0:T(8,128)(2,1)S(1)} %get-tuple-element.45), channel_id=1, source_target_pairs={{0,8},{1,9},{2,10},{3,11},{4,12},{5,13},{6,14},{7,15},{8,16},{9,17... | collective-permute-start | bytes 1572872 | tf_op jit(solution)/shard_map/ppermute | solution.py:29
  56.2 15.4 %collective-permute-start.11 = (bf16[2,2,128,512]{3,2,1,0:T(8,128)(2,1)S(1)}, bf16[2,2,128,512]{3,2,1,0:T(8,128)(2,1)S(1)}, u32[]{:S(2)}, u32[]{:S(2)}) collective-permute-start(bf16[2,2,128,512]{3,2,1,0:T(8,128)(2,1)S(1)} %get-tuple-element.46), channel_id=1, source_target_pairs={{0,120},{1,121},{2,122},{3,123},{4,124},{5,125},{6,126},{7,127},{8... | collective-permute-start | bytes 1572872 | tf_op jit(solution)/shard_map/ppermute | solution.py:29
where the time goes:
time: 73.6 us; the launch traced here: 73.3 us
  Pallas kernels  35.1 us (48%)
  starting transfers between devices  24.3 us (33%)
  waiting for transfers between devices  4.8 us (7%)
  other arithmetic  4.34 us (6%)
  local copies, waits for them, and re-layouts  4.01 us (5%)
  between operations  0.81 us (1%)
    pallas_call x7, Pallas kernels, call(): pl.pallas_call(kernel, out_shape=[jax.ShapeDtypeStruct(shape, kind) for s...  35.1 us
    ppermute x12, starting transfers between devices, shifted(): return lax.ppermute(x, ('span', 'chord'), pairs)  24.3 us
    ppermute x12, waiting for transfers between devices, shifted(): return lax.ppermute(x, ('span', 'chord'), pairs)  4.8 us
    another operation x4, other arithmetic, packed(): return jnp.stack([x[index] for x in (key_tiles, value_tiles, out_grad)])  3.96 us
    unnamed x14, local copies, waits for them, and re-layouts  2.38 us
  transfers between devices with their start and end apart: 12, of which 3 were waited for; matrix products, arithmetic and copies ran while one was open for 5% of the time, Pallas kernels for 40%

commit v1 on v0

--- a/solution.py
+++ b/solution.py
@@ -94,7 +94,20 @@
     return top, total, turned
 
 
-def own_totals_kernel(listed, query, key, value, query_pairs, stats_out, attended_out):
+def own_totals_kernel(
+    chord_total, partners, counts, query, key, value, listed, query_pairs, stats_out, attended_out
+):
+    for i in range(72):
+        listed[i] = 0
+    for p in range(4):
+        s, c = p // 2, p % 2
+        own = partners[s, c, 0]
+        for j in range(8):
+            other = partners[s, c, j]
+            row = 1 + s + lax.div(other, chord_total) - lax.div(own, chord_total)
+            column = 1 + c + lax.rem(other, chord_total) - lax.rem(own, chord_total)
+            listed[jnp.where(j < counts[s, c], p * 16 + row * 4 + column, 64)] = 1
+
     def step(h, carry):
         value_turned = value[:, cols(h)].T
         for p in range(4):
@@ -120,8 +133,8 @@
 
 
 def edge_totals_kernel(
-    listed, gain, grad, query_pairs, stats_in, attended_in, from_up, from_down, from_left, from_right,
-    grad_pairs, grad_turned, stats_out, attended_out,
+    listed, query_pairs, stats_in, attended_in, from_up, from_down, from_left, from_right,
+    stats_out, attended_out,
 ):
     ends = ((from_up, UP), (from_down, DOWN))
     sides = ((from_left, LEFT), (from_right, RIGHT))
@@ -133,20 +146,6 @@
         values = {id(source): turned(source) for source, _ in ends + sides}
         for p in range(4):
             s, c = p // 2, p % 2
-            near = (
-                grad[0, c, :, cols(h)] if s == 1 else from_up[2, c, :, cols(h)],
-                grad[1, c, :, cols(h)] if s == 0 else from_down[2, c, :, cols(h)],
-                grad[s, 0, :, cols(h)] if c == 1 else from_left[2, s, :, cols(h)],
-                grad[s, 1, :, cols(h)] if c == 0 else from_right[2, s, :, cols(h)],
-            )
-            own = (s == 1, s == 0, c == 1, c == 0)
-            mixed = grad[s, c, :, cols(h)].astype(jnp.float32)
-            for n in range(4):
-                row = n if own[n] else n + 4
-                mixed = mixed + gain[row : row + 1, cols(h)] * near[n].astype(jnp.float32)
-            mixed = mixed.astype(jnp.bfloat16)
-            grad_pairs[h, p] = stacked_pair(mixed)
-            grad_turned[h, p] = mixed.T
             groups = []
             for source, places in (ends[s], sides[c]):
                 groups.append(
@@ -172,19 +171,47 @@
 
 
 def corner_kernel(
-    listed, stats_in, attended_in, query_pairs, grad_pairs, grad_turned, corner_left, corner_right,
-    finals, left_back, right_back, dq_out,
+    span_total, chord_total, listed, partners, gain, grad, grad_up, grad_down, from_left, from_right,
+    stats_in, attended_in, query_pairs, corner_left, corner_right,
+    grad_pairs, finals, left_back, right_back, dq_out,
 ):
+    first = partners[0, 0, 0]
+    row, column = lax.div(first, chord_total), lax.rem(first, chord_total)
+    inside = [
+        jnp.where(x, 1.0, 0.0)
+        for x in (row > 0, row < span_total - 2, column > 0, column < chord_total - 2)
+    ]
     patches = range(4)
 
     def source(p):
         return (corner_left, corner_right)[p % 2]
 
     def step(h, carry):
+        pairs, grad_turned = [], []
+        for p in patches:
+            s, c = p // 2, p % 2
+            near = (
+                grad[0, c, :, cols(h)] if s == 1 else grad_up[c, :, cols(h)],
+                grad[1, c, :, cols(h)] if s == 0 else grad_down[c, :, cols(h)],
+                grad[s, 0, :, cols(h)] if c == 1 else from_left[2, s, :, cols(h)],
+                grad[s, 1, :, cols(h)] if c == 0 else from_right[2, s, :, cols(h)],
+            )
+            own = (s == 1, s == 0, c == 1, c == 0)
+            mixed = grad[s, c, :, cols(h)].astype(jnp.float32)
+            for n in range(4):
+                factor = gain[n : n + 1, cols(h)]
+                if not own[n]:
+                    factor = factor * inside[n]
+                mixed = mixed + factor * near[n].astype(jnp.float32)
+            mixed = mixed.astype(jnp.bfloat16)
+            pair = stacked_pair(mixed)
+            grad_pairs[h, p] = pair
+            pairs.append(pair)
+            grad_turned.append(mixed.T)
         key_rows = [source(p)[0, p // 2, :, cols(h)] for p in patches]
         value_rows = [source(p)[1, p // 2, :, cols(h)] for p in patches]
         scores = [product(key_rows[p], query_pairs[h, p]) for p in patches]
-        g = [product(value_rows[p], grad_pairs[h, p]) for p in patches]
+        g = [product(value_rows[p], pairs[p]) for p in patches]
         value_turned = [x.T for x in value_rows]
         key_turned = [x.T for x in key_rows]
         half, score_grad = [], []
@@ -197,7 +224,7 @@
             total = old_total * fade + jnp.sum(e, axis=0, keepdims=True)
             attended = diagonal(matmul(value_turned[p], e.astype(jnp.bfloat16)))
             attended = attended + attended_in[h, p] * per_head(fade)
-            dots = grad_turned[h, p].astype(jnp.float32) * attended
+            dots = grad_turned[p].astype(jnp.float32) * attended
             dot = jnp.concatenate(
                 [jnp.sum(dots[:64], axis=0, keepdims=True), jnp.sum(dots[64:], axis=0, keepdims=True)], axis=1
             )
@@ -211,7 +238,7 @@
         for p in patches:
             back = (left_back, right_back)[p % 2]
             back[0, p // 2, :, cols(h)] = matmul(score_grad[p], query_pairs[h, p]).astype(jnp.bfloat16)
-            back[1, p // 2, :, cols(h)] = matmul(half[p], grad_pairs[h, p]).astype(jnp.bfloat16)
+            back[1, p // 2, :, cols(h)] = matmul(half[p], pairs[p]).astype(jnp.bfloat16)
             dq_out[h, p] = diagonal(matmul(key_turned[p], score_grad[p]))
         return carry
 
@@ -270,14 +297,14 @@
     lax.fori_loop(0, PAIRS, step, 0)
 
 
-def add_kernel(listed, up_sum, down_sum, add_left, add_right, up_back, down_back):
+def add_kernel(up_sum, down_sum, add_left, add_right, up_back, down_back):
     for n in range(2):
         for s, (total, back) in enumerate(((up_sum, up_back), (down_sum, down_back))):
             for at, added in enumerate((add_left, add_right)):
                 back[n, at] = (total[n, at] + added[n, s].astype(jnp.float32)).astype(jnp.bfloat16)
 
 
-def last_kernel(listed, own_key, own_value, left, right, up, down, key_grad, value_grad):
+def last_kernel(own_key, own_value, left, right, up, down, key_grad, value_grad):
     for n, (own, out) in enumerate(((own_key, key_grad), (own_value, value_grad))):
         for p in range(4):
             s, c = p // 2, p % 2
@@ -293,13 +320,23 @@
     def step(h, carry):
         key_rows, value_rows = key[:, cols(h)], value[:, cols(h)]
         key_turned = key_rows.T
-        dk, dv = 0.0, 0.0
+        joined_query = jnp.concatenate([query_pairs[h, p] for p in range(4)], axis=0)
+        joined_grad = jnp.concatenate([grad_pairs[h, p] for p in range(4)], axis=0)
+        terms = [
+            gradients(
+                product(key_rows, query_pairs[h, p]),
+                product(value_rows, grad_pairs[h, p]),
+                [penalty(listed, p, w) for w in OWN],
+                finals[h, p : p + 1, :],
+                finals[h, 4 + p : 5 + p, :],
+            )
+            for p in range(4)
+        ]
+        dq = [diagonal(matmul(key_turned, score_grad)) for _, score_grad in terms]
+        dk = matmul(jnp.concatenate([score_grad for _, score_grad in terms], axis=1), joined_query)
+        dv = matmul(jnp.concatenate([half for half, _ in terms], axis=1), joined_grad)
         for p in range(4):
-            more_dk, more_dv, dq = patch_gradients(
-                h, p, key_rows, value_rows, key_turned, listed, OWN, finals, query_pairs, grad_pairs
-            )
-            dk, dv = dk + more_dk, dv + more_dv
-            query_grad[p, :, cols(h)] = (SCALING * (dq_in[h, p] + dq).T).astype(jnp.bfloat16)
+            query_grad[p, :, cols(h)] = (SCALING * (dq_in[h, p] + dq[p]).T).astype(jnp.bfloat16)
         own_key[:, cols(h)] = dk
         own_value[:, cols(h)] = dv
         return carry
@@ -313,15 +350,18 @@
 IN_SMEM = pl.BlockSpec(memory_space=pltpu.SMEM)
 
 
-def call(kernel, outs, flops, listed, *args):
+def call(kernel, outs, flops, *args):
+    def space(kind):
+        return IN_SMEM if kind == jnp.int32 else IN_VMEM
+
     return pl.pallas_call(
         kernel,
         out_shape=[jax.ShapeDtypeStruct(shape, kind) for shape, kind in outs],
-        in_specs=[IN_SMEM] + [IN_VMEM] * len(args),
-        out_specs=[IN_VMEM] * len(outs),
+        in_specs=[space(x.dtype) for x in args],
+        out_specs=[space(kind) for _, kind in outs],
         compiler_params=pltpu.CompilerParams(vmem_limit_bytes=40 * 1024 * 1024),
         cost_estimate=pl.CostEstimate(flops=flops, bytes_accessed=10**6, transcendentals=0),
-    )(listed, *args)
+    )(*args)
 
 
 PAIR_SHAPE = ((PAIRS, 4, 256, 128), BF16)
@@ -331,47 +371,42 @@
 
 
 def local(query_tiles, key_tiles, value_tiles, out_grad, mix_gain, partners, counts):
-    span_at, chord_at = lax.axis_index("span"), lax.axis_index("chord")
-    span_end, chord_end = lax.axis_size("span") - 1, lax.axis_size("chord") - 1
-    chord_total = 2 * lax.axis_size("chord")
-    span_pos = partners // chord_total - 2 * span_at + 1
-    chord_pos = partners % chord_total - 2 * chord_at + 1
-    slots = (span_pos * 4 + chord_pos).reshape(4, 8, 1)
-    live = lax.broadcasted_iota(jnp.int32, (4, 8, 16), 1) < counts.reshape(4, 1, 1)
-    matches = slots == lax.broadcasted_iota(jnp.int32, (4, 8, 16), 2)
-    listed = jnp.any(live & matches, axis=1).astype(jnp.int32).reshape(64)
-    inside = jnp.stack([span_at > 0, span_at < span_end, chord_at > 0, chord_at < chord_end])
-    gain = jnp.concatenate([mix_gain, jnp.where(inside[:, None], mix_gain, 0.0)], axis=0)
-
-    def packed(*index):
-        return jnp.stack([x[index] for x in (key_tiles, value_tiles, out_grad)])
-
+    span_total, chord_total = 2 * lax.axis_size("span"), 2 * lax.axis_size("chord")
     every = slice(None)
-    from_up = shifted(packed(1), 1, 0)
-    from_down = shifted(packed(0), -1, 0)
-    from_left = shifted(packed(every, 1), 0, 1)
-    from_right = shifted(packed(every, 0), 0, -1)
+
+    def packed(tiles, *index):
+        return jnp.stack([x[index] for x in tiles])
+
+    from_up = shifted(packed((key_tiles, value_tiles), 1), 1, 0)
+    from_down = shifted(packed((key_tiles, value_tiles), 0), -1, 0)
+    from_left = shifted(packed((key_tiles, value_tiles, out_grad), every, 1), 0, 1)
+    from_right = shifted(packed((key_tiles, value_tiles, out_grad), every, 0), 0, -1)
 
     def corners(c):
-        return jnp.stack([from_up[:2, c], from_down[:2, c]], axis=1)
+        return jnp.stack([from_up[:, c], from_down[:, c]], axis=1)
 
     corner_left = shifted(corners(1), 0, 1)
     corner_right = shifted(corners(0), 0, -1)
 
     key_rows, value_rows = key_tiles.reshape(4 * PATCH, D), value_tiles.reshape(4 * PATCH, D)
-    query_pairs, stats, attended = call(
-        own_totals_kernel, [PAIR_SHAPE, STATS, TURNED], 6 * 10**9,
-        listed, query_tiles.reshape((4,) + TILE), key_rows, value_rows,
-    )
-    grad_pairs, grad_turned, stats, attended = call(
-        edge_totals_kernel, [PAIR_SHAPE, ((PAIRS, 4, 128, PATCH), BF16), STATS, TURNED], 6 * 10**9,
-        listed, gain, out_grad, query_pairs, stats, attended, from_up, from_down, from_left, from_right,
+    listed, query_pairs, stats, attended = call(
+        functools.partial(own_totals_kernel, chord_total),
+        [((72,), jnp.int32), PAIR_SHAPE, STATS, TURNED], 6 * 10**9,
+        partners, counts, query_tiles.reshape((4,) + TILE), key_rows, value_rows,
+    )
+    upper, lower, stats = lax.optimization_barrier((out_grad[0], out_grad[1], stats))
+    grad_up, grad_down = shifted(lower, 1, 0), shifted(upper, -1, 0)
+    stats, attended = call(
+        edge_totals_kernel, [STATS, TURNED], 6 * 10**9,
+        listed, query_pairs, stats, attended, from_up, from_down, from_left, from_right,
+    )
+    grad_pairs, finals, left_back, right_back, dq = call(
+        functools.partial(corner_kernel, span_total, chord_total),
+        [PAIR_SHAPE, STATS, TWO, TWO, TURNED], 3 * 10**9,
+        listed, partners, mix_gain, out_grad, grad_up, grad_down, from_left, from_right,
+        stats, attended, query_pairs, corner_left, corner_right,
     )
     pairs = query_pairs, grad_pairs
-    finals, left_back, right_back, dq = call(
-        corner_kernel, [STATS, TWO, TWO, TURNED], 2 * 10**9,
-        listed, stats, attended, *pairs, grad_turned, corner_left, corner_right,
-    )
     add_right = shifted(left_back, 0, -1)
     add_left = shifted(right_back, 0, 1)
     wide = ((2, 2) + TILE, F32)
@@ -380,10 +415,11 @@
         listed, finals, *pairs, dq, from_up, from_down, from_left, from_right,
     )
     up_back, down_back = call(
-        add_kernel, [TWO, TWO], 10**7, listed, up_sum, down_sum, add_left, add_right
+        add_kernel, [TWO, TWO], 10**7, up_sum, down_sum, add_left, add_right
     )
     end_down = shifted(up_back, -1, 0)
     end_up = shifted(down_back, 1, 0)
+    left_back, right_back, *_ = lax.optimization_barrier((left_back, right_back, up_back, down_back))
     side_right = shifted(left_back, 0, -1)
     side_left = shifted(right_back, 0, 1)
     own_key, own_value, query_grad = call(
@@ -393,7 +429,7 @@
 
     key_grad, value_grad = call(
         last_kernel, [TWO, TWO], 10**7,
-        listed, own_key, own_value, side_left, side_right, end_up, end_down,
+        own_key, own_value, side_left, side_right, end_up, end_down,
     )
     return (query_grad.reshape((2, 2) + TILE), key_grad, value_grad)
 

time: 73.6 us -> 68.2 us (0.927)
  other arithmetic: 4.34 us -> 0.38 us
  Pallas kernels: 35.1 us -> 31.7 us
  waiting for transfers between devices: 4.8 us -> 7.67 us
  local copies, waits for them, and re-layouts: 4.01 us -> 2.19 us
  starting transfers between devices: 24.3 us -> 25.2 us
    another operation x7 -> x6, other arithmetic: 4.14 us -> 0.38 us  [the longest x4 0.28 us: packed(): return jnp.stack([x[index] for x in tiles])]
    pallas_call x7, Pallas kernels: 35.1 us -> 31.7 us  [call(): pl.pallas_call(kernel, out_shape=[jax.ShapeDtypeStruct(shape, kind) for s...]
    ppermute x12 -> x14, waiting for transfers between devices: 4.8 us -> 7.67 us  [shifted(): return lax.ppermute(x, ('span', 'chord'), pairs)]
    unnamed x14, local copies, waits for them, and re-layouts: 2.38 us -> 0.71 us
    ppermute x12 -> x14, starting transfers between devices: 24.3 us -> 25.2 us  [shifted(): return lax.ppermute(x, ('span', 'chord'), pairs)]
  transfers between devices with their start and end apart: 12 -> 14, of which waited for: 3 -> 5; matrix products, arithmetic and copies ran while one was open for 5% -> 1% of each run, Pallas kernels for 40% -> 39%
where the time goes in v1:
time: 68.2 us; the launch traced here: 68 us
  Pallas kernels  31.7 us (46%)
  starting transfers between devices  25.2 us (37%)
  waiting for transfers between devices  7.67 us (11%)
  local copies, waits for them, and re-layouts  2.19 us (3%)
  between operations  0.84 us (1%)
    pallas_call x7, Pallas kernels, call(): pl.pallas_call(kernel, out_shape=[jax.ShapeDtypeStruct(shape, kind) for s...  31.7 us
    ppermute x14, starting transfers between devices, shifted(): return lax.ppermute(x, ('span', 'chord'), pairs)  25.2 us
    ppermute x14, waiting for transfers between devices, shifted(): return lax.ppermute(x, ('span', 'chord'), pairs)  7.67 us
  transfers between devices with their start and end apart: 14, of which 5 were waited for; matrix products, arithmetic and copies ran while one was open for 1% of the time, Pallas kernels for 39%

profile of v1, /device:TPU:0, one launch (start us, length us, event | category | flops | bytes accessed | tf_op | source)
XLA Modules:
  0.0 68.0 jit_solution(3680191500287254041)
XLA Ops:
  0.6 1.3 %fusion.2 = (bf16[1,2,128,512]{3,2,1,0:T(8,128)(2,1)S(1)}, bf16[1,2,128,512]{3,2,1,0:T(8,128)(2,1)S(1)}, bf16[1,2,128,512]{3,2,1,0:T(8,128)(2,1)S(1)}, bf16[1,2,128,512]{3,2,1,0:T(8,128)(2,1)S(1)}) fusion(bf16[2,2,128,512]{3,2,1,0:T(8,128)(2,1)} %param.8, bf16[2,2,128,512]{3,2,1,0:T(8,128)(2,1)} %param.9), kind=kLoop, calls=%fused_computation.16 | loop fusion | bytes 2097152 | tf_op jit(solution)/shard_map/slice | solution.py:378
  1.9 0.1 pad_maximum_fusion.2
  2.0 1.7 %collective-permute-start.4 = (bf16[2,2,128,512]{3,2,1,0:T(8,128)(2,1)S(1)}, bf16[2,2,128,512]{3,2,1,0:T(8,128)(2,1)S(1)}, u32[]{:S(2)}, u32[]{:S(2)}) collective-permute-start(bf16[2,2,128,512]{3,2,1,0:T(8,128)(2,1)S(1)} %pad_maximum_fusion.2), channel_id=1, source_target_pairs={{0,8},{1,9},{2,10},{3,11},{4,12},{5,13},{6,14},{7,15},{8,16},{9,17... | collective-permute-start | bytes 1572872 | tf_op jit(solution)/shard_map/ppermute | solution.py:29
  3.7 0.1 pad_maximum_fusion.3
  3.8 5.0 %collective-permute-start.5 = (bf16[2,2,128,512]{3,2,1,0:T(8,128)(2,1)S(1)}, bf16[2,2,128,512]{3,2,1,0:T(8,128)(2,1)S(1)}, u32[]{:S(2)}, u32[]{:S(2)}) collective-permute-start(bf16[2,2,128,512]{3,2,1,0:T(8,128)(2,1)S(1)} %pad_maximum_fusion.3), channel_id=1, source_target_pairs={{0,120},{1,121},{2,122},{3,123},{4,124},{5,125},{6,126},{7,127},{8... | collective-permute-start | bytes 1572872 | tf_op jit(solution)/shard_map/ppermute | solution.py:29
  8.8 0.1 slice_bitcast_fusion.1
  8.9 0.1 pad_maximum_fusion
  9.0 0.0 collective-permute-start.2
  9.0 0.1 pad_maximum_fusion.1
  9.1 2.9 %collective-permute-start.3 = (bf16[3,2,128,512]{3,2,1,0:T(8,128)(2,1)S(1)}, bf16[3,2,128,512]{3,2,1,0:T(8,128)(2,1)S(1)}, u32[]{:S(2)}, u32[]{:S(2)}) collective-permute-start(bf16[3,2,128,512]{3,2,1,0:T(8,128)(2,1)S(1)} %pad_maximum_fusion.1), channel_id=1, source_target_pairs={{0,7},{1,0},{2,1},{3,2},{4,3},{5,4},{6,5},{7,6},{8,15},{9,8},{10,9... | collective-permute-start | bytes 2359304 | tf_op jit(solution)/shard_map/ppermute | solution.py:29
  12.1 0.7 copy-done.5
  12.8 6.7 %shard_map.94 = (s32[72]{0:T(128)S(1)}, bf16[4,4,256,128]{3,2,1,0:T(8,128)(2,1)S(1)}, f32[4,8,256]{2,1,0:T(8,128)S(1)}, f32[4,4,128,128]{3,2,1,0:T(8,128)S(1)}) custom-call(s32[2,2,8]{2,1,0:T(2,128)S(1)} %copy-done.5, s32[2,2]{1,0:T(2,128)S(1)} %copy-done.6, bf16[4,128,512]{2,1,0:T(8,128)(2,1)S(1)} %bitcast.36, bf16[512,512]{1,0:T(8,128)(2,1)S(1)} %bitcast.32, ...), custom_call_target="tpu_custom_call" | custom-call | flops 6000000000 | bytes 1000000 | tf_op jit(solution)/shard_map/pallas_call | solution.py:357
  19.5 0.1 collective-permute-start
  19.6 0.9 %collective-permute-done.4.from_up = bf16[2,2,128,512]{3,2,1,0:T(8,128)(2,1)S(1)} collective-permute-done((bf16[2,2,128,512]{3,2,1,0:T(8,128)(2,1)S(1)}, bf16[2,2,128,512]{3,2,1,0:T(8,128)(2,1)S(1)}, u32[]{:S(2)}, u32[]{:S(2)}) %collective-permute-start.4) | collective-permute-done | bytes 524320 | tf_op jit(solution)/shard_map/ppermute | solution.py:29
  20.5 4.4 %collective-permute-start.1 = (bf16[2,128,512]{2,1,0:T(8,128)(2,1)S(1)}, bf16[2,128,512]{2,1,0:T(8,128)(2,1)S(1)}, u32[]{:S(2)}, u32[]{:S(2)}) collective-permute-start(bf16[2,128,512]{2,1,0:T(8,128)(2,1)S(1)} %get-tuple-element.34), channel_id=1, source_target_pairs={{0,120},{1,121},{2,122},{3,123},{4,124},{5,125},{6,126},{7,127},{8... | collective-permute-start | bytes 786440 | tf_op jit(solution)/shard_map/ppermute | solution.py:29
  25.0 0.1 pad_maximum_fusion.4
  25.1 0.1 pad_maximum_fusion.5
  25.2 2.9 %collective-permute-start.7 = (bf16[2,2,128,512]{3,2,1,0:T(8,128)(2,1)S(1)}, bf16[2,2,128,512]{3,2,1,0:T(8,128)(2,1)S(1)}, u32[]{:S(2)}, u32[]{:S(2)}) collective-permute-start(bf16[2,2,128,512]{3,2,1,0:T(8,128)(2,1)S(1)} %pad_maximum_fusion.5), channel_id=1, source_target_pairs={{0,7},{1,0},{2,1},{3,2},{4,3},{5,4},{6,5},{7,6},{8,15},{9,8},{10,9... | collective-permute-start | bytes 1572872 | tf_op jit(solution)/shard_map/ppermute | solution.py:29
  28.1 6.5 %shard_map.95 = (f32[4,8,256]{2,1,0:T(8,128)S(1)}, f32[4,4,128,128]{3,2,1,0:T(8,128)S(1)}) custom-call(s32[72]{0:T(128)S(1)} %get-tuple-element.31.listed, bf16[4,4,256,128]{3,2,1,0:T(8,128)(2,1)S(1)} %get-tuple-element.35.query_pairs, f32[4,8,256]{2,1,0:T(8,128)S(1)} %get-tuple-element.36.stats_in, f32[4,4,128,128]{3,2,1,0:T(8,128)S(1)} %get-tuple-element.37.attended_in, ...), custom_call_target="tpu_custom_call" | custom-call | flops 6000000000 | bytes 1000000 | tf_op jit(solution)/shard_map/pallas_call | solution.py:357
  34.6 0.3 collective-permute-done.6.corner_left
  34.9 4.1 %shard_map.96 = (bf16[4,4,256,128]{3,2,1,0:T(8,128)(2,1)S(1)}, f32[4,8,256]{2,1,0:T(8,128)S(1)}, bf16[2,2,128,512]{3,2,1,0:T(8,128)(2,1)S(1)}, bf16[2,2,128,512]...) custom-call(s32[72]{0:T(128)S(1)} %get-tuple-element.31.listed, s32[2,2,8]{2,1,0:T(2,128)S(1)} %copy-done.5, ...), custom_call_target="tpu_custom_call" | custom-call | flops 3000000000 | bytes 1000000 | tf_op jit(solution)/shard_map/pallas_call | solution.py:357
  39.0 3.0 %collective-permute-start.9 = (bf16[2,2,128,512]{3,2,1,0:T(8,128)(2,1)S(1)}, bf16[2,2,128,512]{3,2,1,0:T(8,128)(2,1)S(1)}, u32[]{:S(2)}, u32[]{:S(2)}) collective-permute-start(bf16[2,2,128,512]{3,2,1,0:T(8,128)(2,1)S(1)} %get-tuple-element.52), channel_id=1, source_target_pairs={{0,7},{1,0},{2,1},{3,2},{4,3},{5,4},{6,5},{7,6},{8,15},{9,8},{10,9... | collective-permute-start | bytes 1572872 | tf_op jit(solution)/shard_map/ppermute | solution.py:29
  42.1 6.1 %shard_map.97 = (f32[2,2,128,512]{3,2,1,0:T(8,128)S(1)}, f32[2,2,128,512]{3,2,1,0:T(8,128)S(1)}, bf16[2,2,128,512]{3,2,1,0:T(8,128)(2,1)S(1)}, bf16[2,2,128,512]...) custom-call(s32[72]{0:T(128)S(1)} %get-tuple-element.31.listed, f32[4,8,256]{2,1,0:T(8,128)S(1)} %get-tuple-element.40.finals, ...), custom_call_target="tpu_custom_call" | custom-call | flops 8000000000 | bytes 1000000 | tf_op jit(solution)/shard_map/pallas_call | solution.py:357
  48.2 0.7 %collective-permute-done.8.add_left = bf16[2,2,128,512]{3,2,1,0:T(8,128)(2,1)S(1)} collective-permute-done((bf16[2,2,128,512]{3,2,1,0:T(8,128)(2,1)S(1)}, bf16[2,2,128,512]{3,2,1,0:T(8,128)(2,1)S(1)}, u32[]{:S(2)}, u32[]{:S(2)}) %collective-permute-start.8) | collective-permute-done | bytes 524320 | tf_op jit(solution)/shard_map/ppermute | solution.py:29
  48.9 0.2 shard_map.99
  49.1 0.9 %collective-permute-start.13 = (bf16[2,2,128,512]{3,2,1,0:T(8,128)(2,1)S(1)}, bf16[2,2,128,512]{3,2,1,0:T(8,128)(2,1)S(1)}, u32[]{:S(2)}, u32[]{:S(2)}) collective-permute-start(bf16[2,2,128,512]{3,2,1,0:T(8,128)(2,1)S(1)} %get-tuple-element.53), channel_id=1, source_target_pairs={{0,120},{1,121},{2,122},{3,123},{4,124},{5,125},{6,126},{7,127},{8... | collective-permute-start | bytes 1572872 | tf_op jit(solution)/shard_map/ppermute | solution.py:29
  49.9 1.2 %collective-permute-start.12 = (bf16[2,2,128,512]{3,2,1,0:T(8,128)(2,1)S(1)}, bf16[2,2,128,512]{3,2,1,0:T(8,128)(2,1)S(1)}, u32[]{:S(2)}, u32[]{:S(2)}) collective-permute-start(bf16[2,2,128,512]{3,2,1,0:T(8,128)(2,1)S(1)} %get-tuple-element.54), channel_id=1, source_target_pairs={{0,8},{1,9},{2,10},{3,11},{4,12},{5,13},{6,14},{7,15},{8,16},{9,17... | collective-permute-start | bytes 1572872 | tf_op jit(solution)/shard_map/ppermute | solution.py:29
  51.2 3.0 %collective-permute-start.11 = (bf16[2,2,128,512]{3,2,1,0:T(8,128)(2,1)S(1)}, bf16[2,2,128,512]{3,2,1,0:T(8,128)(2,1)S(1)}, u32[]{:S(2)}, u32[]{:S(2)}) collective-permute-start(bf16[2,2,128,512]{3,2,1,0:T(8,128)(2,1)S(1)} %get-tuple-element.56), channel_id=1, source_target_pairs={{0,7},{1,0},{2,1},{3,2},{4,3},{5,4},{6,5},{7,6},{8,15},{9,8},{10,9... | collective-permute-start | bytes 1572872 | tf_op jit(solution)/shard_map/ppermute | solution.py:29
  54.1 7.0 %shard_map.98 = (f32[512,512]{1,0:T(8,128)S(1)}, f32[512,512]{1,0:T(8,128)S(1)}, bf16[4,128,512]{2,1,0:T(8,128)(2,1)}) custom-call(s32[72]{0:T(128)S(1)} %get-tuple-element.31.listed, f32[4,8,256]{2,1,0:T(8,128)S(1)} %get-tuple-element.40.finals, bf16[4,4,256,128]{3,2,1,0:T(8,128)(2,1)S(1)} %get-tuple-element.35.query_pairs, ...), custom_call_target="tpu_custom_call" | custom-call | flops 10000000000 | bytes 1000000 | tf_op jit(solution)/shard_map/pallas_call | solution.py:357
  61.1 0.5 collective-permute-done.13.down
  61.6 5.3 %collective-permute-done.12.up = bf16[2,2,128,512]{3,2,1,0:T(8,128)(2,1)S(1)} collective-permute-done((bf16[2,2,128,512]{3,2,1,0:T(8,128)(2,1)S(1)}, bf16[2,2,128,512]{3,2,1,0:T(8,128)(2,1)S(1)}, u32[]{:S(2)}, u32[]{:S(2)}) %collective-permute-start.12) | collective-permute-done | bytes 524320 | tf_op jit(solution)/shard_map/ppermute | solution.py:29
  66.8 1.2 %shard_map.100 = (bf16[2,2,128,512]{3,2,1,0:T(8,128)(2,1)}, bf16[2,2,128,512]{3,2,1,0:T(8,128)(2,1)}) custom-call(f32[512,512]{1,0:T(8,128)S(1)} %get-tuple-element.45.own_key, f32[512,512]{1,0:T(8,128)S(1)} %get-tuple-element.46.own_value, bf16[2,2,128,512]{3,2,1,0:T(8,128)(2,1)S(1)} %collective-permute-done.10.left, ...), custom_call_target="tpu_custom_call" | custom-call | flops 10000000 | bytes 1000000 | tf_op jit(solution)/shard_map/pallas_call | solution.py:357
  (29 shorter events, 0.2 us)
Async XLA Ops:
  2.0 18.6 %collective-permute-start.4 = (bf16[2,2,128,512]{3,2,1,0:T(8,128)(2,1)S(1)}, bf16[2,2,128,512]{3,2,1,0:T(8,128)(2,1)S(1)}, u32[]{:S(2)}, u32[]{:S(2)}) collective-permute-start(bf16[2,2,128,512]{3,2,1,0:T(8,128)(2,1)S(1)} %pad_maximum_fusion.2), channel_id=1, source_target_pairs={{0,8},{1,9},{2,10},{3,11},{4,12},{5,13},{6,14},{7,15},{8,16},{9,17... | collective-permute-start | bytes 1572872 | tf_op jit(solution)/shard_map/ppermute | solution.py:29
  3.7 5.1 %copy-start.1 = (bf16[2,2,128,512]{3,2,1,0:T(8,128)(2,1)S(1)}, bf16[2,2,128,512]{3,2,1,0:T(8,128)(2,1)}, u32[]{:S(2)}) copy-start(bf16[2,2,128,512]{3,2,1,0:T(8,128)(2,1)} %param.8) | copy-start | bytes 1572868
  3.7 5.1 %copy-start.2 = (bf16[2,2,128,512]{3,2,1,0:T(8,128)(2,1)S(1)}, bf16[2,2,128,512]{3,2,1,0:T(8,128)(2,1)}, u32[]{:S(2)}) copy-start(bf16[2,2,128,512]{3,2,1,0:T(8,128)(2,1)} %param.9) | copy-start | bytes 1572868
  3.7 5.1 %copy-start = (bf16[2,2,128,512]{3,2,1,0:T(8,128)(2,1)S(1)}, bf16[2,2,128,512]{3,2,1,0:T(8,128)(2,1)}, u32[]{:S(2)}) copy-start(bf16[2,2,128,512]{3,2,1,0:T(8,128)(2,1)} %grad.1) | copy-start | bytes 1572868
  3.8 21.2 %collective-permute-start.5 = (bf16[2,2,128,512]{3,2,1,0:T(8,128)(2,1)S(1)}, bf16[2,2,128,512]{3,2,1,0:T(8,128)(2,1)S(1)}, u32[]{:S(2)}, u32[]{:S(2)}) collective-permute-start(bf16[2,2,128,512]{3,2,1,0:T(8,128)(2,1)S(1)} %pad_maximum_fusion.3), channel_id=1, source_target_pairs={{0,120},{1,121},{2,122},{3,123},{4,124},{5,125},{6,126},{7,127},{8... | collective-permute-start | bytes 1572872 | tf_op jit(solution)/shard_map/ppermute | solution.py:29
  9.0 16.1 %collective-permute-start.2 = (bf16[3,2,128,512]{3,2,1,0:T(8,128)(2,1)S(1)}, bf16[3,2,128,512]{3,2,1,0:T(8,128)(2,1)S(1)}, u32[]{:S(2)}, u32[]{:S(2)}) collective-permute-start(bf16[3,2,128,512]{3,2,1,0:T(8,128)(2,1)S(1)} %pad_maximum_fusion), channel_id=1, source_target_pairs={{0,1},{1,2},{2,3},{3,4},{4,5},{5,6},{6,7},{7,0},{8,9},{9,10},{10,1... | collective-permute-start | bytes 2359304 | tf_op jit(solution)/shard_map/ppermute | solution.py:29
  9.0 3.1 %copy-start.3 = (bf16[2,2,128,512]{3,2,1,0:T(8,128)(2,1)S(1)}, bf16[2,2,128,512]{3,2,1,0:T(8,128)(2,1)}, u32[]{:S(2)}) copy-start(bf16[2,2,128,512]{3,2,1,0:T(8,128)(2,1)} %param.7) | copy-start | bytes 1572868
  9.1 19.0 %collective-permute-start.3 = (bf16[3,2,128,512]{3,2,1,0:T(8,128)(2,1)S(1)}, bf16[3,2,128,512]{3,2,1,0:T(8,128)(2,1)S(1)}, u32[]{:S(2)}, u32[]{:S(2)}) collective-permute-start(bf16[3,2,128,512]{3,2,1,0:T(8,128)(2,1)S(1)} %pad_maximum_fusion.1), channel_id=1, source_target_pairs={{0,7},{1,0},{2,1},{3,2},{4,3},{5,4},{6,5},{7,6},{8,15},{9,8},{10,9... | collective-permute-start | bytes 2359304 | tf_op jit(solution)/shard_map/ppermute | solution.py:29
  12.1 0.7 %copy-start.5 = (s32[2,2,8]{2,1,0:T(2,128)S(1)}, s32[2,2,8]{2,1,0:T(2,128)}, u32[]{:S(2)}) copy-start(s32[2,2,8]{2,1,0:T(2,128)} %partners.3) | copy-start | bytes 388
  12.1 0.7 %copy-start.6 = (s32[2,2]{1,0:T(2,128)S(1)}, s32[2,2]{1,0:T(2,128)}, u32[]{:S(2)}) copy-start(s32[2,2]{1,0:T(2,128)} %counts.1) | copy-start | bytes 52
  19.5 15.1 %collective-permute-start = (bf16[2,128,512]{2,1,0:T(8,128)(2,1)S(1)}, bf16[2,128,512]{2,1,0:T(8,128)(2,1)S(1)}, u32[]{:S(2)}, u32[]{:S(2)}) collective-permute-start(bf16[2,128,512]{2,1,0:T(8,128)(2,1)S(1)} %get-tuple-element.33), channel_id=1, source_target_pairs={{0,8},{1,9},{2,10},{3,11},{4,12},{5,13},{6,14},{7,15},{8,16},{9,17... | collective-permute-start | bytes 786440 | tf_op jit(solution)/shard_map/ppermute | solution.py:29
  20.5 14.1 %collective-permute-start.1 = (bf16[2,128,512]{2,1,0:T(8,128)(2,1)S(1)}, bf16[2,128,512]{2,1,0:T(8,128)(2,1)S(1)}, u32[]{:S(2)}, u32[]{:S(2)}) collective-permute-start(bf16[2,128,512]{2,1,0:T(8,128)(2,1)S(1)} %get-tuple-element.34), channel_id=1, source_target_pairs={{0,120},{1,121},{2,122},{3,123},{4,124},{5,125},{6,126},{7,127},{8... | collective-permute-start | bytes 786440 | tf_op jit(solution)/shard_map/ppermute | solution.py:29
  25.1 9.8 %collective-permute-start.6 = (bf16[2,2,128,512]{3,2,1,0:T(8,128)(2,1)S(1)}, bf16[2,2,128,512]{3,2,1,0:T(8,128)(2,1)S(1)}, u32[]{:S(2)}, u32[]{:S(2)}) collective-permute-start(bf16[2,2,128,512]{3,2,1,0:T(8,128)(2,1)S(1)} %pad_maximum_fusion.4), channel_id=1, source_target_pairs={{0,1},{1,2},{2,3},{3,4},{4,5},{5,6},{6,7},{7,0},{8,9},{9,10},{10,1... | collective-permute-start | bytes 1572872 | tf_op jit(solution)/shard_map/ppermute | solution.py:29
  25.2 9.7 %collective-permute-start.7 = (bf16[2,2,128,512]{3,2,1,0:T(8,128)(2,1)S(1)}, bf16[2,2,128,512]{3,2,1,0:T(8,128)(2,1)S(1)}, u32[]{:S(2)}, u32[]{:S(2)}) collective-permute-start(bf16[2,2,128,512]{3,2,1,0:T(8,128)(2,1)S(1)} %pad_maximum_fusion.5), channel_id=1, source_target_pairs={{0,7},{1,0},{2,1},{3,2},{4,3},{5,4},{6,5},{7,6},{8,15},{9,8},{10,9... | collective-permute-start | bytes 1572872 | tf_op jit(solution)/shard_map/ppermute | solution.py:29
  28.1 6.8 %copy-start.4 = (f32[4,512]{1,0:T(4,128)S(1)}, f32[4,512]{1,0:T(4,128)}, u32[]{:S(2)}) copy-start(f32[4,512]{1,0:T(4,128)} %gain.1) | copy-start | bytes 24580
  39.0 9.9 %collective-permute-start.8 = (bf16[2,2,128,512]{3,2,1,0:T(8,128)(2,1)S(1)}, bf16[2,2,128,512]{3,2,1,0:T(8,128)(2,1)S(1)}, u32[]{:S(2)}, u32[]{:S(2)}) collective-permute-start(bf16[2,2,128,512]{3,2,1,0:T(8,128)(2,1)S(1)} %get-tuple-element.51), channel_id=1, source_target_pairs={{0,1},{1,2},{2,3},{3,4},{4,5},{5,6},{6,7},{7,0},{8,9},{9,10},{10,1... | collective-permute-start | bytes 1572872 | tf_op jit(solution)/shard_map/ppermute | solution.py:29
  39.0 9.9 %collective-permute-start.9 = (bf16[2,2,128,512]{3,2,1,0:T(8,128)(2,1)S(1)}, bf16[2,2,128,512]{3,2,1,0:T(8,128)(2,1)S(1)}, u32[]{:S(2)}, u32[]{:S(2)}) collective-permute-start(bf16[2,2,128,512]{3,2,1,0:T(8,128)(2,1)S(1)} %get-tuple-element.52), channel_id=1, source_target_pairs={{0,7},{1,0},{2,1},{3,2},{4,3},{5,4},{6,5},{7,6},{8,15},{9,8},{10,9... | collective-permute-start | bytes 1572872 | tf_op jit(solution)/shard_map/ppermute | solution.py:29
  49.1 12.5 %collective-permute-start.13 = (bf16[2,2,128,512]{3,2,1,0:T(8,128)(2,1)S(1)}, bf16[2,2,128,512]{3,2,1,0:T(8,128)(2,1)S(1)}, u32[]{:S(2)}, u32[]{:S(2)}) collective-permute-start(bf16[2,2,128,512]{3,2,1,0:T(8,128)(2,1)S(1)} %get-tuple-element.53), channel_id=1, source_target_pairs={{0,120},{1,121},{2,122},{3,123},{4,124},{5,125},{6,126},{7,127},{8... | collective-permute-start | bytes 1572872 | tf_op jit(solution)/shard_map/ppermute | solution.py:29
  49.9 16.9 %collective-permute-start.12 = (bf16[2,2,128,512]{3,2,1,0:T(8,128)(2,1)S(1)}, bf16[2,2,128,512]{3,2,1,0:T(8,128)(2,1)S(1)}, u32[]{:S(2)}, u32[]{:S(2)}) collective-permute-start(bf16[2,2,128,512]{3,2,1,0:T(8,128)(2,1)S(1)} %get-tuple-element.54), channel_id=1, source_target_pairs={{0,8},{1,9},{2,10},{3,11},{4,12},{5,13},{6,14},{7,15},{8,16},{9,17... | collective-permute-start | bytes 1572872 | tf_op jit(solution)/shard_map/ppermute | solution.py:29
  51.2 9.9 %collective-permute-start.10 = (bf16[2,2,128,512]{3,2,1,0:T(8,128)(2,1)S(1)}, bf16[2,2,128,512]{3,2,1,0:T(8,128)(2,1)S(1)}, u32[]{:S(2)}, u32[]{:S(2)}) collective-permute-start(bf16[2,2,128,512]{3,2,1,0:T(8,128)(2,1)S(1)} %get-tuple-element.55), channel_id=1, source_target_pairs={{0,1},{1,2},{2,3},{3,4},{4,5},{5,6},{6,7},{7,0},{8,9},{9,10},{10,1... | collective-permute-start | bytes 1572872 | tf_op jit(solution)/shard_map/ppermute | solution.py:29
  51.2 9.9 %collective-permute-start.11 = (bf16[2,2,128,512]{3,2,1,0:T(8,128)(2,1)S(1)}, bf16[2,2,128,512]{3,2,1,0:T(8,128)(2,1)S(1)}, u32[]{:S(2)}, u32[]{:S(2)}) collective-permute-start(bf16[2,2,128,512]{3,2,1,0:T(8,128)(2,1)S(1)} %get-tuple-element.56), channel_id=1, source_target_pairs={{0,7},{1,0},{2,1},{3,2},{4,3},{5,4},{6,5},{7,6},{8,15},{9,8},{10,9... | collective-permute-start | bytes 1572872 | tf_op jit(solution)/shard_map/ppermute | solution.py:29

commit v2 on v1

--- a/solution.py
+++ b/solution.py
@@ -110,7 +110,8 @@
 
     def step(h, carry):
         value_turned = value[:, cols(h)].T
-        for p in range(4):
+
+        def groups_of(p):
             pair = stacked_pair(query[p, :, cols(h)] * jnp.bfloat16(SCALING))
             query_pairs[h, p] = pair
             groups = []
@@ -123,6 +124,12 @@
                         value_turned[:, rows],
                     )
                 )
+            return groups
+
+        ahead = groups_of(0)
+        for p in range(4):
+            groups = ahead
+            ahead = groups_of(p + 1) if p < 3 else None
             top, total, turned = merged(groups, None, None)
             stats_out[h, p : p + 1, :] = top
             stats_out[h, 4 + p : 5 + p, :] = total
@@ -144,17 +151,21 @@
             return source[1, :, :, cols(h)].reshape(256, 128).T
 
         values = {id(source): turned(source) for source, _ in ends + sides}
+
+        def groups_of(p):
+            return [
+                (
+                    product(source[0, :, :, cols(h)].reshape(256, 128), query_pairs[h, p]),
+                    [penalty(listed, p, w) for w in places],
+                    values[id(source)],
+                )
+                for source, places in (ends[p // 2], sides[p % 2])
+            ]
+
+        ahead = groups_of(0)
         for p in range(4):
-            s, c = p // 2, p % 2
-            groups = []
-            for source, places in (ends[s], sides[c]):
-                groups.append(
-                    (
-                        product(source[0, :, :, cols(h)].reshape(256, 128), query_pairs[h, p]),
-                        [penalty(listed, p, w) for w in places],
-                        values[id(source)],
-                    )
-                )
+            groups = ahead
+            ahead = groups_of(p + 1) if p < 3 else None
             stats = stats_in[h, p : p + 1, :], stats_in[h, 4 + p : 5 + p, :]
             top, total, attended = merged(groups, stats, attended_in[h, p])
             stats_out[h, p : p + 1, :] = top
@@ -385,8 +396,9 @@
     def corners(c):
         return jnp.stack([from_up[:, c], from_down[:, c]], axis=1)
 
-    corner_left = shifted(corners(1), 0, 1)
-    corner_right = shifted(corners(0), 0, -1)
+    for_left, for_right = corners(0), corners(1)
+    corner_left = shifted(for_right, 0, 1)
+    corner_right = shifted(for_left, 0, -1)
 
     key_rows, value_rows = key_tiles.reshape(4 * PATCH, D), value_tiles.reshape(4 * PATCH, D)
     listed, query_pairs, stats, attended = call(
@@ -394,7 +406,7 @@
         [((72,), jnp.int32), PAIR_SHAPE, STATS, TURNED], 6 * 10**9,
         partners, counts, query_tiles.reshape((4,) + TILE), key_rows, value_rows,
     )
-    upper, lower, stats = lax.optimization_barrier((out_grad[0], out_grad[1], stats))
+    upper, lower, *_ = lax.optimization_barrier((out_grad[0], out_grad[1], for_left, for_right))
     grad_up, grad_down = shifted(lower, 1, 0), shifted(upper, -1, 0)
     stats, attended = call(
         edge_totals_kernel, [STATS, TURNED], 6 * 10**9,

time: 68.2 us -> 77 us (1.13)
  waiting for transfers between devices: 7.67 us -> 17 us
  Pallas kernels: 31.7 us -> 27.9 us
  starting transfers between devices: 25.2 us -> 27.2 us
  local copies, waits for them, and re-layouts: 2.19 us -> 3.33 us
    ppermute x14, waiting for transfers between devices: 7.67 us -> 17 us  [shifted(): return lax.ppermute(x, ('span', 'chord'), pairs)]
    pallas_call x7, Pallas kernels: 31.7 us -> 27.9 us  [call(): pl.pallas_call(kernel, out_shape=[jax.ShapeDtypeStruct(shape, kind) for s...]
    ppermute x14, starting transfers between devices: 25.2 us -> 27.2 us  [shifted(): return lax.ppermute(x, ('span', 'chord'), pairs)]
    unnamed x14, local copies, waits for them, and re-layouts: 0.71 us -> 1.85 us
  transfers between devices with their start and end apart: 14 -> 14, of which waited for: 5 -> 6; matrix products, arithmetic and copies ran while one was open for 1% -> 1% of each run, Pallas kernels for 39% -> 29%
where the time goes in v2:
time: 77 us; the launch traced here: 76.5 us
  Pallas kernels  27.9 us (36%)
  starting transfers between devices  27.2 us (35%)
  waiting for transfers between devices  17 us (22%)
  local copies, waits for them, and re-layouts  3.33 us (4%)
  between operations  0.82 us (1%)
    pallas_call x7, Pallas kernels, call(): pl.pallas_call(kernel, out_shape=[jax.ShapeDtypeStruct(shape, kind) for s...  27.9 us
    ppermute x14, starting transfers between devices, shifted(): return lax.ppermute(x, ('span', 'chord'), pairs)  27.2 us
    ppermute x14, waiting for transfers between devices, shifted(): return lax.ppermute(x, ('span', 'chord'), pairs)  17 us
    unnamed x14, local copies, waits for them, and re-layouts  1.85 us
  transfers between devices with their start and end apart: 14, of which 6 were waited for; matrix products, arithmetic and copies ran while one was open for 1% of the time, Pallas kernels for 29%

profile of v2, /device:TPU:0, one launch (start us, length us, event | category | flops | bytes accessed | tf_op | source)
XLA Modules:
  0.0 76.5 jit_solution(6740268072666340979)
XLA Ops:
  0.6 1.3 %fusion.2 = (bf16[1,2,128,512]{3,2,1,0:T(8,128)(2,1)S(1)}, bf16[1,2,128,512]{3,2,1,0:T(8,128)(2,1)S(1)}, bf16[1,2,128,512]{3,2,1,0:T(8,128)(2,1)S(1)}, bf16[1,2,128,512]{3,2,1,0:T(8,128)(2,1)S(1)}) fusion(bf16[2,2,128,512]{3,2,1,0:T(8,128)(2,1)} %param.8, bf16[2,2,128,512]{3,2,1,0:T(8,128)(2,1)} %param.9), kind=kLoop, calls=%fused_computation.16 | loop fusion | bytes 2097152 | tf_op jit(solution)/shard_map/slice | solution.py:389
  1.9 0.1 pad_maximum_fusion.3
  2.0 6.6 %collective-permute-start.1 = (bf16[2,2,128,512]{3,2,1,0:T(8,128)(2,1)S(1)}, bf16[2,2,128,512]{3,2,1,0:T(8,128)(2,1)S(1)}, u32[]{:S(2)}, u32[]{:S(2)}) collective-permute-start(bf16[2,2,128,512]{3,2,1,0:T(8,128)(2,1)S(1)} %pad_maximum_fusion.3), channel_id=1, source_target_pairs={{0,120},{1,121},{2,122},{3,123},{4,124},{5,125},{6,126},{7,127},{8... | collective-permute-start | bytes 1572872 | tf_op jit(solution)/shard_map/ppermute | solution.py:29
  8.7 0.1 collective-permute-start
  8.7 0.9 %copy-done.1 = bf16[2,2,128,512]{3,2,1,0:T(8,128)(2,1)S(1)} copy-done((bf16[2,2,128,512]{3,2,1,0:T(8,128)(2,1)S(1)}, bf16[2,2,128,512]{3,2,1,0:T(8,128)(2,1)}, u32[]{:S(2)}) %copy-start.1) | copy-done | bytes 524312
  9.6 0.2 copy-done.2
  9.8 0.1 slice_bitcast_fusion.1
  9.9 0.1 copy-done
  10.0 0.1 pad_maximum_fusion
  10.1 0.1 pad_maximum_fusion.1
  10.2 2.9 %collective-permute-start.5 = (bf16[3,2,128,512]{3,2,1,0:T(8,128)(2,1)S(1)}, bf16[3,2,128,512]{3,2,1,0:T(8,128)(2,1)S(1)}, u32[]{:S(2)}, u32[]{:S(2)}) collective-permute-start(bf16[3,2,128,512]{3,2,1,0:T(8,128)(2,1)S(1)} %pad_maximum_fusion.1), channel_id=1, source_target_pairs={{0,7},{1,0},{2,1},{3,2},{4,3},{5,4},{6,5},{7,6},{8,15},{9,8},{10,9... | collective-permute-start | bytes 2359304 | tf_op jit(solution)/shard_map/ppermute | solution.py:29
  13.2 0.7 copy-done.5
  13.9 4.8 %shard_map.94 = (s32[72]{0:T(128)S(1)}, bf16[4,4,256,128]{3,2,1,0:T(8,128)(2,1)S(1)}, f32[4,8,256]{2,1,0:T(8,128)S(1)}, f32[4,4,128,128]{3,2,1,0:T(8,128)S(1)}) custom-call(s32[2,2,8]{2,1,0:T(2,128)S(1)} %copy-done.5, s32[2,2]{1,0:T(2,128)S(1)} %copy-done.6, bf16[4,128,512]{2,1,0:T(8,128)(2,1)S(1)} %bitcast.36, bf16[512,512]{1,0:T(8,128)(2,1)S(1)} %bitcast.32, ...), custom_call_target="tpu_custom_call" | custom-call | flops 6000000000 | bytes 1000000 | tf_op jit(solution)/shard_map/pallas_call | solution.py:368
  18.7 1.1 %collective-permute-done.1.from_down = bf16[2,2,128,512]{3,2,1,0:T(8,128)(2,1)S(1)} collective-permute-done((bf16[2,2,128,512]{3,2,1,0:T(8,128)(2,1)S(1)}, bf16[2,2,128,512]{3,2,1,0:T(8,128)(2,1)S(1)}, u32[]{:S(2)}, u32[]{:S(2)}) %collective-permute-start.1) | collective-permute-done | bytes 524320 | tf_op jit(solution)/shard_map/ppermute | solution.py:29
  19.8 5.6 %collective-permute-done.from_up = bf16[2,2,128,512]{3,2,1,0:T(8,128)(2,1)S(1)} collective-permute-done((bf16[2,2,128,512]{3,2,1,0:T(8,128)(2,1)S(1)}, bf16[2,2,128,512]{3,2,1,0:T(8,128)(2,1)S(1)}, u32[]{:S(2)}, u32[]{:S(2)}) %collective-permute-start) | collective-permute-done | bytes 524320 | tf_op jit(solution)/shard_map/ppermute | solution.py:29
  25.5 1.0 %collective-permute-start.7 = (bf16[2,2,128,512]{3,2,1,0:T(8,128)(2,1)S(1)}, bf16[2,2,128,512]{3,2,1,0:T(8,128)(2,1)S(1)}, u32[]{:S(2)}, u32[]{:S(2)}) collective-permute-start(bf16[2,2,128,512]{3,2,1,0:T(8,128)(2,1)S(1)} %pad_maximum_fusion.4), channel_id=1, source_target_pairs={{0,7},{1,0},{2,1},{3,2},{4,3},{5,4},{6,5},{7,6},{8,15},{9,8},{10,9... | collective-permute-start | bytes 1572872 | tf_op jit(solution)/shard_map/ppermute | solution.py:29
  26.6 0.1 collective-permute-start.2
  26.7 5.3 %collective-permute-start.3 = (bf16[2,128,512]{2,1,0:T(8,128)(2,1)S(1)}, bf16[2,128,512]{2,1,0:T(8,128)(2,1)S(1)}, u32[]{:S(2)}, u32[]{:S(2)}) collective-permute-start(bf16[2,128,512]{2,1,0:T(8,128)(2,1)S(1)} %get-tuple-element.32), channel_id=1, source_target_pairs={{0,120},{1,121},{2,122},{3,123},{4,124},{5,125},{6,126},{7,127},{8... | collective-permute-start | bytes 786440 | tf_op jit(solution)/shard_map/ppermute | solution.py:29
  32.1 4.5 %shard_map.95 = (f32[4,8,256]{2,1,0:T(8,128)S(1)}, f32[4,4,128,128]{3,2,1,0:T(8,128)S(1)}) custom-call(s32[72]{0:T(128)S(1)} %get-tuple-element.30.listed, bf16[4,4,256,128]{3,2,1,0:T(8,128)(2,1)S(1)} %get-tuple-element.33.query_pairs, f32[4,8,256]{2,1,0:T(8,128)S(1)} %get-tuple-element.34.stats_in, f32[4,4,128,128]{3,2,1,0:T(8,128)S(1)} %get-tuple-element.35.attended_in, ...), custom_call_target="tpu_custom_call" | custom-call | flops 6000000000 | bytes 1000000 | tf_op jit(solution)/shard_map/pallas_call | solution.py:368
  36.6 2.2 %collective-permute-done.2.grad_up = bf16[2,128,512]{2,1,0:T(8,128)(2,1)S(1)} collective-permute-done((bf16[2,128,512]{2,1,0:T(8,128)(2,1)S(1)}, bf16[2,128,512]{2,1,0:T(8,128)(2,1)S(1)}, u32[]{:S(2)}, u32[]{:S(2)}) %collective-permute-start.2) | collective-permute-done | bytes 262176 | tf_op jit(solution)/shard_map/ppermute | solution.py:29
  38.8 4.1 %shard_map.96 = (bf16[4,4,256,128]{3,2,1,0:T(8,128)(2,1)S(1)}, f32[4,8,256]{2,1,0:T(8,128)S(1)}, bf16[2,2,128,512]{3,2,1,0:T(8,128)(2,1)S(1)}, bf16[2,2,128,512]...) custom-call(s32[72]{0:T(128)S(1)} %get-tuple-element.30.listed, s32[2,2,8]{2,1,0:T(2,128)S(1)} %copy-done.5, ...), custom_call_target="tpu_custom_call" | custom-call | flops 3000000000 | bytes 1000000 | tf_op jit(solution)/shard_map/pallas_call | solution.py:368
  42.9 2.9 %collective-permute-start.9 = (bf16[2,2,128,512]{3,2,1,0:T(8,128)(2,1)S(1)}, bf16[2,2,128,512]{3,2,1,0:T(8,128)(2,1)S(1)}, u32[]{:S(2)}, u32[]{:S(2)}) collective-permute-start(bf16[2,2,128,512]{3,2,1,0:T(8,128)(2,1)S(1)} %get-tuple-element.50), channel_id=1, source_target_pairs={{0,7},{1,0},{2,1},{3,2},{4,3},{5,4},{6,5},{7,6},{8,15},{9,8},{10,9... | collective-permute-start | bytes 1572872 | tf_op jit(solution)/shard_map/ppermute | solution.py:29
  45.9 6.1 %shard_map.97 = (f32[2,2,128,512]{3,2,1,0:T(8,128)S(1)}, f32[2,2,128,512]{3,2,1,0:T(8,128)S(1)}, bf16[2,2,128,512]{3,2,1,0:T(8,128)(2,1)S(1)}, bf16[2,2,128,512]...) custom-call(s32[72]{0:T(128)S(1)} %get-tuple-element.30.listed, f32[4,8,256]{2,1,0:T(8,128)S(1)} %get-tuple-element.38.finals, ...), custom_call_target="tpu_custom_call" | custom-call | flops 8000000000 | bytes 1000000 | tf_op jit(solution)/shard_map/pallas_call | solution.py:368
  52.0 0.7 collective-permute-done.8.add_left
  52.7 0.2 shard_map.99
  52.9 5.1 %collective-permute-start.13 = (bf16[2,2,128,512]{3,2,1,0:T(8,128)(2,1)S(1)}, bf16[2,2,128,512]{3,2,1,0:T(8,128)(2,1)S(1)}, u32[]{:S(2)}, u32[]{:S(2)}) collective-permute-start(bf16[2,2,128,512]{3,2,1,0:T(8,128)(2,1)S(1)} %get-tuple-element.51), channel_id=1, source_target_pairs={{0,120},{1,121},{2,122},{3,123},{4,124},{5,125},{6,126},{7,127},{8... | collective-permute-start | bytes 1572872 | tf_op jit(solution)/shard_map/ppermute | solution.py:29
  58.0 0.1 collective-permute-start.10
  58.2 2.8 %collective-permute-start.11 = (bf16[2,2,128,512]{3,2,1,0:T(8,128)(2,1)S(1)}, bf16[2,2,128,512]{3,2,1,0:T(8,128)(2,1)S(1)}, u32[]{:S(2)}, u32[]{:S(2)}) collective-permute-start(bf16[2,2,128,512]{3,2,1,0:T(8,128)(2,1)S(1)} %get-tuple-element.54), channel_id=1, source_target_pairs={{0,7},{1,0},{2,1},{3,2},{4,3},{5,4},{6,5},{7,6},{8,15},{9,8},{10,9... | collective-permute-start | bytes 1572872 | tf_op jit(solution)/shard_map/ppermute | solution.py:29
  61.0 7.0 %shard_map.98 = (f32[512,512]{1,0:T(8,128)S(1)}, f32[512,512]{1,0:T(8,128)S(1)}, bf16[4,128,512]{2,1,0:T(8,128)(2,1)}) custom-call(s32[72]{0:T(128)S(1)} %get-tuple-element.30.listed, f32[4,8,256]{2,1,0:T(8,128)S(1)} %get-tuple-element.38.finals, bf16[4,4,256,128]{3,2,1,0:T(8,128)(2,1)S(1)} %get-tuple-element.33.query_pairs, ...), custom_call_target="tpu_custom_call" | custom-call | flops 10000000000 | bytes 1000000 | tf_op jit(solution)/shard_map/pallas_call | solution.py:368
  68.0 1.8 %collective-permute-done.13.down = bf16[2,2,128,512]{3,2,1,0:T(8,128)(2,1)S(1)} collective-permute-done((bf16[2,2,128,512]{3,2,1,0:T(8,128)(2,1)S(1)}, bf16[2,2,128,512]{3,2,1,0:T(8,128)(2,1)S(1)}, u32[]{:S(2)}, u32[]{:S(2)}) %collective-permute-start.13) | collective-permute-done | bytes 524320 | tf_op jit(solution)/shard_map/ppermute | solution.py:29
  69.8 5.5 %collective-permute-done.12.up = bf16[2,2,128,512]{3,2,1,0:T(8,128)(2,1)S(1)} collective-permute-done((bf16[2,2,128,512]{3,2,1,0:T(8,128)(2,1)S(1)}, bf16[2,2,128,512]{3,2,1,0:T(8,128)(2,1)S(1)}, u32[]{:S(2)}, u32[]{:S(2)}) %collective-permute-start.12) | collective-permute-done | bytes 524320 | tf_op jit(solution)/shard_map/ppermute | solution.py:29
  75.3 1.2 %shard_map.100 = (bf16[2,2,128,512]{3,2,1,0:T(8,128)(2,1)}, bf16[2,2,128,512]{3,2,1,0:T(8,128)(2,1)}) custom-call(f32[512,512]{1,0:T(8,128)S(1)} %get-tuple-element.43.own_key, f32[512,512]{1,0:T(8,128)S(1)} %get-tuple-element.44.own_value, bf16[2,2,128,512]{3,2,1,0:T(8,128)(2,1)S(1)} %collective-permute-done.10.left, ...), custom_call_target="tpu_custom_call" | custom-call | flops 10000000 | bytes 1000000 | tf_op jit(solution)/shard_map/pallas_call | solution.py:368
  (29 shorter events, 0.4 us)
Async XLA Ops:
  2.0 17.8 %collective-permute-start.1 = (bf16[2,2,128,512]{3,2,1,0:T(8,128)(2,1)S(1)}, bf16[2,2,128,512]{3,2,1,0:T(8,128)(2,1)S(1)}, u32[]{:S(2)}, u32[]{:S(2)}) collective-permute-start(bf16[2,2,128,512]{3,2,1,0:T(8,128)(2,1)S(1)} %pad_maximum_fusion.3), channel_id=1, source_target_pairs={{0,120},{1,121},{2,122},{3,123},{4,124},{5,125},{6,126},{7,127},{8... | collective-permute-start | bytes 1572872 | tf_op jit(solution)/shard_map/ppermute | solution.py:29
  8.6 1.0 %copy-start.1 = (bf16[2,2,128,512]{3,2,1,0:T(8,128)(2,1)S(1)}, bf16[2,2,128,512]{3,2,1,0:T(8,128)(2,1)}, u32[]{:S(2)}) copy-start(bf16[2,2,128,512]{3,2,1,0:T(8,128)(2,1)} %param.8) | copy-start | bytes 1572868
  8.6 1.2 %copy-start.2 = (bf16[2,2,128,512]{3,2,1,0:T(8,128)(2,1)S(1)}, bf16[2,2,128,512]{3,2,1,0:T(8,128)(2,1)}, u32[]{:S(2)}) copy-start(bf16[2,2,128,512]{3,2,1,0:T(8,128)(2,1)} %param.9) | copy-start | bytes 1572868
  8.6 1.3 %copy-start = (bf16[2,2,128,512]{3,2,1,0:T(8,128)(2,1)S(1)}, bf16[2,2,128,512]{3,2,1,0:T(8,128)(2,1)}, u32[]{:S(2)}) copy-start(bf16[2,2,128,512]{3,2,1,0:T(8,128)(2,1)} %grad.1) | copy-start | bytes 1572868
  8.7 16.8 %collective-permute-start = (bf16[2,2,128,512]{3,2,1,0:T(8,128)(2,1)S(1)}, bf16[2,2,128,512]{3,2,1,0:T(8,128)(2,1)S(1)}, u32[]{:S(2)}, u32[]{:S(2)}) collective-permute-start(bf16[2,2,128,512]{3,2,1,0:T(8,128)(2,1)S(1)} %pad_maximum_fusion.2), channel_id=1, source_target_pairs={{0,8},{1,9},{2,10},{3,11},{4,12},{5,13},{6,14},{7,15},{8,16},{9,17... | collective-permute-start | bytes 1572872 | tf_op jit(solution)/shard_map/ppermute | solution.py:29
  10.1 16.6 %collective-permute-start.4 = (bf16[3,2,128,512]{3,2,1,0:T(8,128)(2,1)S(1)}, bf16[3,2,128,512]{3,2,1,0:T(8,128)(2,1)S(1)}, u32[]{:S(2)}, u32[]{:S(2)}) collective-permute-start(bf16[3,2,128,512]{3,2,1,0:T(8,128)(2,1)S(1)} %pad_maximum_fusion), channel_id=1, source_target_pairs={{0,1},{1,2},{2,3},{3,4},{4,5},{5,6},{6,7},{7,0},{8,9},{9,10},{10,1... | collective-permute-start | bytes 2359304 | tf_op jit(solution)/shard_map/ppermute | solution.py:29
  10.1 3.1 %copy-start.3 = (bf16[2,2,128,512]{3,2,1,0:T(8,128)(2,1)S(1)}, bf16[2,2,128,512]{3,2,1,0:T(8,128)(2,1)}, u32[]{:S(2)}) copy-start(bf16[2,2,128,512]{3,2,1,0:T(8,128)(2,1)} %param.7) | copy-start | bytes 1572868
  10.2 21.8 %collective-permute-start.5 = (bf16[3,2,128,512]{3,2,1,0:T(8,128)(2,1)S(1)}, bf16[3,2,128,512]{3,2,1,0:T(8,128)(2,1)S(1)}, u32[]{:S(2)}, u32[]{:S(2)}) collective-permute-start(bf16[3,2,128,512]{3,2,1,0:T(8,128)(2,1)S(1)} %pad_maximum_fusion.1), channel_id=1, source_target_pairs={{0,7},{1,0},{2,1},{3,2},{4,3},{5,4},{6,5},{7,6},{8,15},{9,8},{10,9... | collective-permute-start | bytes 2359304 | tf_op jit(solution)/shard_map/ppermute | solution.py:29
  13.2 0.7 copy-start.5
  13.2 0.7 copy-start.6
  25.5 13.2 %collective-permute-start.7 = (bf16[2,2,128,512]{3,2,1,0:T(8,128)(2,1)S(1)}, bf16[2,2,128,512]{3,2,1,0:T(8,128)(2,1)S(1)}, u32[]{:S(2)}, u32[]{:S(2)}) collective-permute-start(bf16[2,2,128,512]{3,2,1,0:T(8,128)(2,1)S(1)} %pad_maximum_fusion.4), channel_id=1, source_target_pairs={{0,7},{1,0},{2,1},{3,2},{4,3},{5,4},{6,5},{7,6},{8,15},{9,8},{10,9... | collective-permute-start | bytes 1572872 | tf_op jit(solution)/shard_map/ppermute | solution.py:29
  26.6 12.2 %collective-permute-start.6 = (bf16[2,2,128,512]{3,2,1,0:T(8,128)(2,1)S(1)}, bf16[2,2,128,512]{3,2,1,0:T(8,128)(2,1)S(1)}, u32[]{:S(2)}, u32[]{:S(2)}) collective-permute-start(bf16[2,2,128,512]{3,2,1,0:T(8,128)(2,1)S(1)} %pad_maximum_fusion.5), channel_id=1, source_target_pairs={{0,1},{1,2},{2,3},{3,4},{4,5},{5,6},{6,7},{7,0},{8,9},{9,10},{10,1... | collective-permute-start | bytes 1572872 | tf_op jit(solution)/shard_map/ppermute | solution.py:29
  26.6 12.1 %collective-permute-start.2 = (bf16[2,128,512]{2,1,0:T(8,128)(2,1)S(1)}, bf16[2,128,512]{2,1,0:T(8,128)(2,1)S(1)}, u32[]{:S(2)}, u32[]{:S(2)}) collective-permute-start(bf16[2,128,512]{2,1,0:T(8,128)(2,1)S(1)} %get-tuple-element.31), channel_id=1, source_target_pairs={{0,8},{1,9},{2,10},{3,11},{4,12},{5,13},{6,14},{7,15},{8,16},{9,17... | collective-permute-start | bytes 786440 | tf_op jit(solution)/shard_map/ppermute | solution.py:29
  26.7 12.0 %collective-permute-start.3 = (bf16[2,128,512]{2,1,0:T(8,128)(2,1)S(1)}, bf16[2,128,512]{2,1,0:T(8,128)(2,1)S(1)}, u32[]{:S(2)}, u32[]{:S(2)}) collective-permute-start(bf16[2,128,512]{2,1,0:T(8,128)(2,1)S(1)} %get-tuple-element.32), channel_id=1, source_target_pairs={{0,120},{1,121},{2,122},{3,123},{4,124},{5,125},{6,126},{7,127},{8... | collective-permute-start | bytes 786440 | tf_op jit(solution)/shard_map/ppermute | solution.py:29
  32.1 6.7 %copy-start.4 = (f32[4,512]{1,0:T(4,128)S(1)}, f32[4,512]{1,0:T(4,128)}, u32[]{:S(2)}) copy-start(f32[4,512]{1,0:T(4,128)} %gain.1) | copy-start | bytes 24580
  42.9 9.8 %collective-permute-start.8 = (bf16[2,2,128,512]{3,2,1,0:T(8,128)(2,1)S(1)}, bf16[2,2,128,512]{3,2,1,0:T(8,128)(2,1)S(1)}, u32[]{:S(2)}, u32[]{:S(2)}) collective-permute-start(bf16[2,2,128,512]{3,2,1,0:T(8,128)(2,1)S(1)} %get-tuple-element.49), channel_id=1, source_target_pairs={{0,1},{1,2},{2,3},{3,4},{4,5},{5,6},{6,7},{7,0},{8,9},{9,10},{10,1... | collective-permute-start | bytes 1572872 | tf_op jit(solution)/shard_map/ppermute | solution.py:29
  42.9 9.8 %collective-permute-start.9 = (bf16[2,2,128,512]{3,2,1,0:T(8,128)(2,1)S(1)}, bf16[2,2,128,512]{3,2,1,0:T(8,128)(2,1)S(1)}, u32[]{:S(2)}, u32[]{:S(2)}) collective-permute-start(bf16[2,2,128,512]{3,2,1,0:T(8,128)(2,1)S(1)} %get-tuple-element.50), channel_id=1, source_target_pairs={{0,7},{1,0},{2,1},{3,2},{4,3},{5,4},{6,5},{7,6},{8,15},{9,8},{10,9... | collective-permute-start | bytes 1572872 | tf_op jit(solution)/shard_map/ppermute | solution.py:29
  52.9 16.9 %collective-permute-start.13 = (bf16[2,2,128,512]{3,2,1,0:T(8,128)(2,1)S(1)}, bf16[2,2,128,512]{3,2,1,0:T(8,128)(2,1)S(1)}, u32[]{:S(2)}, u32[]{:S(2)}) collective-permute-start(bf16[2,2,128,512]{3,2,1,0:T(8,128)(2,1)S(1)} %get-tuple-element.51), channel_id=1, source_target_pairs={{0,120},{1,121},{2,122},{3,123},{4,124},{5,125},{6,126},{7,127},{8... | collective-permute-start | bytes 1572872 | tf_op jit(solution)/shard_map/ppermute | solution.py:29
  58.0 17.3 %collective-permute-start.12 = (bf16[2,2,128,512]{3,2,1,0:T(8,128)(2,1)S(1)}, bf16[2,2,128,512]{3,2,1,0:T(8,128)(2,1)S(1)}, u32[]{:S(2)}, u32[]{:S(2)}) collective-permute-start(bf16[2,2,128,512]{3,2,1,0:T(8,128)(2,1)S(1)} %get-tuple-element.52), channel_id=1, source_target_pairs={{0,8},{1,9},{2,10},{3,11},{4,12},{5,13},{6,14},{7,15},{8,16},{9,17... | collective-permute-start | bytes 1572872 | tf_op jit(solution)/shard_map/ppermute | solution.py:29
  58.0 9.9 %collective-permute-start.10 = (bf16[2,2,128,512]{3,2,1,0:T(8,128)(2,1)S(1)}, bf16[2,2,128,512]{3,2,1,0:T(8,128)(2,1)S(1)}, u32[]{:S(2)}, u32[]{:S(2)}) collective-permute-start(bf16[2,2,128,512]{3,2,1,0:T(8,128)(2,1)S(1)} %get-tuple-element.53), channel_id=1, source_target_pairs={{0,1},{1,2},{2,3},{3,4},{4,5},{5,6},{6,7},{7,0},{8,9},{9,10},{10,1... | collective-permute-start | bytes 1572872 | tf_op jit(solution)/shard_map/ppermute | solution.py:29
  58.2 9.8 %collective-permute-start.11 = (bf16[2,2,128,512]{3,2,1,0:T(8,128)(2,1)S(1)}, bf16[2,2,128,512]{3,2,1,0:T(8,128)(2,1)S(1)}, u32[]{:S(2)}, u32[]{:S(2)}) collective-permute-start(bf16[2,2,128,512]{3,2,1,0:T(8,128)(2,1)S(1)} %get-tuple-element.54), channel_id=1, source_target_pairs={{0,7},{1,0},{2,1},{3,2},{4,3},{5,4},{6,5},{7,6},{8,15},{9,8},{10,9... | collective-permute-start | bytes 1572872 | tf_op jit(solution)/shard_map/ppermute | solution.py:29

commit v3 on v2

--- a/solution.py
+++ b/solution.py
@@ -396,9 +396,8 @@
     def corners(c):
         return jnp.stack([from_up[:, c], from_down[:, c]], axis=1)
 
-    for_left, for_right = corners(0), corners(1)
-    corner_left = shifted(for_right, 0, 1)
-    corner_right = shifted(for_left, 0, -1)
+    corner_left = shifted(corners(1), 0, 1)
+    corner_right = shifted(corners(0), 0, -1)
 
     key_rows, value_rows = key_tiles.reshape(4 * PATCH, D), value_tiles.reshape(4 * PATCH, D)
     listed, query_pairs, stats, attended = call(
@@ -406,7 +405,7 @@
         [((72,), jnp.int32), PAIR_SHAPE, STATS, TURNED], 6 * 10**9,
         partners, counts, query_tiles.reshape((4,) + TILE), key_rows, value_rows,
     )
-    upper, lower, *_ = lax.optimization_barrier((out_grad[0], out_grad[1], for_left, for_right))
+    upper, lower, stats = lax.optimization_barrier((out_grad[0], out_grad[1], stats))
     grad_up, grad_down = shifted(lower, 1, 0), shifted(upper, -1, 0)
     stats, attended = call(
         edge_totals_kernel, [STATS, TURNED], 6 * 10**9,

time: 77 us -> 67.7 us (0.88)
  waiting for transfers between devices: 17 us -> 12.2 us
  starting transfers between devices: 27.2 us -> 24 us
  local copies, waits for them, and re-layouts: 3.33 us -> 2.19 us
    ppermute x14, waiting for transfers between devices: 17 us -> 12.2 us  [shifted(): return lax.ppermute(x, ('span', 'chord'), pairs)]
    ppermute x14, starting transfers between devices: 27.2 us -> 24 us  [shifted(): return lax.ppermute(x, ('span', 'chord'), pairs)]
    unnamed x14, local copies, waits for them, and re-layouts: 1.85 us -> 0.71 us
  transfers between devices with their start and end apart: 14 -> 14, of which waited for: 6 -> 5; matrix products, arithmetic and copies ran while one was open for 1% -> 1% of each run, Pallas kernels for 29% -> 33%
where the time goes in v3:
time: 67.7 us; the launch traced here: 67.5 us
  Pallas kernels  27.9 us (41%)
  starting transfers between devices  24 us (35%)
  waiting for transfers between devices  12.2 us (18%)
  local copies, waits for them, and re-layouts  2.19 us (3%)
  between operations  0.83 us (1%)
    pallas_call x7, Pallas kernels, call(): pl.pallas_call(kernel, out_shape=[jax.ShapeDtypeStruct(shape, kind) for s...  27.9 us
    ppermute x14, starting transfers between devices, shifted(): return lax.ppermute(x, ('span', 'chord'), pairs)  24 us
    ppermute x14, waiting for transfers between devices, shifted(): return lax.ppermute(x, ('span', 'chord'), pairs)  12.2 us
  transfers between devices with their start and end apart: 14, of which 5 were waited for; matrix products, arithmetic and copies ran while one was open for 1% of the time, Pallas kernels for 33%

profile of v3, /device:TPU:0, one launch (start us, length us, event | category | flops | bytes accessed | tf_op | source)
XLA Modules:
  0.0 67.5 jit_solution(9906909047316676864)
XLA Ops:
  0.6 1.3 %fusion.2 = (bf16[1,2,128,512]{3,2,1,0:T(8,128)(2,1)S(1)}, bf16[1,2,128,512]{3,2,1,0:T(8,128)(2,1)S(1)}, bf16[1,2,128,512]{3,2,1,0:T(8,128)(2,1)S(1)}, bf16[1,2,128,512]{3,2,1,0:T(8,128)(2,1)S(1)}) fusion(bf16[2,2,128,512]{3,2,1,0:T(8,128)(2,1)} %param.8, bf16[2,2,128,512]{3,2,1,0:T(8,128)(2,1)} %param.9), kind=kLoop, calls=%fused_computation.16 | loop fusion | bytes 2097152 | tf_op jit(solution)/shard_map/slice | solution.py:389
  1.9 0.1 pad_maximum_fusion.2
  2.0 1.7 %collective-permute-start.4 = (bf16[2,2,128,512]{3,2,1,0:T(8,128)(2,1)S(1)}, bf16[2,2,128,512]{3,2,1,0:T(8,128)(2,1)S(1)}, u32[]{:S(2)}, u32[]{:S(2)}) collective-permute-start(bf16[2,2,128,512]{3,2,1,0:T(8,128)(2,1)S(1)} %pad_maximum_fusion.2), channel_id=1, source_target_pairs={{0,8},{1,9},{2,10},{3,11},{4,12},{5,13},{6,14},{7,15},{8,16},{9,17... | collective-permute-start | bytes 1572872 | tf_op jit(solution)/shard_map/ppermute | solution.py:29
  3.7 0.1 pad_maximum_fusion.3
  3.8 5.0 %collective-permute-start.5 = (bf16[2,2,128,512]{3,2,1,0:T(8,128)(2,1)S(1)}, bf16[2,2,128,512]{3,2,1,0:T(8,128)(2,1)S(1)}, u32[]{:S(2)}, u32[]{:S(2)}) collective-permute-start(bf16[2,2,128,512]{3,2,1,0:T(8,128)(2,1)S(1)} %pad_maximum_fusion.3), channel_id=1, source_target_pairs={{0,120},{1,121},{2,122},{3,123},{4,124},{5,125},{6,126},{7,127},{8... | collective-permute-start | bytes 1572872 | tf_op jit(solution)/shard_map/ppermute | solution.py:29
  8.8 0.1 slice_bitcast_fusion.1
  8.9 0.1 pad_maximum_fusion
  9.0 0.0 collective-permute-start.2
  9.0 0.1 pad_maximum_fusion.1
  9.1 2.9 %collective-permute-start.3 = (bf16[3,2,128,512]{3,2,1,0:T(8,128)(2,1)S(1)}, bf16[3,2,128,512]{3,2,1,0:T(8,128)(2,1)S(1)}, u32[]{:S(2)}, u32[]{:S(2)}) collective-permute-start(bf16[3,2,128,512]{3,2,1,0:T(8,128)(2,1)S(1)} %pad_maximum_fusion.1), channel_id=1, source_target_pairs={{0,7},{1,0},{2,1},{3,2},{4,3},{5,4},{6,5},{7,6},{8,15},{9,8},{10,9... | collective-permute-start | bytes 2359304 | tf_op jit(solution)/shard_map/ppermute | solution.py:29
  12.1 0.7 copy-done.5
  12.8 4.8 %shard_map.94 = (s32[72]{0:T(128)S(1)}, bf16[4,4,256,128]{3,2,1,0:T(8,128)(2,1)S(1)}, f32[4,8,256]{2,1,0:T(8,128)S(1)}, f32[4,4,128,128]{3,2,1,0:T(8,128)S(1)}) custom-call(s32[2,2,8]{2,1,0:T(2,128)S(1)} %copy-done.5, s32[2,2]{1,0:T(2,128)S(1)} %copy-done.6, bf16[4,128,512]{2,1,0:T(8,128)(2,1)S(1)} %bitcast.36, bf16[512,512]{1,0:T(8,128)(2,1)S(1)} %bitcast.32, ...), custom_call_target="tpu_custom_call" | custom-call | flops 6000000000 | bytes 1000000 | tf_op jit(solution)/shard_map/pallas_call | solution.py:368
  17.6 0.1 collective-permute-start
  17.7 2.8 %collective-permute-done.4.from_up = bf16[2,2,128,512]{3,2,1,0:T(8,128)(2,1)S(1)} collective-permute-done((bf16[2,2,128,512]{3,2,1,0:T(8,128)(2,1)S(1)}, bf16[2,2,128,512]{3,2,1,0:T(8,128)(2,1)S(1)}, u32[]{:S(2)}, u32[]{:S(2)}) %collective-permute-start.4) | collective-permute-done | bytes 524320 | tf_op jit(solution)/shard_map/ppermute | solution.py:29
  20.5 2.8 %collective-permute-start.1 = (bf16[2,128,512]{2,1,0:T(8,128)(2,1)S(1)}, bf16[2,128,512]{2,1,0:T(8,128)(2,1)S(1)}, u32[]{:S(2)}, u32[]{:S(2)}) collective-permute-start(bf16[2,128,512]{2,1,0:T(8,128)(2,1)S(1)} %get-tuple-element.34), channel_id=1, source_target_pairs={{0,120},{1,121},{2,122},{3,123},{4,124},{5,125},{6,126},{7,127},{8... | collective-permute-start | bytes 786440 | tf_op jit(solution)/shard_map/ppermute | solution.py:29
  23.4 0.1 pad_maximum_fusion.4
  23.5 0.1 pad_maximum_fusion.5
  23.5 2.9 %collective-permute-start.7 = (bf16[2,2,128,512]{3,2,1,0:T(8,128)(2,1)S(1)}, bf16[2,2,128,512]{3,2,1,0:T(8,128)(2,1)S(1)}, u32[]{:S(2)}, u32[]{:S(2)}) collective-permute-start(bf16[2,2,128,512]{3,2,1,0:T(8,128)(2,1)S(1)} %pad_maximum_fusion.5), channel_id=1, source_target_pairs={{0,7},{1,0},{2,1},{3,2},{4,3},{5,4},{6,5},{7,6},{8,15},{9,8},{10,9... | collective-permute-start | bytes 1572872 | tf_op jit(solution)/shard_map/ppermute | solution.py:29
  26.5 4.5 %shard_map.95 = (f32[4,8,256]{2,1,0:T(8,128)S(1)}, f32[4,4,128,128]{3,2,1,0:T(8,128)S(1)}) custom-call(s32[72]{0:T(128)S(1)} %get-tuple-element.31.listed, bf16[4,4,256,128]{3,2,1,0:T(8,128)(2,1)S(1)} %get-tuple-element.35.query_pairs, f32[4,8,256]{2,1,0:T(8,128)S(1)} %get-tuple-element.36.stats_in, f32[4,4,128,128]{3,2,1,0:T(8,128)S(1)} %get-tuple-element.37.attended_in, ...), custom_call_target="tpu_custom_call" | custom-call | flops 6000000000 | bytes 1000000 | tf_op jit(solution)/shard_map/pallas_call | solution.py:368
  31.0 2.2 %collective-permute-done.6.corner_left = bf16[2,2,128,512]{3,2,1,0:T(8,128)(2,1)S(1)} collective-permute-done((bf16[2,2,128,512]{3,2,1,0:T(8,128)(2,1)S(1)}, bf16[2,2,128,512]{3,2,1,0:T(8,128)(2,1)S(1)}, u32[]{:S(2)}, u32[]{:S(2)}) %collective-permute-start.6) | collective-permute-done | bytes 524320 | tf_op jit(solution)/shard_map/ppermute | solution.py:29
  33.3 4.1 %shard_map.96 = (bf16[4,4,256,128]{3,2,1,0:T(8,128)(2,1)S(1)}, f32[4,8,256]{2,1,0:T(8,128)S(1)}, bf16[2,2,128,512]{3,2,1,0:T(8,128)(2,1)S(1)}, bf16[2,2,128,512]...) custom-call(s32[72]{0:T(128)S(1)} %get-tuple-element.31.listed, s32[2,2,8]{2,1,0:T(2,128)S(1)} %copy-done.5, ...), custom_call_target="tpu_custom_call" | custom-call | flops 3000000000 | bytes 1000000 | tf_op jit(solution)/shard_map/pallas_call | solution.py:368
  37.4 0.5 collective-permute-start.8
  37.8 2.6 %collective-permute-start.9 = (bf16[2,2,128,512]{3,2,1,0:T(8,128)(2,1)S(1)}, bf16[2,2,128,512]{3,2,1,0:T(8,128)(2,1)S(1)}, u32[]{:S(2)}, u32[]{:S(2)}) collective-permute-start(bf16[2,2,128,512]{3,2,1,0:T(8,128)(2,1)S(1)} %get-tuple-element.52), channel_id=1, source_target_pairs={{0,7},{1,0},{2,1},{3,2},{4,3},{5,4},{6,5},{7,6},{8,15},{9,8},{10,9... | collective-permute-start | bytes 1572872 | tf_op jit(solution)/shard_map/ppermute | solution.py:29
  40.4 6.1 %shard_map.97 = (f32[2,2,128,512]{3,2,1,0:T(8,128)S(1)}, f32[2,2,128,512]{3,2,1,0:T(8,128)S(1)}, bf16[2,2,128,512]{3,2,1,0:T(8,128)(2,1)S(1)}, bf16[2,2,128,512]...) custom-call(s32[72]{0:T(128)S(1)} %get-tuple-element.31.listed, f32[4,8,256]{2,1,0:T(8,128)S(1)} %get-tuple-element.40.finals, ...), custom_call_target="tpu_custom_call" | custom-call | flops 8000000000 | bytes 1000000 | tf_op jit(solution)/shard_map/pallas_call | solution.py:368
  46.6 0.7 %collective-permute-done.8.add_left = bf16[2,2,128,512]{3,2,1,0:T(8,128)(2,1)S(1)} collective-permute-done((bf16[2,2,128,512]{3,2,1,0:T(8,128)(2,1)S(1)}, bf16[2,2,128,512]{3,2,1,0:T(8,128)(2,1)S(1)}, u32[]{:S(2)}, u32[]{:S(2)}) %collective-permute-start.8) | collective-permute-done | bytes 524320 | tf_op jit(solution)/shard_map/ppermute | solution.py:29
  47.3 0.2 shard_map.99
  47.4 2.5 %collective-permute-start.13 = (bf16[2,2,128,512]{3,2,1,0:T(8,128)(2,1)S(1)}, bf16[2,2,128,512]{3,2,1,0:T(8,128)(2,1)S(1)}, u32[]{:S(2)}, u32[]{:S(2)}) collective-permute-start(bf16[2,2,128,512]{3,2,1,0:T(8,128)(2,1)S(1)} %get-tuple-element.53), channel_id=1, source_target_pairs={{0,120},{1,121},{2,122},{3,123},{4,124},{5,125},{6,126},{7,127},{8... | collective-permute-start | bytes 1572872 | tf_op jit(solution)/shard_map/ppermute | solution.py:29
  49.9 3.0 %collective-permute-start.11 = (bf16[2,2,128,512]{3,2,1,0:T(8,128)(2,1)S(1)}, bf16[2,2,128,512]{3,2,1,0:T(8,128)(2,1)S(1)}, u32[]{:S(2)}, u32[]{:S(2)}) collective-permute-start(bf16[2,2,128,512]{3,2,1,0:T(8,128)(2,1)S(1)} %get-tuple-element.56), channel_id=1, source_target_pairs={{0,7},{1,0},{2,1},{3,2},{4,3},{5,4},{6,5},{7,6},{8,15},{9,8},{10,9... | collective-permute-start | bytes 1572872 | tf_op jit(solution)/shard_map/ppermute | solution.py:29
  52.9 7.0 %shard_map.98 = (f32[512,512]{1,0:T(8,128)S(1)}, f32[512,512]{1,0:T(8,128)S(1)}, bf16[4,128,512]{2,1,0:T(8,128)(2,1)}) custom-call(s32[72]{0:T(128)S(1)} %get-tuple-element.31.listed, f32[4,8,256]{2,1,0:T(8,128)S(1)} %get-tuple-element.40.finals, bf16[4,4,256,128]{3,2,1,0:T(8,128)(2,1)S(1)} %get-tuple-element.35.query_pairs, ...), custom_call_target="tpu_custom_call" | custom-call | flops 10000000000 | bytes 1000000 | tf_op jit(solution)/shard_map/pallas_call | solution.py:368
  59.9 1.0 %collective-permute-done.13.down = bf16[2,2,128,512]{3,2,1,0:T(8,128)(2,1)S(1)} collective-permute-done((bf16[2,2,128,512]{3,2,1,0:T(8,128)(2,1)S(1)}, bf16[2,2,128,512]{3,2,1,0:T(8,128)(2,1)S(1)}, u32[]{:S(2)}, u32[]{:S(2)}) %collective-permute-start.13) | collective-permute-done | bytes 524320 | tf_op jit(solution)/shard_map/ppermute | solution.py:29
  60.8 5.5 %collective-permute-done.12.up = bf16[2,2,128,512]{3,2,1,0:T(8,128)(2,1)S(1)} collective-permute-done((bf16[2,2,128,512]{3,2,1,0:T(8,128)(2,1)S(1)}, bf16[2,2,128,512]{3,2,1,0:T(8,128)(2,1)S(1)}, u32[]{:S(2)}, u32[]{:S(2)}) %collective-permute-start.12) | collective-permute-done | bytes 524320 | tf_op jit(solution)/shard_map/ppermute | solution.py:29
  66.3 1.2 %shard_map.100 = (bf16[2,2,128,512]{3,2,1,0:T(8,128)(2,1)}, bf16[2,2,128,512]{3,2,1,0:T(8,128)(2,1)}) custom-call(f32[512,512]{1,0:T(8,128)S(1)} %get-tuple-element.45.own_key, f32[512,512]{1,0:T(8,128)S(1)} %get-tuple-element.46.own_value, bf16[2,2,128,512]{3,2,1,0:T(8,128)(2,1)S(1)} %collective-permute-done.10.left, ...), custom_call_target="tpu_custom_call" | custom-call | flops 10000000 | bytes 1000000 | tf_op jit(solution)/shard_map/pallas_call | solution.py:368
  (29 shorter events, 0.2 us)
Async XLA Ops:
  2.0 18.6 %collective-permute-start.4 = (bf16[2,2,128,512]{3,2,1,0:T(8,128)(2,1)S(1)}, bf16[2,2,128,512]{3,2,1,0:T(8,128)(2,1)S(1)}, u32[]{:S(2)}, u32[]{:S(2)}) collective-permute-start(bf16[2,2,128,512]{3,2,1,0:T(8,128)(2,1)S(1)} %pad_maximum_fusion.2), channel_id=1, source_target_pairs={{0,8},{1,9},{2,10},{3,11},{4,12},{5,13},{6,14},{7,15},{8,16},{9,17... | collective-permute-start | bytes 1572872 | tf_op jit(solution)/shard_map/ppermute | solution.py:29
  3.7 5.1 %copy-start.1 = (bf16[2,2,128,512]{3,2,1,0:T(8,128)(2,1)S(1)}, bf16[2,2,128,512]{3,2,1,0:T(8,128)(2,1)}, u32[]{:S(2)}) copy-start(bf16[2,2,128,512]{3,2,1,0:T(8,128)(2,1)} %param.8) | copy-start | bytes 1572868
  3.7 5.1 %copy-start.2 = (bf16[2,2,128,512]{3,2,1,0:T(8,128)(2,1)S(1)}, bf16[2,2,128,512]{3,2,1,0:T(8,128)(2,1)}, u32[]{:S(2)}) copy-start(bf16[2,2,128,512]{3,2,1,0:T(8,128)(2,1)} %param.9) | copy-start | bytes 1572868
  3.7 5.1 %copy-start = (bf16[2,2,128,512]{3,2,1,0:T(8,128)(2,1)S(1)}, bf16[2,2,128,512]{3,2,1,0:T(8,128)(2,1)}, u32[]{:S(2)}) copy-start(bf16[2,2,128,512]{3,2,1,0:T(8,128)(2,1)} %grad.1) | copy-start | bytes 1572868
  3.8 19.6 %collective-permute-start.5 = (bf16[2,2,128,512]{3,2,1,0:T(8,128)(2,1)S(1)}, bf16[2,2,128,512]{3,2,1,0:T(8,128)(2,1)S(1)}, u32[]{:S(2)}, u32[]{:S(2)}) collective-permute-start(bf16[2,2,128,512]{3,2,1,0:T(8,128)(2,1)S(1)} %pad_maximum_fusion.3), channel_id=1, source_target_pairs={{0,120},{1,121},{2,122},{3,123},{4,124},{5,125},{6,126},{7,127},{8... | collective-permute-start | bytes 1572872 | tf_op jit(solution)/shard_map/ppermute | solution.py:29
  9.0 14.5 %collective-permute-start.2 = (bf16[3,2,128,512]{3,2,1,0:T(8,128)(2,1)S(1)}, bf16[3,2,128,512]{3,2,1,0:T(8,128)(2,1)S(1)}, u32[]{:S(2)}, u32[]{:S(2)}) collective-permute-start(bf16[3,2,128,512]{3,2,1,0:T(8,128)(2,1)S(1)} %pad_maximum_fusion), channel_id=1, source_target_pairs={{0,1},{1,2},{2,3},{3,4},{4,5},{5,6},{6,7},{7,0},{8,9},{9,10},{10,1... | collective-permute-start | bytes 2359304 | tf_op jit(solution)/shard_map/ppermute | solution.py:29
  9.0 3.1 %copy-start.3 = (bf16[2,2,128,512]{3,2,1,0:T(8,128)(2,1)S(1)}, bf16[2,2,128,512]{3,2,1,0:T(8,128)(2,1)}, u32[]{:S(2)}) copy-start(bf16[2,2,128,512]{3,2,1,0:T(8,128)(2,1)} %param.7) | copy-start | bytes 1572868
  9.1 17.3 %collective-permute-start.3 = (bf16[3,2,128,512]{3,2,1,0:T(8,128)(2,1)S(1)}, bf16[3,2,128,512]{3,2,1,0:T(8,128)(2,1)S(1)}, u32[]{:S(2)}, u32[]{:S(2)}) collective-permute-start(bf16[3,2,128,512]{3,2,1,0:T(8,128)(2,1)S(1)} %pad_maximum_fusion.1), channel_id=1, source_target_pairs={{0,7},{1,0},{2,1},{3,2},{4,3},{5,4},{6,5},{7,6},{8,15},{9,8},{10,9... | collective-permute-start | bytes 2359304 | tf_op jit(solution)/shard_map/ppermute | solution.py:29
  12.1 0.7 %copy-start.5 = (s32[2,2,8]{2,1,0:T(2,128)S(1)}, s32[2,2,8]{2,1,0:T(2,128)}, u32[]{:S(2)}) copy-start(s32[2,2,8]{2,1,0:T(2,128)} %partners.3) | copy-start | bytes 388
  12.1 0.7 %copy-start.6 = (s32[2,2]{1,0:T(2,128)S(1)}, s32[2,2]{1,0:T(2,128)}, u32[]{:S(2)}) copy-start(s32[2,2]{1,0:T(2,128)} %counts.1) | copy-start | bytes 52
  17.6 13.4 %collective-permute-start = (bf16[2,128,512]{2,1,0:T(8,128)(2,1)S(1)}, bf16[2,128,512]{2,1,0:T(8,128)(2,1)S(1)}, u32[]{:S(2)}, u32[]{:S(2)}) collective-permute-start(bf16[2,128,512]{2,1,0:T(8,128)(2,1)S(1)} %get-tuple-element.33), channel_id=1, source_target_pairs={{0,8},{1,9},{2,10},{3,11},{4,12},{5,13},{6,14},{7,15},{8,16},{9,17... | collective-permute-start | bytes 786440 | tf_op jit(solution)/shard_map/ppermute | solution.py:29
  20.5 10.5 %collective-permute-start.1 = (bf16[2,128,512]{2,1,0:T(8,128)(2,1)S(1)}, bf16[2,128,512]{2,1,0:T(8,128)(2,1)S(1)}, u32[]{:S(2)}, u32[]{:S(2)}) collective-permute-start(bf16[2,128,512]{2,1,0:T(8,128)(2,1)S(1)} %get-tuple-element.34), channel_id=1, source_target_pairs={{0,120},{1,121},{2,122},{3,123},{4,124},{5,125},{6,126},{7,127},{8... | collective-permute-start | bytes 786440 | tf_op jit(solution)/shard_map/ppermute | solution.py:29
  23.4 9.8 %collective-permute-start.6 = (bf16[2,2,128,512]{3,2,1,0:T(8,128)(2,1)S(1)}, bf16[2,2,128,512]{3,2,1,0:T(8,128)(2,1)S(1)}, u32[]{:S(2)}, u32[]{:S(2)}) collective-permute-start(bf16[2,2,128,512]{3,2,1,0:T(8,128)(2,1)S(1)} %pad_maximum_fusion.4), channel_id=1, source_target_pairs={{0,1},{1,2},{2,3},{3,4},{4,5},{5,6},{6,7},{7,0},{8,9},{9,10},{10,1... | collective-permute-start | bytes 1572872 | tf_op jit(solution)/shard_map/ppermute | solution.py:29
  23.5 9.7 %collective-permute-start.7 = (bf16[2,2,128,512]{3,2,1,0:T(8,128)(2,1)S(1)}, bf16[2,2,128,512]{3,2,1,0:T(8,128)(2,1)S(1)}, u32[]{:S(2)}, u32[]{:S(2)}) collective-permute-start(bf16[2,2,128,512]{3,2,1,0:T(8,128)(2,1)S(1)} %pad_maximum_fusion.5), channel_id=1, source_target_pairs={{0,7},{1,0},{2,1},{3,2},{4,3},{5,4},{6,5},{7,6},{8,15},{9,8},{10,9... | collective-permute-start | bytes 1572872 | tf_op jit(solution)/shard_map/ppermute | solution.py:29
  26.5 6.8 %copy-start.4 = (f32[4,512]{1,0:T(4,128)S(1)}, f32[4,512]{1,0:T(4,128)}, u32[]{:S(2)}) copy-start(f32[4,512]{1,0:T(4,128)} %gain.1) | copy-start | bytes 24580
  37.4 9.9 %collective-permute-start.8 = (bf16[2,2,128,512]{3,2,1,0:T(8,128)(2,1)S(1)}, bf16[2,2,128,512]{3,2,1,0:T(8,128)(2,1)S(1)}, u32[]{:S(2)}, u32[]{:S(2)}) collective-permute-start(bf16[2,2,128,512]{3,2,1,0:T(8,128)(2,1)S(1)} %get-tuple-element.51), channel_id=1, source_target_pairs={{0,1},{1,2},{2,3},{3,4},{4,5},{5,6},{6,7},{7,0},{8,9},{9,10},{10,1... | collective-permute-start | bytes 1572872 | tf_op jit(solution)/shard_map/ppermute | solution.py:29
  37.8 9.4 %collective-permute-start.9 = (bf16[2,2,128,512]{3,2,1,0:T(8,128)(2,1)S(1)}, bf16[2,2,128,512]{3,2,1,0:T(8,128)(2,1)S(1)}, u32[]{:S(2)}, u32[]{:S(2)}) collective-permute-start(bf16[2,2,128,512]{3,2,1,0:T(8,128)(2,1)S(1)} %get-tuple-element.52), channel_id=1, source_target_pairs={{0,7},{1,0},{2,1},{3,2},{4,3},{5,4},{6,5},{7,6},{8,15},{9,8},{10,9... | collective-permute-start | bytes 1572872 | tf_op jit(solution)/shard_map/ppermute | solution.py:29
  47.4 13.4 %collective-permute-start.13 = (bf16[2,2,128,512]{3,2,1,0:T(8,128)(2,1)S(1)}, bf16[2,2,128,512]{3,2,1,0:T(8,128)(2,1)S(1)}, u32[]{:S(2)}, u32[]{:S(2)}) collective-permute-start(bf16[2,2,128,512]{3,2,1,0:T(8,128)(2,1)S(1)} %get-tuple-element.53), channel_id=1, source_target_pairs={{0,120},{1,121},{2,122},{3,123},{4,124},{5,125},{6,126},{7,127},{8... | collective-permute-start | bytes 1572872 | tf_op jit(solution)/shard_map/ppermute | solution.py:29
  49.9 16.4 %collective-permute-start.12 = (bf16[2,2,128,512]{3,2,1,0:T(8,128)(2,1)S(1)}, bf16[2,2,128,512]{3,2,1,0:T(8,128)(2,1)S(1)}, u32[]{:S(2)}, u32[]{:S(2)}) collective-permute-start(bf16[2,2,128,512]{3,2,1,0:T(8,128)(2,1)S(1)} %get-tuple-element.54), channel_id=1, source_target_pairs={{0,8},{1,9},{2,10},{3,11},{4,12},{5,13},{6,14},{7,15},{8,16},{9,17... | collective-permute-start | bytes 1572872 | tf_op jit(solution)/shard_map/ppermute | solution.py:29
  49.9 9.9 %collective-permute-start.10 = (bf16[2,2,128,512]{3,2,1,0:T(8,128)(2,1)S(1)}, bf16[2,2,128,512]{3,2,1,0:T(8,128)(2,1)S(1)}, u32[]{:S(2)}, u32[]{:S(2)}) collective-permute-start(bf16[2,2,128,512]{3,2,1,0:T(8,128)(2,1)S(1)} %get-tuple-element.55), channel_id=1, source_target_pairs={{0,1},{1,2},{2,3},{3,4},{4,5},{5,6},{6,7},{7,0},{8,9},{9,10},{10,1... | collective-permute-start | bytes 1572872 | tf_op jit(solution)/shard_map/ppermute | solution.py:29
  49.9 9.9 %collective-permute-start.11 = (bf16[2,2,128,512]{3,2,1,0:T(8,128)(2,1)S(1)}, bf16[2,2,128,512]{3,2,1,0:T(8,128)(2,1)S(1)}, u32[]{:S(2)}, u32[]{:S(2)}) collective-permute-start(bf16[2,2,128,512]{3,2,1,0:T(8,128)(2,1)S(1)} %get-tuple-element.56), channel_id=1, source_target_pairs={{0,7},{1,0},{2,1},{3,2},{4,3},{5,4},{6,5},{7,6},{8,15},{9,8},{10,9... | collective-permute-start | bytes 1572872 | tf_op jit(solution)/shard_map/ppermute | solution.py:29

commit v4 on v3

--- a/solution.py
+++ b/solution.py
@@ -181,10 +181,9 @@
     return prob.astype(jnp.bfloat16), (prob * (g - delta)).astype(jnp.bfloat16)
 
 
-def corner_kernel(
-    span_total, chord_total, listed, partners, gain, grad, grad_up, grad_down, from_left, from_right,
-    stats_in, attended_in, query_pairs, corner_left, corner_right,
-    grad_pairs, finals, left_back, right_back, dq_out,
+def mixed_kernel(
+    span_total, chord_total, partners, gain, grad, grad_up, grad_down, from_left, from_right, after,
+    grad_pairs, grad_turned,
 ):
     first = partners[0, 0, 0]
     row, column = lax.div(first, chord_total), lax.rem(first, chord_total)
@@ -192,14 +191,9 @@
         jnp.where(x, 1.0, 0.0)
         for x in (row > 0, row < span_total - 2, column > 0, column < chord_total - 2)
     ]
-    patches = range(4)
-
-    def source(p):
-        return (corner_left, corner_right)[p % 2]
-
-    def step(h, carry):
-        pairs, grad_turned = [], []
-        for p in patches:
+
+    def step(h, carry):
+        for p in range(4):
             s, c = p // 2, p % 2
             near = (
                 grad[0, c, :, cols(h)] if s == 1 else grad_up[c, :, cols(h)],
@@ -215,16 +209,28 @@
                     factor = factor * inside[n]
                 mixed = mixed + factor * near[n].astype(jnp.float32)
             mixed = mixed.astype(jnp.bfloat16)
-            pair = stacked_pair(mixed)
-            grad_pairs[h, p] = pair
-            pairs.append(pair)
-            grad_turned.append(mixed.T)
+            grad_pairs[h, p] = stacked_pair(mixed)
+            grad_turned[h, p] = mixed.T
+        return carry
+
+    lax.fori_loop(0, PAIRS, step, 0)
+
+
+def corner_kernel(
+    listed, stats_in, attended_in, query_pairs, grad_pairs, grad_turned, corner_left, corner_right,
+    finals, left_back, right_back, score_grads,
+):
+    patches = range(4)
+
+    def source(p):
+        return (corner_left, corner_right)[p % 2]
+
+    def step(h, carry):
         key_rows = [source(p)[0, p // 2, :, cols(h)] for p in patches]
         value_rows = [source(p)[1, p // 2, :, cols(h)] for p in patches]
         scores = [product(key_rows[p], query_pairs[h, p]) for p in patches]
-        g = [product(value_rows[p], pairs[p]) for p in patches]
+        g = [product(value_rows[p], grad_pairs[h, p]) for p in patches]
         value_turned = [x.T for x in value_rows]
-        key_turned = [x.T for x in key_rows]
         half, score_grad = [], []
         for p in patches:
             missing = penalty(listed, p, CORNERS[p])
@@ -235,7 +241,7 @@
             total = old_total * fade + jnp.sum(e, axis=0, keepdims=True)
             attended = diagonal(matmul(value_turned[p], e.astype(jnp.bfloat16)))
             attended = attended + attended_in[h, p] * per_head(fade)
-            dots = grad_turned[p].astype(jnp.float32) * attended
+            dots = grad_turned[h, p].astype(jnp.float32) * attended
             dot = jnp.concatenate(
                 [jnp.sum(dots[:64], axis=0, keepdims=True), jnp.sum(dots[64:], axis=0, keepdims=True)], axis=1
             )
@@ -249,8 +255,8 @@
         for p in patches:
             back = (left_back, right_back)[p % 2]
             back[0, p // 2, :, cols(h)] = matmul(score_grad[p], query_pairs[h, p]).astype(jnp.bfloat16)
-            back[1, p // 2, :, cols(h)] = matmul(half[p], pairs[p]).astype(jnp.bfloat16)
-            dq_out[h, p] = diagonal(matmul(key_turned[p], score_grad[p]))
+            back[1, p // 2, :, cols(h)] = matmul(half[p], grad_pairs[h, p]).astype(jnp.bfloat16)
+            score_grads[h, p] = score_grad[p]
         return carry
 
     lax.fori_loop(0, PAIRS, step, 0)
@@ -270,7 +276,8 @@
 
 
 def edge_kernel(
-    listed, finals, query_pairs, grad_pairs, dq_in, from_up, from_down, from_left, from_right,
+    listed, finals, query_pairs, grad_pairs, score_grads, corner_left, corner_right,
+    from_up, from_down, from_left, from_right,
     up_sum, down_sum, left_back, right_back, dq_out,
 ):
     ends = ((from_up, UP), (from_down, DOWN))
@@ -290,7 +297,8 @@
                 h, p, key_rows, value_rows, key_rows.T, listed, pair[0][1] + pair[1][1],
                 finals, query_pairs, grad_pairs,
             )
-            dq_out[h, p] = dq_in[h, p] + dq
+            corner_rows = (corner_left, corner_right)[c][0, s, :, cols(h)]
+            dq_out[h, p] = dq + diagonal(matmul(corner_rows.T, score_grads[h, p]))
             both = jnp.concatenate([dk, dv], axis=1)
             end_sums[s] = end_sums[s] + both[:256]
             side_sums[c] = side_sums[c] + both[256:]
@@ -390,8 +398,9 @@
 
     from_up = shifted(packed((key_tiles, value_tiles), 1), 1, 0)
     from_down = shifted(packed((key_tiles, value_tiles), 0), -1, 0)
-    from_left = shifted(packed((key_tiles, value_tiles, out_grad), every, 1), 0, 1)
-    from_right = shifted(packed((key_tiles, value_tiles, out_grad), every, 0), 0, -1)
+    for_left = packed((key_tiles, value_tiles, out_grad), every, 0)
+    for_right = packed((key_tiles, value_tiles, out_grad), every, 1)
+    from_left, from_right = shifted(for_right, 0, 1), shifted(for_left, 0, -1)
 
     def corners(c):
         return jnp.stack([from_up[:, c], from_down[:, c]], axis=1)
@@ -405,17 +414,20 @@
         [((72,), jnp.int32), PAIR_SHAPE, STATS, TURNED], 6 * 10**9,
         partners, counts, query_tiles.reshape((4,) + TILE), key_rows, value_rows,
     )
-    upper, lower, stats = lax.optimization_barrier((out_grad[0], out_grad[1], stats))
+    upper, lower, *_ = lax.optimization_barrier((out_grad[0], out_grad[1], for_left, for_right))
     grad_up, grad_down = shifted(lower, 1, 0), shifted(upper, -1, 0)
     stats, attended = call(
         edge_totals_kernel, [STATS, TURNED], 6 * 10**9,
         listed, query_pairs, stats, attended, from_up, from_down, from_left, from_right,
     )
-    grad_pairs, finals, left_back, right_back, dq = call(
-        functools.partial(corner_kernel, span_total, chord_total),
-        [PAIR_SHAPE, STATS, TWO, TWO, TURNED], 3 * 10**9,
-        listed, partners, mix_gain, out_grad, grad_up, grad_down, from_left, from_right,
-        stats, attended, query_pairs, corner_left, corner_right,
+    grad_pairs, grad_turned = call(
+        functools.partial(mixed_kernel, span_total, chord_total),
+        [PAIR_SHAPE, ((PAIRS, 4, 128, PATCH), BF16)], 10**9,
+        partners, mix_gain, out_grad, grad_up, grad_down, from_left, from_right, stats,
+    )
+    finals, left_back, right_back, score_grads = call(
+        corner_kernel, [STATS, TWO, TWO, ((PAIRS, 4, PATCH, 256), BF16)], 2 * 10**9,
+        listed, stats, attended, query_pairs, grad_pairs, grad_turned, corner_left, corner_right,
     )
     pairs = query_pairs, grad_pairs
     add_right = shifted(left_back, 0, -1)
@@ -423,7 +435,8 @@
     wide = ((2, 2) + TILE, F32)
     up_sum, down_sum, left_back, right_back, dq = call(
         edge_kernel, [wide, wide, TWO, TWO, TURNED], 8 * 10**9,
-        listed, finals, *pairs, dq, from_up, from_down, from_left, from_right,
+        listed, finals, *pairs, score_grads, corner_left, corner_right,
+        from_up, from_down, from_left, from_right,
     )
     up_back, down_back = call(
         add_kernel, [TWO, TWO], 10**7, up_sum, down_sum, add_left, add_right

time: 67.7 us -> 67.2 us (level)
  Pallas kernels: 27.9 us -> 29.4 us
  waiting for transfers between devices: 12.2 us -> 11 us
  starting transfers between devices: 24 us -> 23.2 us
    pallas_call x7 -> x8, Pallas kernels: 27.9 us -> 29.4 us  [call(): pl.pallas_call(kernel, out_shape=[jax.ShapeDtypeStruct(shape, kind) for s...]
    ppermute x14, waiting for transfers between devices: 12.2 us -> 11 us  [shifted(): return lax.ppermute(x, ('span', 'chord'), pairs)]
    ppermute x14, starting transfers between devices: 24 us -> 23.2 us  [shifted(): return lax.ppermute(x, ('span', 'chord'), pairs)]
  transfers between devices with their start and end apart: 14 -> 14, of which waited for: 5 -> 5; matrix products, arithmetic and copies ran while one was open for 1% -> 1% of each run, Pallas kernels for 33% -> 36%
where the time goes in v4:
time: 67.2 us; the launch traced here: 67 us
  Pallas kernels  29.4 us (44%)
  starting transfers between devices  23.2 us (35%)
  waiting for transfers between devices  11 us (16%)
  local copies, waits for them, and re-layouts  2.17 us (3%)
  between operations  0.86 us (1%)
    pallas_call x8, Pallas kernels, call(): pl.pallas_call(kernel, out_shape=[jax.ShapeDtypeStruct(shape, kind) for s...  29.4 us
    ppermute x14, starting transfers between devices, shifted(): return lax.ppermute(x, ('span', 'chord'), pairs)  23.2 us
    ppermute x14, waiting for transfers between devices, shifted(): return lax.ppermute(x, ('span', 'chord'), pairs)  11 us
  transfers between devices with their start and end apart: 14, of which 5 were waited for; matrix products, arithmetic and copies ran while one was open for 1% of the time, Pallas kernels for 36%

profile of v4, /device:TPU:0, one launch (start us, length us, event | category | flops | bytes accessed | tf_op | source)
XLA Modules:
  0.0 67.0 jit_solution(2225676687494132808)
XLA Ops:
  0.6 1.3 %fusion.2 = (bf16[1,2,128,512]{3,2,1,0:T(8,128)(2,1)S(1)}, bf16[1,2,128,512]{3,2,1,0:T(8,128)(2,1)S(1)}, bf16[1,2,128,512]{3,2,1,0:T(8,128)(2,1)S(1)}, bf16[1,2,128,512]{3,2,1,0:T(8,128)(2,1)S(1)}) fusion(bf16[2,2,128,512]{3,2,1,0:T(8,128)(2,1)} %param.8, bf16[2,2,128,512]{3,2,1,0:T(8,128)(2,1)} %param.9), kind=kLoop, calls=%fused_computation.16 | loop fusion | bytes 2097152 | tf_op jit(solution)/shard_map/slice | solution.py:397
  1.9 0.1 pad_maximum_fusion.2
  2.0 1.7 %collective-permute-start = (bf16[2,2,128,512]{3,2,1,0:T(8,128)(2,1)S(1)}, bf16[2,2,128,512]{3,2,1,0:T(8,128)(2,1)S(1)}, u32[]{:S(2)}, u32[]{:S(2)}) collective-permute-start(bf16[2,2,128,512]{3,2,1,0:T(8,128)(2,1)S(1)} %pad_maximum_fusion.2), channel_id=1, source_target_pairs={{0,8},{1,9},{2,10},{3,11},{4,12},{5,13},{6,14},{7,15},{8,16},{9,17... | collective-permute-start | bytes 1572872 | tf_op jit(solution)/shard_map/ppermute | solution.py:29
  3.7 0.1 pad_maximum_fusion.3
  3.8 5.0 %collective-permute-start.1 = (bf16[2,2,128,512]{3,2,1,0:T(8,128)(2,1)S(1)}, bf16[2,2,128,512]{3,2,1,0:T(8,128)(2,1)S(1)}, u32[]{:S(2)}, u32[]{:S(2)}) collective-permute-start(bf16[2,2,128,512]{3,2,1,0:T(8,128)(2,1)S(1)} %pad_maximum_fusion.3), channel_id=1, source_target_pairs={{0,120},{1,121},{2,122},{3,123},{4,124},{5,125},{6,126},{7,127},{8... | collective-permute-start | bytes 1572872 | tf_op jit(solution)/shard_map/ppermute | solution.py:29
  8.8 0.1 slice_bitcast_fusion.3
  8.9 0.1 pad_maximum_fusion
  9.0 0.1 pad_maximum_fusion.1
  9.1 2.9 %collective-permute-start.3 = (bf16[3,2,128,512]{3,2,1,0:T(8,128)(2,1)S(1)}, bf16[3,2,128,512]{3,2,1,0:T(8,128)(2,1)S(1)}, u32[]{:S(2)}, u32[]{:S(2)}) collective-permute-start(bf16[3,2,128,512]{3,2,1,0:T(8,128)(2,1)S(1)} %pad_maximum_fusion.1), channel_id=1, source_target_pairs={{0,7},{1,0},{2,1},{3,2},{4,3},{5,4},{6,5},{7,6},{8,15},{9,8},{10,9... | collective-permute-start | bytes 2359304 | tf_op jit(solution)/shard_map/ppermute | solution.py:29
  12.1 0.1 collective-permute-start.4
  12.2 0.7 copy-done.5
  12.9 4.8 %shard_map.94 = (s32[72]{0:T(128)S(1)}, bf16[4,4,256,128]{3,2,1,0:T(8,128)(2,1)S(1)}, f32[4,8,256]{2,1,0:T(8,128)S(1)}, f32[4,4,128,128]{3,2,1,0:T(8,128)S(1)}) custom-call(s32[2,2,8]{2,1,0:T(2,128)S(1)} %copy-done.5, s32[2,2]{1,0:T(2,128)S(1)} %copy-done.6, bf16[4,128,512]{2,1,0:T(8,128)(2,1)S(1)} %bitcast.36, bf16[512,512]{1,0:T(8,128)(2,1)S(1)} %bitcast.32, ...), custom_call_target="tpu_custom_call" | custom-call | flops 6000000000 | bytes 1000000 | tf_op jit(solution)/shard_map/pallas_call | solution.py:376
  17.7 3.6 %collective-permute-done.from_up = bf16[2,2,128,512]{3,2,1,0:T(8,128)(2,1)S(1)} collective-permute-done((bf16[2,2,128,512]{3,2,1,0:T(8,128)(2,1)S(1)}, bf16[2,2,128,512]{3,2,1,0:T(8,128)(2,1)S(1)}, u32[]{:S(2)}, u32[]{:S(2)}) %collective-permute-start) | collective-permute-done | bytes 524320 | tf_op jit(solution)/shard_map/ppermute | solution.py:29
  21.3 2.1 %collective-permute-start.5 = (bf16[2,128,512]{2,1,0:T(8,128)(2,1)S(1)}, bf16[2,128,512]{2,1,0:T(8,128)(2,1)S(1)}, u32[]{:S(2)}, u32[]{:S(2)}) collective-permute-start(bf16[2,128,512]{2,1,0:T(8,128)(2,1)S(1)} %get-tuple-element.38), channel_id=1, source_target_pairs={{0,120},{1,121},{2,122},{3,123},{4,124},{5,125},{6,126},{7,127},{8... | collective-permute-start | bytes 786440 | tf_op jit(solution)/shard_map/ppermute | solution.py:29
  23.5 0.1 pad_maximum_fusion.4
  23.6 0.1 pad_maximum_fusion.5
  23.6 2.9 %collective-permute-start.7 = (bf16[2,2,128,512]{3,2,1,0:T(8,128)(2,1)S(1)}, bf16[2,2,128,512]{3,2,1,0:T(8,128)(2,1)S(1)}, u32[]{:S(2)}, u32[]{:S(2)}) collective-permute-start(bf16[2,2,128,512]{3,2,1,0:T(8,128)(2,1)S(1)} %pad_maximum_fusion.5), channel_id=1, source_target_pairs={{0,7},{1,0},{2,1},{3,2},{4,3},{5,4},{6,5},{7,6},{8,15},{9,8},{10,9... | collective-permute-start | bytes 1572872 | tf_op jit(solution)/shard_map/ppermute | solution.py:29
  26.6 4.5 %shard_map.95 = (f32[4,8,256]{2,1,0:T(8,128)S(1)}, f32[4,4,128,128]{3,2,1,0:T(8,128)S(1)}) custom-call(s32[72]{0:T(128)S(1)} %get-tuple-element.31.listed, bf16[4,4,256,128]{3,2,1,0:T(8,128)(2,1)S(1)} %get-tuple-element.32.query_pairs, f32[4,8,256]{2,1,0:T(8,128)S(1)} %get-tuple-element.33.stats_in, f32[4,4,128,128]{3,2,1,0:T(8,128)S(1)} %get-tuple-element.34.attended_in, ...), custom_call_target="tpu_custom_call" | custom-call | flops 6000000000 | bytes 1000000 | tf_op jit(solution)/shard_map/pallas_call | solution.py:376
  31.2 1.4 %shard_map.96 = (bf16[4,4,256,128]{3,2,1,0:T(8,128)(2,1)S(1)}, bf16[4,4,128,128]{3,2,1,0:T(8,128)(2,1)S(1)}) custom-call(s32[2,2,8]{2,1,0:T(2,128)S(1)} %copy-done.5, f32[4,512]{1,0:T(4,128)S(1)} %copy-done.4, bf16[2,2,128,512]{3,2,1,0:T(8,128)(2,1)S(1)} %copy-done, bf16[2,128,512]{2,1,0:T(8,128)(2,1)S(1)} %collective-permute-done.4.grad_up, ...), custom_call_target="tpu_custom_call" | custom-call | flops 1000000000 | bytes 1000000 | tf_op jit(solution)/shard_map/pallas_call | solution.py:376
  32.5 0.9 %collective-permute-done.6.corner_left = bf16[2,2,128,512]{3,2,1,0:T(8,128)(2,1)S(1)} collective-permute-done((bf16[2,2,128,512]{3,2,1,0:T(8,128)(2,1)S(1)}, bf16[2,2,128,512]{3,2,1,0:T(8,128)(2,1)S(1)}, u32[]{:S(2)}, u32[]{:S(2)}) %collective-permute-start.6) | collective-permute-done | bytes 524320 | tf_op jit(solution)/shard_map/ppermute | solution.py:29
  33.4 3.6 %shard_map.97 = (f32[4,8,256]{2,1,0:T(8,128)S(1)}, bf16[2,2,128,512]{3,2,1,0:T(8,128)(2,1)S(1)}, bf16[2,2,128,512]{3,2,1,0:T(8,128)(2,1)S(1)}, bf16[4,4,128,256]{3,2,1,0:T(8,128)(2,1)S(1)}) custom-call(s32[72]{0:T(128)S(1)} %get-tuple-element.31.listed, f32[4,8,256]{2,1,0:T(8,128)S(1)} %get-tuple-element.35.after.stats_in, ...), custom_call_target="tpu_custom_call" | custom-call | flops 2000000000 | bytes 1000000 | tf_op jit(solution)/shard_map/pallas_call | solution.py:376
  37.0 0.5 collective-permute-start.8
  37.5 2.6 %collective-permute-start.9 = (bf16[2,2,128,512]{3,2,1,0:T(8,128)(2,1)S(1)}, bf16[2,2,128,512]{3,2,1,0:T(8,128)(2,1)S(1)}, u32[]{:S(2)}, u32[]{:S(2)}) collective-permute-start(bf16[2,2,128,512]{3,2,1,0:T(8,128)(2,1)S(1)} %get-tuple-element.52), channel_id=1, source_target_pairs={{0,7},{1,0},{2,1},{3,2},{4,3},{5,4},{6,5},{7,6},{8,15},{9,8},{10,9... | collective-permute-start | bytes 1572872 | tf_op jit(solution)/shard_map/ppermute | solution.py:29
  40.1 6.8 %shard_map.98 = (f32[2,2,128,512]{3,2,1,0:T(8,128)S(1)}, f32[2,2,128,512]{3,2,1,0:T(8,128)S(1)}, bf16[2,2,128,512]{3,2,1,0:T(8,128)(2,1)S(1)}, bf16[2,2,128,512]...) custom-call(s32[72]{0:T(128)S(1)} %get-tuple-element.31.listed, f32[4,8,256]{2,1,0:T(8,128)S(1)} %get-tuple-element.41.finals, ...), custom_call_target="tpu_custom_call" | custom-call | flops 8000000000 | bytes 1000000 | tf_op jit(solution)/shard_map/pallas_call | solution.py:376
  46.8 0.1 collective-permute-done.8.add_left
  46.9 0.2 shard_map.100
  47.1 2.4 %collective-permute-start.13 = (bf16[2,2,128,512]{3,2,1,0:T(8,128)(2,1)S(1)}, bf16[2,2,128,512]{3,2,1,0:T(8,128)(2,1)S(1)}, u32[]{:S(2)}, u32[]{:S(2)}) collective-permute-start(bf16[2,2,128,512]{3,2,1,0:T(8,128)(2,1)S(1)} %get-tuple-element.53), channel_id=1, source_target_pairs={{0,120},{1,121},{2,122},{3,123},{4,124},{5,125},{6,126},{7,127},{8... | collective-permute-start | bytes 1572872 | tf_op jit(solution)/shard_map/ppermute | solution.py:29
  49.5 3.0 %collective-permute-start.11 = (bf16[2,2,128,512]{3,2,1,0:T(8,128)(2,1)S(1)}, bf16[2,2,128,512]{3,2,1,0:T(8,128)(2,1)S(1)}, u32[]{:S(2)}, u32[]{:S(2)}) collective-permute-start(bf16[2,2,128,512]{3,2,1,0:T(8,128)(2,1)S(1)} %get-tuple-element.56), channel_id=1, source_target_pairs={{0,7},{1,0},{2,1},{3,2},{4,3},{5,4},{6,5},{7,6},{8,15},{9,8},{10,9... | collective-permute-start | bytes 1572872 | tf_op jit(solution)/shard_map/ppermute | solution.py:29
  52.4 7.0 %shard_map.99 = (f32[512,512]{1,0:T(8,128)S(1)}, f32[512,512]{1,0:T(8,128)S(1)}, bf16[4,128,512]{2,1,0:T(8,128)(2,1)}) custom-call(s32[72]{0:T(128)S(1)} %get-tuple-element.31.listed, f32[4,8,256]{2,1,0:T(8,128)S(1)} %get-tuple-element.41.finals, bf16[4,4,256,128]{3,2,1,0:T(8,128)(2,1)S(1)} %get-tuple-element.32.query_pairs, ...), custom_call_target="tpu_custom_call" | custom-call | flops 10000000000 | bytes 1000000 | tf_op jit(solution)/shard_map/pallas_call | solution.py:376
  59.4 1.1 %collective-permute-done.13.down = bf16[2,2,128,512]{3,2,1,0:T(8,128)(2,1)S(1)} collective-permute-done((bf16[2,2,128,512]{3,2,1,0:T(8,128)(2,1)S(1)}, bf16[2,2,128,512]{3,2,1,0:T(8,128)(2,1)S(1)}, u32[]{:S(2)}, u32[]{:S(2)}) %collective-permute-start.13) | collective-permute-done | bytes 524320 | tf_op jit(solution)/shard_map/ppermute | solution.py:29
  60.5 5.3 %collective-permute-done.12.up = bf16[2,2,128,512]{3,2,1,0:T(8,128)(2,1)S(1)} collective-permute-done((bf16[2,2,128,512]{3,2,1,0:T(8,128)(2,1)S(1)}, bf16[2,2,128,512]{3,2,1,0:T(8,128)(2,1)S(1)}, u32[]{:S(2)}, u32[]{:S(2)}) %collective-permute-start.12) | collective-permute-done | bytes 524320 | tf_op jit(solution)/shard_map/ppermute | solution.py:29
  65.8 1.2 %shard_map.101 = (bf16[2,2,128,512]{3,2,1,0:T(8,128)(2,1)}, bf16[2,2,128,512]{3,2,1,0:T(8,128)(2,1)}) custom-call(f32[512,512]{1,0:T(8,128)S(1)} %get-tuple-element.45.own_key, f32[512,512]{1,0:T(8,128)S(1)} %get-tuple-element.46.own_value, bf16[2,2,128,512]{3,2,1,0:T(8,128)(2,1)S(1)} %collective-permute-done.10.left, ...), custom_call_target="tpu_custom_call" | custom-call | flops 10000000 | bytes 1000000 | tf_op jit(solution)/shard_map/pallas_call | solution.py:376
  (30 shorter events, 0.2 us)
Async XLA Ops:
  2.0 19.4 %collective-permute-start = (bf16[2,2,128,512]{3,2,1,0:T(8,128)(2,1)S(1)}, bf16[2,2,128,512]{3,2,1,0:T(8,128)(2,1)S(1)}, u32[]{:S(2)}, u32[]{:S(2)}) collective-permute-start(bf16[2,2,128,512]{3,2,1,0:T(8,128)(2,1)S(1)} %pad_maximum_fusion.2), channel_id=1, source_target_pairs={{0,8},{1,9},{2,10},{3,11},{4,12},{5,13},{6,14},{7,15},{8,16},{9,17... | collective-permute-start | bytes 1572872 | tf_op jit(solution)/shard_map/ppermute | solution.py:29
  3.7 5.1 %copy-start.1 = (bf16[2,2,128,512]{3,2,1,0:T(8,128)(2,1)S(1)}, bf16[2,2,128,512]{3,2,1,0:T(8,128)(2,1)}, u32[]{:S(2)}) copy-start(bf16[2,2,128,512]{3,2,1,0:T(8,128)(2,1)} %param.8) | copy-start | bytes 1572868
  3.7 5.1 %copy-start.2 = (bf16[2,2,128,512]{3,2,1,0:T(8,128)(2,1)S(1)}, bf16[2,2,128,512]{3,2,1,0:T(8,128)(2,1)}, u32[]{:S(2)}) copy-start(bf16[2,2,128,512]{3,2,1,0:T(8,128)(2,1)} %param.9) | copy-start | bytes 1572868
  3.7 5.1 %copy-start = (bf16[2,2,128,512]{3,2,1,0:T(8,128)(2,1)S(1)}, bf16[2,2,128,512]{3,2,1,0:T(8,128)(2,1)}, u32[]{:S(2)}) copy-start(bf16[2,2,128,512]{3,2,1,0:T(8,128)(2,1)} %grad.1) | copy-start | bytes 1572868
  3.8 19.7 %collective-permute-start.1 = (bf16[2,2,128,512]{3,2,1,0:T(8,128)(2,1)S(1)}, bf16[2,2,128,512]{3,2,1,0:T(8,128)(2,1)S(1)}, u32[]{:S(2)}, u32[]{:S(2)}) collective-permute-start(bf16[2,2,128,512]{3,2,1,0:T(8,128)(2,1)S(1)} %pad_maximum_fusion.3), channel_id=1, source_target_pairs={{0,120},{1,121},{2,122},{3,123},{4,124},{5,125},{6,126},{7,127},{8... | collective-permute-start | bytes 1572872 | tf_op jit(solution)/shard_map/ppermute | solution.py:29
  9.0 14.6 %collective-permute-start.2 = (bf16[3,2,128,512]{3,2,1,0:T(8,128)(2,1)S(1)}, bf16[3,2,128,512]{3,2,1,0:T(8,128)(2,1)S(1)}, u32[]{:S(2)}, u32[]{:S(2)}) collective-permute-start(bf16[3,2,128,512]{3,2,1,0:T(8,128)(2,1)S(1)} %pad_maximum_fusion), channel_id=1, source_target_pairs={{0,1},{1,2},{2,3},{3,4},{4,5},{5,6},{6,7},{7,0},{8,9},{9,10},{10,1... | collective-permute-start | bytes 2359304 | tf_op jit(solution)/shard_map/ppermute | solution.py:29
  9.1 3.1 %copy-start.3 = (bf16[2,2,128,512]{3,2,1,0:T(8,128)(2,1)S(1)}, bf16[2,2,128,512]{3,2,1,0:T(8,128)(2,1)}, u32[]{:S(2)}) copy-start(bf16[2,2,128,512]{3,2,1,0:T(8,128)(2,1)} %param.7) | copy-start | bytes 1572868
  9.1 17.5 %collective-permute-start.3 = (bf16[3,2,128,512]{3,2,1,0:T(8,128)(2,1)S(1)}, bf16[3,2,128,512]{3,2,1,0:T(8,128)(2,1)S(1)}, u32[]{:S(2)}, u32[]{:S(2)}) collective-permute-start(bf16[3,2,128,512]{3,2,1,0:T(8,128)(2,1)S(1)} %pad_maximum_fusion.1), channel_id=1, source_target_pairs={{0,7},{1,0},{2,1},{3,2},{4,3},{5,4},{6,5},{7,6},{8,15},{9,8},{10,9... | collective-permute-start | bytes 2359304 | tf_op jit(solution)/shard_map/ppermute | solution.py:29
  12.1 19.0 %collective-permute-start.4 = (bf16[2,128,512]{2,1,0:T(8,128)(2,1)S(1)}, bf16[2,128,512]{2,1,0:T(8,128)(2,1)S(1)}, u32[]{:S(2)}, u32[]{:S(2)}) collective-permute-start(bf16[2,128,512]{2,1,0:T(8,128)(2,1)S(1)} %get-tuple-element.37), channel_id=1, source_target_pairs={{0,8},{1,9},{2,10},{3,11},{4,12},{5,13},{6,14},{7,15},{8,16},{9,17... | collective-permute-start | bytes 786440 | tf_op jit(solution)/shard_map/ppermute | solution.py:29
  12.2 0.7 %copy-start.5 = (s32[2,2,8]{2,1,0:T(2,128)S(1)}, s32[2,2,8]{2,1,0:T(2,128)}, u32[]{:S(2)}) copy-start(s32[2,2,8]{2,1,0:T(2,128)} %partners.3) | copy-start | bytes 388
  12.2 0.7 %copy-start.6 = (s32[2,2]{1,0:T(2,128)S(1)}, s32[2,2]{1,0:T(2,128)}, u32[]{:S(2)}) copy-start(s32[2,2]{1,0:T(2,128)} %counts.1) | copy-start | bytes 52
  21.3 9.8 %collective-permute-start.5 = (bf16[2,128,512]{2,1,0:T(8,128)(2,1)S(1)}, bf16[2,128,512]{2,1,0:T(8,128)(2,1)S(1)}, u32[]{:S(2)}, u32[]{:S(2)}) collective-permute-start(bf16[2,128,512]{2,1,0:T(8,128)(2,1)S(1)} %get-tuple-element.38), channel_id=1, source_target_pairs={{0,120},{1,121},{2,122},{3,123},{4,124},{5,125},{6,126},{7,127},{8... | collective-permute-start | bytes 786440 | tf_op jit(solution)/shard_map/ppermute | solution.py:29
  23.6 9.8 %collective-permute-start.6 = (bf16[2,2,128,512]{3,2,1,0:T(8,128)(2,1)S(1)}, bf16[2,2,128,512]{3,2,1,0:T(8,128)(2,1)S(1)}, u32[]{:S(2)}, u32[]{:S(2)}) collective-permute-start(bf16[2,2,128,512]{3,2,1,0:T(8,128)(2,1)S(1)} %pad_maximum_fusion.4), channel_id=1, source_target_pairs={{0,1},{1,2},{2,3},{3,4},{4,5},{5,6},{6,7},{7,0},{8,9},{9,10},{10,1... | collective-permute-start | bytes 1572872 | tf_op jit(solution)/shard_map/ppermute | solution.py:29
  23.6 9.7 %collective-permute-start.7 = (bf16[2,2,128,512]{3,2,1,0:T(8,128)(2,1)S(1)}, bf16[2,2,128,512]{3,2,1,0:T(8,128)(2,1)S(1)}, u32[]{:S(2)}, u32[]{:S(2)}) collective-permute-start(bf16[2,2,128,512]{3,2,1,0:T(8,128)(2,1)S(1)} %pad_maximum_fusion.5), channel_id=1, source_target_pairs={{0,7},{1,0},{2,1},{3,2},{4,3},{5,4},{6,5},{7,6},{8,15},{9,8},{10,9... | collective-permute-start | bytes 1572872 | tf_op jit(solution)/shard_map/ppermute | solution.py:29
  26.6 4.5 %copy-start.4 = (f32[4,512]{1,0:T(4,128)S(1)}, f32[4,512]{1,0:T(4,128)}, u32[]{:S(2)}) copy-start(f32[4,512]{1,0:T(4,128)} %gain.1) | copy-start | bytes 24580
  37.0 9.9 %collective-permute-start.8 = (bf16[2,2,128,512]{3,2,1,0:T(8,128)(2,1)S(1)}, bf16[2,2,128,512]{3,2,1,0:T(8,128)(2,1)S(1)}, u32[]{:S(2)}, u32[]{:S(2)}) collective-permute-start(bf16[2,2,128,512]{3,2,1,0:T(8,128)(2,1)S(1)} %get-tuple-element.51), channel_id=1, source_target_pairs={{0,1},{1,2},{2,3},{3,4},{4,5},{5,6},{6,7},{7,0},{8,9},{9,10},{10,1... | collective-permute-start | bytes 1572872 | tf_op jit(solution)/shard_map/ppermute | solution.py:29
  37.5 9.4 %collective-permute-start.9 = (bf16[2,2,128,512]{3,2,1,0:T(8,128)(2,1)S(1)}, bf16[2,2,128,512]{3,2,1,0:T(8,128)(2,1)S(1)}, u32[]{:S(2)}, u32[]{:S(2)}) collective-permute-start(bf16[2,2,128,512]{3,2,1,0:T(8,128)(2,1)S(1)} %get-tuple-element.52), channel_id=1, source_target_pairs={{0,7},{1,0},{2,1},{3,2},{4,3},{5,4},{6,5},{7,6},{8,15},{9,8},{10,9... | collective-permute-start | bytes 1572872 | tf_op jit(solution)/shard_map/ppermute | solution.py:29
  47.1 13.4 %collective-permute-start.13 = (bf16[2,2,128,512]{3,2,1,0:T(8,128)(2,1)S(1)}, bf16[2,2,128,512]{3,2,1,0:T(8,128)(2,1)S(1)}, u32[]{:S(2)}, u32[]{:S(2)}) collective-permute-start(bf16[2,2,128,512]{3,2,1,0:T(8,128)(2,1)S(1)} %get-tuple-element.53), channel_id=1, source_target_pairs={{0,120},{1,121},{2,122},{3,123},{4,124},{5,125},{6,126},{7,127},{8... | collective-permute-start | bytes 1572872 | tf_op jit(solution)/shard_map/ppermute | solution.py:29
  49.5 16.4 %collective-permute-start.12 = (bf16[2,2,128,512]{3,2,1,0:T(8,128)(2,1)S(1)}, bf16[2,2,128,512]{3,2,1,0:T(8,128)(2,1)S(1)}, u32[]{:S(2)}, u32[]{:S(2)}) collective-permute-start(bf16[2,2,128,512]{3,2,1,0:T(8,128)(2,1)S(1)} %get-tuple-element.54), channel_id=1, source_target_pairs={{0,8},{1,9},{2,10},{3,11},{4,12},{5,13},{6,14},{7,15},{8,16},{9,17... | collective-permute-start | bytes 1572872 | tf_op jit(solution)/shard_map/ppermute | solution.py:29
  49.5 9.9 %collective-permute-start.10 = (bf16[2,2,128,512]{3,2,1,0:T(8,128)(2,1)S(1)}, bf16[2,2,128,512]{3,2,1,0:T(8,128)(2,1)S(1)}, u32[]{:S(2)}, u32[]{:S(2)}) collective-permute-start(bf16[2,2,128,512]{3,2,1,0:T(8,128)(2,1)S(1)} %get-tuple-element.55), channel_id=1, source_target_pairs={{0,1},{1,2},{2,3},{3,4},{4,5},{5,6},{6,7},{7,0},{8,9},{9,10},{10,1... | collective-permute-start | bytes 1572872 | tf_op jit(solution)/shard_map/ppermute | solution.py:29
  49.5 9.9 %collective-permute-start.11 = (bf16[2,2,128,512]{3,2,1,0:T(8,128)(2,1)S(1)}, bf16[2,2,128,512]{3,2,1,0:T(8,128)(2,1)S(1)}, u32[]{:S(2)}, u32[]{:S(2)}) collective-permute-start(bf16[2,2,128,512]{3,2,1,0:T(8,128)(2,1)S(1)} %get-tuple-element.56), channel_id=1, source_target_pairs={{0,7},{1,0},{2,1},{3,2},{4,3},{5,4},{6,5},{7,6},{8,15},{9,8},{10,9... | collective-permute-start | bytes 1572872 | tf_op jit(solution)/shard_map/ppermute | solution.py:29

commit v5 on v4

--- a/solution.py
+++ b/solution.py
@@ -405,8 +405,9 @@
     def corners(c):
         return jnp.stack([from_up[:, c], from_down[:, c]], axis=1)
 
-    corner_left = shifted(corners(1), 0, 1)
-    corner_right = shifted(corners(0), 0, -1)
+    left_corners, right_corners = corners(0), corners(1)
+    corner_left = shifted(right_corners, 0, 1)
+    corner_right = shifted(left_corners, 0, -1)
 
     key_rows, value_rows = key_tiles.reshape(4 * PATCH, D), value_tiles.reshape(4 * PATCH, D)
     listed, query_pairs, stats, attended = call(
@@ -414,7 +415,8 @@
         [((72,), jnp.int32), PAIR_SHAPE, STATS, TURNED], 6 * 10**9,
         partners, counts, query_tiles.reshape((4,) + TILE), key_rows, value_rows,
     )
-    upper, lower, *_ = lax.optimization_barrier((out_grad[0], out_grad[1], for_left, for_right))
+    lower, *_ = lax.optimization_barrier((out_grad[1], for_left, for_right))
+    upper, *_ = lax.optimization_barrier((out_grad[0], left_corners, right_corners))
     grad_up, grad_down = shifted(lower, 1, 0), shifted(upper, -1, 0)
     stats, attended = call(
         edge_totals_kernel, [STATS, TURNED], 6 * 10**9,

time: 67.2 us -> 72.5 us (1.079)
  starting transfers between devices: 23.2 us -> 27.4 us
  waiting for transfers between devices: 11 us -> 12.2 us
    ppermute x14, starting transfers between devices: 23.2 us -> 27.4 us  [shifted(): return lax.ppermute(x, ('span', 'chord'), pairs)]
    ppermute x14, waiting for transfers between devices: 11 us -> 12.2 us  [shifted(): return lax.ppermute(x, ('span', 'chord'), pairs)]
  transfers between devices with their start and end apart: 14 -> 14, of which waited for: 5 -> 5; matrix products, arithmetic and copies ran while one was open for 1% -> 1% of each run, Pallas kernels for 36% -> 34%
where the time goes in v5:
time: 72.5 us; the launch traced here: 72.4 us
  Pallas kernels  29.4 us (41%)
  starting transfers between devices  27.4 us (38%)
  waiting for transfers between devices  12.2 us (17%)
  local copies, waits for them, and re-layouts  2.17 us (3%)
  between operations  0.87 us (1%)
    pallas_call x8, Pallas kernels, call(): pl.pallas_call(kernel, out_shape=[jax.ShapeDtypeStruct(shape, kind) for s...  29.4 us
    ppermute x14, starting transfers between devices, shifted(): return lax.ppermute(x, ('span', 'chord'), pairs)  27.4 us
    ppermute x14, waiting for transfers between devices, shifted(): return lax.ppermute(x, ('span', 'chord'), pairs)  12.2 us
  transfers between devices with their start and end apart: 14, of which 5 were waited for; matrix products, arithmetic and copies ran while one was open for 1% of the time, Pallas kernels for 34%

profile of v5, /device:TPU:0, one launch (start us, length us, event | category | flops | bytes accessed | tf_op | source)
XLA Modules:
  0.0 72.4 jit_solution(16587503738916914542)
XLA Ops:
  0.6 1.3 %fusion.2 = (bf16[1,2,128,512]{3,2,1,0:T(8,128)(2,1)S(1)}, bf16[1,2,128,512]{3,2,1,0:T(8,128)(2,1)S(1)}, bf16[1,2,128,512]{3,2,1,0:T(8,128)(2,1)S(1)}, bf16[1,2,128,512]{3,2,1,0:T(8,128)(2,1)S(1)}) fusion(bf16[2,2,128,512]{3,2,1,0:T(8,128)(2,1)} %param.8, bf16[2,2,128,512]{3,2,1,0:T(8,128)(2,1)} %param.9), kind=kLoop, calls=%fused_computation.16 | loop fusion | bytes 2097152 | tf_op jit(solution)/shard_map/slice | solution.py:397
  1.9 0.1 pad_maximum_fusion.2
  2.0 1.7 %collective-permute-start = (bf16[2,2,128,512]{3,2,1,0:T(8,128)(2,1)S(1)}, bf16[2,2,128,512]{3,2,1,0:T(8,128)(2,1)S(1)}, u32[]{:S(2)}, u32[]{:S(2)}) collective-permute-start(bf16[2,2,128,512]{3,2,1,0:T(8,128)(2,1)S(1)} %pad_maximum_fusion.2), channel_id=1, source_target_pairs={{0,8},{1,9},{2,10},{3,11},{4,12},{5,13},{6,14},{7,15},{8,16},{9,17... | collective-permute-start | bytes 1572872 | tf_op jit(solution)/shard_map/ppermute | solution.py:29
  3.7 0.1 pad_maximum_fusion.3
  3.8 5.0 %collective-permute-start.1 = (bf16[2,2,128,512]{3,2,1,0:T(8,128)(2,1)S(1)}, bf16[2,2,128,512]{3,2,1,0:T(8,128)(2,1)S(1)}, u32[]{:S(2)}, u32[]{:S(2)}) collective-permute-start(bf16[2,2,128,512]{3,2,1,0:T(8,128)(2,1)S(1)} %pad_maximum_fusion.3), channel_id=1, source_target_pairs={{0,120},{1,121},{2,122},{3,123},{4,124},{5,125},{6,126},{7,127},{8... | collective-permute-start | bytes 1572872 | tf_op jit(solution)/shard_map/ppermute | solution.py:29
  8.8 0.1 slice_bitcast_fusion.3
  8.9 0.1 pad_maximum_fusion
  9.0 0.0 collective-permute-start.2
  9.0 0.1 pad_maximum_fusion.1
  9.1 2.9 %collective-permute-start.3 = (bf16[3,2,128,512]{3,2,1,0:T(8,128)(2,1)S(1)}, bf16[3,2,128,512]{3,2,1,0:T(8,128)(2,1)S(1)}, u32[]{:S(2)}, u32[]{:S(2)}) collective-permute-start(bf16[3,2,128,512]{3,2,1,0:T(8,128)(2,1)S(1)} %pad_maximum_fusion.1), channel_id=1, source_target_pairs={{0,7},{1,0},{2,1},{3,2},{4,3},{5,4},{6,5},{7,6},{8,15},{9,8},{10,9... | collective-permute-start | bytes 2359304 | tf_op jit(solution)/shard_map/ppermute | solution.py:29
  12.1 0.1 collective-permute-start.4
  12.2 0.7 copy-done.5
  12.9 4.8 %shard_map.94 = (s32[72]{0:T(128)S(1)}, bf16[4,4,256,128]{3,2,1,0:T(8,128)(2,1)S(1)}, f32[4,8,256]{2,1,0:T(8,128)S(1)}, f32[4,4,128,128]{3,2,1,0:T(8,128)S(1)}) custom-call(s32[2,2,8]{2,1,0:T(2,128)S(1)} %copy-done.5, s32[2,2]{1,0:T(2,128)S(1)} %copy-done.6, bf16[4,128,512]{2,1,0:T(8,128)(2,1)S(1)} %bitcast.36, bf16[512,512]{1,0:T(8,128)(2,1)S(1)} %bitcast.32, ...), custom_call_target="tpu_custom_call" | custom-call | flops 6000000000 | bytes 1000000 | tf_op jit(solution)/shard_map/pallas_call | solution.py:376
  17.7 3.6 %collective-permute-done.from_up = bf16[2,2,128,512]{3,2,1,0:T(8,128)(2,1)S(1)} collective-permute-done((bf16[2,2,128,512]{3,2,1,0:T(8,128)(2,1)S(1)}, bf16[2,2,128,512]{3,2,1,0:T(8,128)(2,1)S(1)}, u32[]{:S(2)}, u32[]{:S(2)}) %collective-permute-start) | collective-permute-done | bytes 524320 | tf_op jit(solution)/shard_map/ppermute | solution.py:29
  21.4 0.1 pad_maximum_fusion.4
  21.5 0.8 %collective-permute-start.7 = (bf16[2,2,128,512]{3,2,1,0:T(8,128)(2,1)S(1)}, bf16[2,2,128,512]{3,2,1,0:T(8,128)(2,1)S(1)}, u32[]{:S(2)}, u32[]{:S(2)}) collective-permute-start(bf16[2,2,128,512]{3,2,1,0:T(8,128)(2,1)S(1)} %pad_maximum_fusion.4), channel_id=1, source_target_pairs={{0,7},{1,0},{2,1},{3,2},{4,3},{5,4},{6,5},{7,6},{8,15},{9,8},{10,9... | collective-permute-start | bytes 1572872 | tf_op jit(solution)/shard_map/ppermute | solution.py:29
  22.3 0.1 pad_maximum_fusion.5
  22.4 4.9 %collective-permute-start.5 = (bf16[2,128,512]{2,1,0:T(8,128)(2,1)S(1)}, bf16[2,128,512]{2,1,0:T(8,128)(2,1)S(1)}, u32[]{:S(2)}, u32[]{:S(2)}) collective-permute-start(bf16[2,128,512]{2,1,0:T(8,128)(2,1)S(1)} %get-tuple-element.38), channel_id=1, source_target_pairs={{0,120},{1,121},{2,122},{3,123},{4,124},{5,125},{6,126},{7,127},{8... | collective-permute-start | bytes 786440 | tf_op jit(solution)/shard_map/ppermute | solution.py:29
  27.4 4.5 %shard_map.95 = (f32[4,8,256]{2,1,0:T(8,128)S(1)}, f32[4,4,128,128]{3,2,1,0:T(8,128)S(1)}) custom-call(s32[72]{0:T(128)S(1)} %get-tuple-element.31.listed, bf16[4,4,256,128]{3,2,1,0:T(8,128)(2,1)S(1)} %get-tuple-element.32.query_pairs, f32[4,8,256]{2,1,0:T(8,128)S(1)} %get-tuple-element.33.stats_in, f32[4,4,128,128]{3,2,1,0:T(8,128)S(1)} %get-tuple-element.34.attended_in, ...), custom_call_target="tpu_custom_call" | custom-call | flops 6000000000 | bytes 1000000 | tf_op jit(solution)/shard_map/pallas_call | solution.py:376
  31.9 1.4 %collective-permute-done.5.grad_down = bf16[2,128,512]{2,1,0:T(8,128)(2,1)S(1)} collective-permute-done((bf16[2,128,512]{2,1,0:T(8,128)(2,1)S(1)}, bf16[2,128,512]{2,1,0:T(8,128)(2,1)S(1)}, u32[]{:S(2)}, u32[]{:S(2)}) %collective-permute-start.5) | collective-permute-done | bytes 262176 | tf_op jit(solution)/shard_map/ppermute | solution.py:29
  33.3 1.4 %shard_map.96 = (bf16[4,4,256,128]{3,2,1,0:T(8,128)(2,1)S(1)}, bf16[4,4,128,128]{3,2,1,0:T(8,128)(2,1)S(1)}) custom-call(s32[2,2,8]{2,1,0:T(2,128)S(1)} %copy-done.5, f32[4,512]{1,0:T(4,128)S(1)} %copy-done.4, bf16[2,2,128,512]{3,2,1,0:T(8,128)(2,1)S(1)} %copy-done, bf16[2,128,512]{2,1,0:T(8,128)(2,1)S(1)} %collective-permute-done.4.grad_up, ...), custom_call_target="tpu_custom_call" | custom-call | flops 1000000000 | bytes 1000000 | tf_op jit(solution)/shard_map/pallas_call | solution.py:376
  34.7 3.6 %shard_map.97 = (f32[4,8,256]{2,1,0:T(8,128)S(1)}, bf16[2,2,128,512]{3,2,1,0:T(8,128)(2,1)S(1)}, bf16[2,2,128,512]{3,2,1,0:T(8,128)(2,1)S(1)}, bf16[4,4,128,256]{3,2,1,0:T(8,128)(2,1)S(1)}) custom-call(s32[72]{0:T(128)S(1)} %get-tuple-element.31.listed, f32[4,8,256]{2,1,0:T(8,128)S(1)} %get-tuple-element.35.after.stats_in, ...), custom_call_target="tpu_custom_call" | custom-call | flops 2000000000 | bytes 1000000 | tf_op jit(solution)/shard_map/pallas_call | solution.py:376
  38.3 2.9 %collective-permute-start.9 = (bf16[2,2,128,512]{3,2,1,0:T(8,128)(2,1)S(1)}, bf16[2,2,128,512]{3,2,1,0:T(8,128)(2,1)S(1)}, u32[]{:S(2)}, u32[]{:S(2)}) collective-permute-start(bf16[2,2,128,512]{3,2,1,0:T(8,128)(2,1)S(1)} %get-tuple-element.52), channel_id=1, source_target_pairs={{0,7},{1,0},{2,1},{3,2},{4,3},{5,4},{6,5},{7,6},{8,15},{9,8},{10,9... | collective-permute-start | bytes 1572872 | tf_op jit(solution)/shard_map/ppermute | solution.py:29
  41.3 6.8 %shard_map.98 = (f32[2,2,128,512]{3,2,1,0:T(8,128)S(1)}, f32[2,2,128,512]{3,2,1,0:T(8,128)S(1)}, bf16[2,2,128,512]{3,2,1,0:T(8,128)(2,1)S(1)}, bf16[2,2,128,512]...) custom-call(s32[72]{0:T(128)S(1)} %get-tuple-element.31.listed, f32[4,8,256]{2,1,0:T(8,128)S(1)} %get-tuple-element.41.finals, ...), custom_call_target="tpu_custom_call" | custom-call | flops 8000000000 | bytes 1000000 | tf_op jit(solution)/shard_map/pallas_call | solution.py:376
  48.0 0.1 collective-permute-done.8.add_left
  48.1 0.2 shard_map.100
  48.3 5.9 %collective-permute-start.13 = (bf16[2,2,128,512]{3,2,1,0:T(8,128)(2,1)S(1)}, bf16[2,2,128,512]{3,2,1,0:T(8,128)(2,1)S(1)}, u32[]{:S(2)}, u32[]{:S(2)}) collective-permute-start(bf16[2,2,128,512]{3,2,1,0:T(8,128)(2,1)S(1)} %get-tuple-element.53), channel_id=1, source_target_pairs={{0,120},{1,121},{2,122},{3,123},{4,124},{5,125},{6,126},{7,127},{8... | collective-permute-start | bytes 1572872 | tf_op jit(solution)/shard_map/ppermute | solution.py:29
  54.2 3.0 %collective-permute-start.11 = (bf16[2,2,128,512]{3,2,1,0:T(8,128)(2,1)S(1)}, bf16[2,2,128,512]{3,2,1,0:T(8,128)(2,1)S(1)}, u32[]{:S(2)}, u32[]{:S(2)}) collective-permute-start(bf16[2,2,128,512]{3,2,1,0:T(8,128)(2,1)S(1)} %get-tuple-element.56), channel_id=1, source_target_pairs={{0,7},{1,0},{2,1},{3,2},{4,3},{5,4},{6,5},{7,6},{8,15},{9,8},{10,9... | collective-permute-start | bytes 1572872 | tf_op jit(solution)/shard_map/ppermute | solution.py:29
  57.1 7.0 %shard_map.99 = (f32[512,512]{1,0:T(8,128)S(1)}, f32[512,512]{1,0:T(8,128)S(1)}, bf16[4,128,512]{2,1,0:T(8,128)(2,1)}) custom-call(s32[72]{0:T(128)S(1)} %get-tuple-element.31.listed, f32[4,8,256]{2,1,0:T(8,128)S(1)} %get-tuple-element.41.finals, bf16[4,4,256,128]{3,2,1,0:T(8,128)(2,1)S(1)} %get-tuple-element.32.query_pairs, ...), custom_call_target="tpu_custom_call" | custom-call | flops 10000000000 | bytes 1000000 | tf_op jit(solution)/shard_map/pallas_call | solution.py:376
  64.1 1.5 %collective-permute-done.13.down = bf16[2,2,128,512]{3,2,1,0:T(8,128)(2,1)S(1)} collective-permute-done((bf16[2,2,128,512]{3,2,1,0:T(8,128)(2,1)S(1)}, bf16[2,2,128,512]{3,2,1,0:T(8,128)(2,1)S(1)}, u32[]{:S(2)}, u32[]{:S(2)}) %collective-permute-start.13) | collective-permute-done | bytes 524320 | tf_op jit(solution)/shard_map/ppermute | solution.py:29
  65.6 5.5 %collective-permute-done.12.up = bf16[2,2,128,512]{3,2,1,0:T(8,128)(2,1)S(1)} collective-permute-done((bf16[2,2,128,512]{3,2,1,0:T(8,128)(2,1)S(1)}, bf16[2,2,128,512]{3,2,1,0:T(8,128)(2,1)S(1)}, u32[]{:S(2)}, u32[]{:S(2)}) %collective-permute-start.12) | collective-permute-done | bytes 524320 | tf_op jit(solution)/shard_map/ppermute | solution.py:29
  71.2 1.2 %shard_map.101 = (bf16[2,2,128,512]{3,2,1,0:T(8,128)(2,1)}, bf16[2,2,128,512]{3,2,1,0:T(8,128)(2,1)}) custom-call(f32[512,512]{1,0:T(8,128)S(1)} %get-tuple-element.45.own_key, f32[512,512]{1,0:T(8,128)S(1)} %get-tuple-element.46.own_value, bf16[2,2,128,512]{3,2,1,0:T(8,128)(2,1)S(1)} %collective-permute-done.10.left, ...), custom_call_target="tpu_custom_call" | custom-call | flops 10000000 | bytes 1000000 | tf_op jit(solution)/shard_map/pallas_call | solution.py:376
  (30 shorter events, 0.2 us)
Async XLA Ops:
  2.0 19.4 %collective-permute-start = (bf16[2,2,128,512]{3,2,1,0:T(8,128)(2,1)S(1)}, bf16[2,2,128,512]{3,2,1,0:T(8,128)(2,1)S(1)}, u32[]{:S(2)}, u32[]{:S(2)}) collective-permute-start(bf16[2,2,128,512]{3,2,1,0:T(8,128)(2,1)S(1)} %pad_maximum_fusion.2), channel_id=1, source_target_pairs={{0,8},{1,9},{2,10},{3,11},{4,12},{5,13},{6,14},{7,15},{8,16},{9,17... | collective-permute-start | bytes 1572872 | tf_op jit(solution)/shard_map/ppermute | solution.py:29
  3.7 5.1 %copy-start.1 = (bf16[2,2,128,512]{3,2,1,0:T(8,128)(2,1)S(1)}, bf16[2,2,128,512]{3,2,1,0:T(8,128)(2,1)}, u32[]{:S(2)}) copy-start(bf16[2,2,128,512]{3,2,1,0:T(8,128)(2,1)} %param.8) | copy-start | bytes 1572868
  3.7 5.1 %copy-start.2 = (bf16[2,2,128,512]{3,2,1,0:T(8,128)(2,1)S(1)}, bf16[2,2,128,512]{3,2,1,0:T(8,128)(2,1)}, u32[]{:S(2)}) copy-start(bf16[2,2,128,512]{3,2,1,0:T(8,128)(2,1)} %param.9) | copy-start | bytes 1572868
  3.7 5.1 %copy-start = (bf16[2,2,128,512]{3,2,1,0:T(8,128)(2,1)S(1)}, bf16[2,2,128,512]{3,2,1,0:T(8,128)(2,1)}, u32[]{:S(2)}) copy-start(bf16[2,2,128,512]{3,2,1,0:T(8,128)(2,1)} %grad.1) | copy-start | bytes 1572868
  3.8 17.6 %collective-permute-start.1 = (bf16[2,2,128,512]{3,2,1,0:T(8,128)(2,1)S(1)}, bf16[2,2,128,512]{3,2,1,0:T(8,128)(2,1)S(1)}, u32[]{:S(2)}, u32[]{:S(2)}) collective-permute-start(bf16[2,2,128,512]{3,2,1,0:T(8,128)(2,1)S(1)} %pad_maximum_fusion.3), channel_id=1, source_target_pairs={{0,120},{1,121},{2,122},{3,123},{4,124},{5,125},{6,126},{7,127},{8... | collective-permute-start | bytes 1572872 | tf_op jit(solution)/shard_map/ppermute | solution.py:29
  9.0 13.4 %collective-permute-start.2 = (bf16[3,2,128,512]{3,2,1,0:T(8,128)(2,1)S(1)}, bf16[3,2,128,512]{3,2,1,0:T(8,128)(2,1)S(1)}, u32[]{:S(2)}, u32[]{:S(2)}) collective-permute-start(bf16[3,2,128,512]{3,2,1,0:T(8,128)(2,1)S(1)} %pad_maximum_fusion), channel_id=1, source_target_pairs={{0,1},{1,2},{2,3},{3,4},{4,5},{5,6},{6,7},{7,0},{8,9},{9,10},{10,1... | collective-permute-start | bytes 2359304 | tf_op jit(solution)/shard_map/ppermute | solution.py:29
  9.1 3.1 %copy-start.3 = (bf16[2,2,128,512]{3,2,1,0:T(8,128)(2,1)S(1)}, bf16[2,2,128,512]{3,2,1,0:T(8,128)(2,1)}, u32[]{:S(2)}) copy-start(bf16[2,2,128,512]{3,2,1,0:T(8,128)(2,1)} %param.7) | copy-start | bytes 1572868
  9.1 18.2 %collective-permute-start.3 = (bf16[3,2,128,512]{3,2,1,0:T(8,128)(2,1)S(1)}, bf16[3,2,128,512]{3,2,1,0:T(8,128)(2,1)S(1)}, u32[]{:S(2)}, u32[]{:S(2)}) collective-permute-start(bf16[3,2,128,512]{3,2,1,0:T(8,128)(2,1)S(1)} %pad_maximum_fusion.1), channel_id=1, source_target_pairs={{0,7},{1,0},{2,1},{3,2},{4,3},{5,4},{6,5},{7,6},{8,15},{9,8},{10,9... | collective-permute-start | bytes 2359304 | tf_op jit(solution)/shard_map/ppermute | solution.py:29
  12.1 19.8 %collective-permute-start.4 = (bf16[2,128,512]{2,1,0:T(8,128)(2,1)S(1)}, bf16[2,128,512]{2,1,0:T(8,128)(2,1)S(1)}, u32[]{:S(2)}, u32[]{:S(2)}) collective-permute-start(bf16[2,128,512]{2,1,0:T(8,128)(2,1)S(1)} %get-tuple-element.37), channel_id=1, source_target_pairs={{0,8},{1,9},{2,10},{3,11},{4,12},{5,13},{6,14},{7,15},{8,16},{9,17... | collective-permute-start | bytes 786440 | tf_op jit(solution)/shard_map/ppermute | solution.py:29
  12.2 0.7 copy-start.5
  12.2 0.7 copy-start.6
  21.5 13.1 %collective-permute-start.7 = (bf16[2,2,128,512]{3,2,1,0:T(8,128)(2,1)S(1)}, bf16[2,2,128,512]{3,2,1,0:T(8,128)(2,1)S(1)}, u32[]{:S(2)}, u32[]{:S(2)}) collective-permute-start(bf16[2,2,128,512]{3,2,1,0:T(8,128)(2,1)S(1)} %pad_maximum_fusion.4), channel_id=1, source_target_pairs={{0,7},{1,0},{2,1},{3,2},{4,3},{5,4},{6,5},{7,6},{8,15},{9,8},{10,9... | collective-permute-start | bytes 1572872 | tf_op jit(solution)/shard_map/ppermute | solution.py:29
  22.4 12.3 %collective-permute-start.6 = (bf16[2,2,128,512]{3,2,1,0:T(8,128)(2,1)S(1)}, bf16[2,2,128,512]{3,2,1,0:T(8,128)(2,1)S(1)}, u32[]{:S(2)}, u32[]{:S(2)}) collective-permute-start(bf16[2,2,128,512]{3,2,1,0:T(8,128)(2,1)S(1)} %pad_maximum_fusion.5), channel_id=1, source_target_pairs={{0,1},{1,2},{2,3},{3,4},{4,5},{5,6},{6,7},{7,0},{8,9},{9,10},{10,1... | collective-permute-start | bytes 1572872 | tf_op jit(solution)/shard_map/ppermute | solution.py:29
  22.4 10.9 %collective-permute-start.5 = (bf16[2,128,512]{2,1,0:T(8,128)(2,1)S(1)}, bf16[2,128,512]{2,1,0:T(8,128)(2,1)S(1)}, u32[]{:S(2)}, u32[]{:S(2)}) collective-permute-start(bf16[2,128,512]{2,1,0:T(8,128)(2,1)S(1)} %get-tuple-element.38), channel_id=1, source_target_pairs={{0,120},{1,121},{2,122},{3,123},{4,124},{5,125},{6,126},{7,127},{8... | collective-permute-start | bytes 786440 | tf_op jit(solution)/shard_map/ppermute | solution.py:29
  27.3 5.9 %copy-start.4 = (f32[4,512]{1,0:T(4,128)S(1)}, f32[4,512]{1,0:T(4,128)}, u32[]{:S(2)}) copy-start(f32[4,512]{1,0:T(4,128)} %gain.1) | copy-start | bytes 24580
  38.3 9.8 %collective-permute-start.8 = (bf16[2,2,128,512]{3,2,1,0:T(8,128)(2,1)S(1)}, bf16[2,2,128,512]{3,2,1,0:T(8,128)(2,1)S(1)}, u32[]{:S(2)}, u32[]{:S(2)}) collective-permute-start(bf16[2,2,128,512]{3,2,1,0:T(8,128)(2,1)S(1)} %get-tuple-element.51), channel_id=1, source_target_pairs={{0,1},{1,2},{2,3},{3,4},{4,5},{5,6},{6,7},{7,0},{8,9},{9,10},{10,1... | collective-permute-start | bytes 1572872 | tf_op jit(solution)/shard_map/ppermute | solution.py:29
  38.3 9.8 %collective-permute-start.9 = (bf16[2,2,128,512]{3,2,1,0:T(8,128)(2,1)S(1)}, bf16[2,2,128,512]{3,2,1,0:T(8,128)(2,1)S(1)}, u32[]{:S(2)}, u32[]{:S(2)}) collective-permute-start(bf16[2,2,128,512]{3,2,1,0:T(8,128)(2,1)S(1)} %get-tuple-element.52), channel_id=1, source_target_pairs={{0,7},{1,0},{2,1},{3,2},{4,3},{5,4},{6,5},{7,6},{8,15},{9,8},{10,9... | collective-permute-start | bytes 1572872 | tf_op jit(solution)/shard_map/ppermute | solution.py:29
  48.3 17.3 %collective-permute-start.13 = (bf16[2,2,128,512]{3,2,1,0:T(8,128)(2,1)S(1)}, bf16[2,2,128,512]{3,2,1,0:T(8,128)(2,1)S(1)}, u32[]{:S(2)}, u32[]{:S(2)}) collective-permute-start(bf16[2,2,128,512]{3,2,1,0:T(8,128)(2,1)S(1)} %get-tuple-element.53), channel_id=1, source_target_pairs={{0,120},{1,121},{2,122},{3,123},{4,124},{5,125},{6,126},{7,127},{8... | collective-permute-start | bytes 1572872 | tf_op jit(solution)/shard_map/ppermute | solution.py:29
  54.2 17.0 %collective-permute-start.12 = (bf16[2,2,128,512]{3,2,1,0:T(8,128)(2,1)S(1)}, bf16[2,2,128,512]{3,2,1,0:T(8,128)(2,1)S(1)}, u32[]{:S(2)}, u32[]{:S(2)}) collective-permute-start(bf16[2,2,128,512]{3,2,1,0:T(8,128)(2,1)S(1)} %get-tuple-element.54), channel_id=1, source_target_pairs={{0,8},{1,9},{2,10},{3,11},{4,12},{5,13},{6,14},{7,15},{8,16},{9,17... | collective-permute-start | bytes 1572872 | tf_op jit(solution)/shard_map/ppermute | solution.py:29
  54.2 9.9 %collective-permute-start.10 = (bf16[2,2,128,512]{3,2,1,0:T(8,128)(2,1)S(1)}, bf16[2,2,128,512]{3,2,1,0:T(8,128)(2,1)S(1)}, u32[]{:S(2)}, u32[]{:S(2)}) collective-permute-start(bf16[2,2,128,512]{3,2,1,0:T(8,128)(2,1)S(1)} %get-tuple-element.55), channel_id=1, source_target_pairs={{0,1},{1,2},{2,3},{3,4},{4,5},{5,6},{6,7},{7,0},{8,9},{9,10},{10,1... | collective-permute-start | bytes 1572872 | tf_op jit(solution)/shard_map/ppermute | solution.py:29
  54.2 9.9 %collective-permute-start.11 = (bf16[2,2,128,512]{3,2,1,0:T(8,128)(2,1)S(1)}, bf16[2,2,128,512]{3,2,1,0:T(8,128)(2,1)S(1)}, u32[]{:S(2)}, u32[]{:S(2)}) collective-permute-start(bf16[2,2,128,512]{3,2,1,0:T(8,128)(2,1)S(1)} %get-tuple-element.56), channel_id=1, source_target_pairs={{0,7},{1,0},{2,1},{3,2},{4,3},{5,4},{6,5},{7,6},{8,15},{9,8},{10,9... | collective-permute-start | bytes 1572872 | tf_op jit(solution)/shard_map/ppermute | solution.py:29
